TPU v7x, 32 devices: a whole 2x2x4 slice. The times are simulated.
32 devices in a mesh: dp: 8 (over y, x, core), cp: 4 (over z).
Axes of the slice: x: 2, y: 2, z: 4, core: 2. Of those that a mesh axis runs over, the one named last changes fastest.
Arguments:
- block_input: bfloat16 [16, 1024, 1024], P('dp', 'cp'), may hold values from -6 to 6
- mixer_gain: bfloat16 [1024], P(('dp', 'cp')), may hold values from 0.5 to 1.5
- qkv_weight: bfloat16 [1024, 3072], P(('dp', 'cp')), may hold values from -0.1875 to 0.1875
- conv_taps: bfloat16 [4, 3072], P(None, ('dp', 'cp')), may hold values from -3 to 3
- beta_weight: bfloat16 [1024, 8], P(('dp', 'cp')), may hold values from -0.1875 to 0.1875
- out_gain: bfloat16 [128], replicated, may hold values from 0.5 to 1.5
- proj_weight: bfloat16 [1024, 1024], P(('dp', 'cp')), may hold values from -0.1875 to 0.1875
- ffn_gain: bfloat16 [1024], P(('dp', 'cp')), may hold values from 0.5 to 1.5
- gate_up: bfloat16 [1024, 5632], P(('dp', 'cp')), may hold values from -0.1875 to 0.1875
- down_weight: bfloat16 [2816, 1024], P(('dp', 'cp')), may hold values from -0.109375 to 0.109375
- cotangent: bfloat16 [16, 1024, 1024], P('dp', 'cp'), may hold values from -6 to 6
Outputs:
- block_output: bfloat16 [16, 1024, 1024], P('dp', 'cp')
- grad_input: float32 [16, 1024, 1024], P('dp', 'cp')
- grad_mixer: float32 [1024], P(('dp', 'cp'))
- grad_qkv: float32 [1024, 3072], P(('dp', 'cp'))
- grad_conv: float32 [4, 3072], P(None, ('dp', 'cp'))
- grad_beta: float32 [1024, 8], P(('dp', 'cp'))
- grad_out: float32 [128], replicated
- grad_proj: float32 [1024, 1024], P(('dp', 'cp'))
- grad_ffn: float32 [1024], P(('dp', 'cp'))
- grad_gateup: float32 [1024, 5632], P(('dp', 'cp'))
- grad_down: float32 [2816, 1024], P(('dp', 'cp'))
- rms_values: float32 [3], replicated
All inputs are finite; a program needn't handle non-finite values.
Results may differ from a plain program's by a relative error of at most 0.018.
Values may be sent and summed in bfloat16 or wider, within the bound.
No kernel may reach another device: no remote copies, remote signals or barrier semaphores. Data moves between devices by JAX's collectives and lax.ppermute only.
A program may use at most 192 MiB of HBM per device.

v0:
```python
import jax
import jax.numpy as jnp
from jax import lax
from jax.sharding import PartitionSpec as P

HEADS = 8
GROUP = 64


norm_eps = 1e-05
unit_eps = 1e-06


def passed_along(value, axis, by):
    peers = lax.axis_size(axis)
    pairs = [(i, i + by) for i in range(peers) if 0 <= i + by < peers]
    return lax.ppermute(value, axis, pairs)


def mixer_inputs(extended, taps):
    width = taps.shape[0]
    count = extended.shape[-2] - width + 1
    conv = taps[0] * extended[..., 0:count, :]
    for lag in range(1, width):
        conv = conv + taps[lag] * extended[..., lag : lag + count, :]
    active = jax.nn.silu(conv)
    model = active.shape[-1] // 3
    shape = active.shape[:-1] + (HEADS, model // HEADS)
    query = active[..., :model].reshape(shape)
    keys = active[..., model : 2 * model].reshape(shape)
    values = active[..., 2 * model :].reshape(shape)
    depth = shape[-1]
    query = (
        query
        * lax.rsqrt(jnp.sum(query * query, axis=-1, keepdims=True) + unit_eps)
        * depth ** (-0.5)
    )
    keys = keys * lax.rsqrt(jnp.sum(keys * keys, axis=-1, keepdims=True) + unit_eps)
    return (query, keys, values)


def group_system(key_heads, rate_heads):
    size = key_heads.shape[1]
    strict = jnp.tril(jnp.ones((size, size), jnp.float32), -1)
    inner = jnp.einsum("hcd,hed->hce", key_heads, key_heads, precision=lax.Precision.HIGHEST)
    return jnp.eye(size, dtype=jnp.float32) + strict * (rate_heads[:, :, None] * inner)


def group_step(state, query, keys, values, rates):
    query_heads = jnp.swapaxes(query, 0, 1)
    key_heads = jnp.swapaxes(keys, 0, 1)
    value_heads = jnp.swapaxes(values, 0, 1)
    rate_heads = jnp.swapaxes(rates, 0, 1)
    size = key_heads.shape[1]
    system = group_system(key_heads, rate_heads)
    recalled = jnp.einsum("hcd,hde->hce", key_heads, state, precision=lax.Precision.HIGHEST)
    errors = jax.scipy.linalg.solve_triangular(
        system, rate_heads[:, :, None] * (value_heads - recalled), lower=True
    )
    causal = jnp.tril(jnp.ones((size, size), jnp.float32), 0)
    scores = (
        jnp.einsum("hcd,hed->hce", query_heads, key_heads, precision=lax.Precision.HIGHEST) * causal
    )
    output = jnp.einsum("hcd,hde->hce", query_heads, state, precision=lax.Precision.HIGHEST)
    output = output + jnp.einsum("hce,hef->hcf", scores, errors, precision=lax.Precision.HIGHEST)
    state = state + jnp.einsum("hcd,hce->hde", key_heads, errors, precision=lax.Precision.HIGHEST)
    return (state, jnp.swapaxes(output, 0, 1))


def delta_rule(state, query, keys, values, rates, block):
    count = query.shape[0] // block

    def split(array):
        return array.reshape((count, block) + array.shape[1:])

    def delta_advance(carry, items):
        return group_step(carry, items[0], items[1], items[2], items[3])

    final, outputs = lax.scan(
        jax.checkpoint(delta_advance),
        state,
        (split(query), split(keys), split(values), split(rates)),
    )
    return (outputs.reshape(query.shape), final)


def group_map(carry, keys, values, rates):
    transfer, offset = carry
    key_heads = jnp.swapaxes(keys, 0, 1)
    value_heads = jnp.swapaxes(values, 0, 1)
    rate_heads = jnp.swapaxes(rates, 0, 1)
    depth = key_heads.shape[2]
    system = group_system(key_heads, rate_heads)
    stacked = jnp.concatenate(
        [rate_heads[:, :, None] * value_heads, rate_heads[:, :, None] * key_heads], axis=-1
    )
    solved = jax.scipy.linalg.solve_triangular(system, stacked, lower=True)
    updates = solved[..., :depth]
    weights = solved[..., depth:]
    forget = jnp.einsum("hcd,hce->hde", key_heads, weights, precision=lax.Precision.HIGHEST)
    transfer = transfer - jnp.einsum(
        "hde,hef->hdf", forget, transfer, precision=lax.Precision.HIGHEST
    )
    offset = offset - jnp.einsum("hde,hef->hdf", forget, offset, precision=lax.Precision.HIGHEST)
    offset = offset + jnp.einsum(
        "hcd,hce->hde", key_heads, updates, precision=lax.Precision.HIGHEST
    )
    return (transfer, offset)


def segment_map(keys, values, rates):
    count = keys.shape[0] // GROUP
    heads, depth = (keys.shape[1], keys.shape[2])
    identity = jnp.broadcast_to(jnp.eye(depth, dtype=jnp.float32), (heads, depth, depth))

    def split(array):
        return array.reshape((count, GROUP) + array.shape[1:])

    def segment_advance(carry, items):
        return (group_map(carry, items[0], items[1], items[2]), None)

    final, unused = lax.scan(
        segment_advance,
        (identity, jnp.zeros_like(identity)),
        (split(keys), split(values), split(rates)),
    )
    return final


def apply_map(transfer, state, offset):
    return jnp.einsum("shij,shjk->shik", transfer, state, precision=lax.Precision.HIGHEST) + offset


def local_rule(start, query, keys, values, rates):

    def single(state, query_one, keys_one, values_one, rates_one):
        return delta_rule(state, query_one, keys_one, values_one, rates_one, GROUP)

    return jax.vmap(single)(start, query, keys, values, rates)


def rows_times(left, right):
    return jnp.einsum("sga,ab->sgb", left, right, preferred_element_type=jnp.float32)


def rows_back(grad, weight):
    return jnp.einsum("sgb,ab->sga", grad, weight, preferred_element_type=jnp.float32)


def weight_grad(left, right):
    return jnp.einsum("sga,sgb->ab", left, right, preferred_element_type=jnp.float32)


def round_trip(values):
    return values.astype(jnp.bfloat16).astype(jnp.float32)


def norm_back(rows, scale, gain, grad):
    weighted = grad * gain
    gain_grad = jnp.sum(grad * rows * scale, axis=tuple(range(rows.ndim - 1)))
    width = rows.shape[-1]
    row_grad = scale * weighted - rows * scale**3 * (
        jnp.sum(weighted * rows, axis=-1, keepdims=True) / width
    )
    return (gain_grad, row_grad)


def per_device(
    block_input,
    mixer_gain,
    qkv_weight,
    conv_taps,
    beta_weight,
    out_gain,
    proj_weight,
    ffn_gain,
    gate_up,
    down_weight,
    cotangent,
):
    gathered = (
        lax.all_gather(mixer_gain, ("dp", "cp"), axis=0, tiled=True),
        lax.all_gather(qkv_weight, ("dp", "cp"), axis=0, tiled=True),
        lax.all_gather(conv_taps, ("dp", "cp"), axis=1, tiled=True),
        lax.all_gather(beta_weight, ("dp", "cp"), axis=0, tiled=True),
        lax.all_gather(proj_weight, ("dp", "cp"), axis=0, tiled=True),
        lax.all_gather(ffn_gain, ("dp", "cp"), axis=0, tiled=True),
        lax.all_gather(gate_up, ("dp", "cp"), axis=0, tiled=True),
        lax.all_gather(down_weight, ("dp", "cp"), axis=0, tiled=True),
    )
    gain_one, w_qkv, taps_full, w_beta, w_proj, gain_two, w_gateup, w_down = gathered
    seqs_here, seg_len, model = block_input.shape
    width = conv_taps.shape[0]
    gain_outf = out_gain.astype(jnp.float32)
    resid_in = block_input.astype(jnp.float32)
    scale_one = lax.rsqrt(jnp.mean(resid_in * resid_in, axis=-1, keepdims=True) + norm_eps)
    normed_one = (resid_in * scale_one * gain_one.astype(jnp.float32)).astype(jnp.bfloat16)
    projected = rows_times(normed_one, w_qkv).astype(jnp.bfloat16)
    tail = projected[:, seg_len - (width - 1) :, :]
    borrowed = passed_along(tail, "cp", 1)
    extended = jnp.concatenate([borrowed, projected], axis=1).astype(jnp.float32)
    (query, keys, values), mixer_pull = jax.vjp(
        mixer_inputs, extended, taps_full.astype(jnp.float32)
    )
    query_low = round_trip(query)
    keys_low = round_trip(keys)
    values_low = round_trip(values)
    rates = jax.nn.sigmoid(rows_times(normed_one, w_beta))
    transfer, offset = jax.vmap(segment_map)(keys_low, values_low, rates)
    carried = jnp.zeros_like(offset)
    for step in range(lax.axis_size("cp") - 1):
        carried = passed_along(apply_map(transfer, carried, offset), "cp", 1)
    (mixed, final), rule_pull = jax.vjp(local_rule, carried, query_low, keys_low, values_low, rates)
    scale_mix = lax.rsqrt(jnp.mean(mixed * mixed, axis=-1, keepdims=True) + norm_eps)
    mixed_low = (
        (mixed * scale_mix * gain_outf).reshape(seqs_here, seg_len, model).astype(jnp.bfloat16)
    )
    attn = rows_times(mixed_low, w_proj)
    middle = resid_in + attn
    scale_two = lax.rsqrt(jnp.mean(middle * middle, axis=-1, keepdims=True) + norm_eps)
    gain_twof = gain_two.astype(jnp.float32)
    normed_two = (middle * scale_two * gain_twof).astype(jnp.bfloat16)
    gates = rows_times(normed_two, w_gateup)
    half = gates.shape[-1] // 2
    gate_part = gates[..., :half]
    up_part = gates[..., half:]
    hidden = (jax.nn.silu(gate_part) * up_part).astype(jnp.bfloat16)
    ffn_out = rows_times(hidden, w_down)
    result = middle + ffn_out
    squares = jnp.stack(
        [jnp.sum(result * result), jnp.sum(attn * attn), jnp.sum(ffn_out * ffn_out)]
    )
    regathered = (
        lax.all_gather(mixer_gain, ("dp", "cp"), axis=0, tiled=True),
        lax.all_gather(qkv_weight, ("dp", "cp"), axis=0, tiled=True),
        lax.all_gather(conv_taps, ("dp", "cp"), axis=1, tiled=True),
        lax.all_gather(beta_weight, ("dp", "cp"), axis=0, tiled=True),
        lax.all_gather(proj_weight, ("dp", "cp"), axis=0, tiled=True),
        lax.all_gather(ffn_gain, ("dp", "cp"), axis=0, tiled=True),
        lax.all_gather(gate_up, ("dp", "cp"), axis=0, tiled=True),
        lax.all_gather(down_weight, ("dp", "cp"), axis=0, tiled=True),
    )
    gain_one, w_qkv, taps_full, w_beta, w_proj, gain_two, w_gateup, w_down = regathered
    gain_twof = gain_two.astype(jnp.float32)
    upstream = cotangent.astype(jnp.float32)
    grad_down = weight_grad(hidden, cotangent)
    grad_hidden = rows_back(cotangent, w_down)
    sigma = jax.nn.sigmoid(gate_part)
    grad_gate = grad_hidden * up_part * (sigma * (1.0 + gate_part * (1.0 - sigma)))
    grad_up = grad_hidden * (gate_part * sigma)
    grad_gates = jnp.concatenate([grad_gate, grad_up], axis=-1).astype(jnp.bfloat16)
    grad_gateup = weight_grad(normed_two, grad_gates)
    grad_normed_two = rows_back(grad_gates, w_gateup)
    grad_ffn, grad_from_norm = norm_back(middle, scale_two, gain_twof, grad_normed_two)
    grad_middle = upstream + grad_from_norm
    grad_attn = grad_middle.astype(jnp.bfloat16)
    grad_proj = weight_grad(mixed_low, grad_attn)
    grad_normed_mix = round_trip(rows_back(grad_attn, w_proj)).reshape(mixed.shape)
    grad_out, grad_mixed = norm_back(mixed, scale_mix, gain_outf, grad_normed_mix)
    local_part = rule_pull((grad_mixed, jnp.zeros_like(final)))[0]
    flipped = jnp.swapaxes(transfer, -1, -2)
    incoming = jnp.zeros_like(local_part)
    for step in range(lax.axis_size("cp") - 1):
        incoming = passed_along(apply_map(flipped, incoming, local_part), "cp", -1)
    unused, grad_query, grad_keys, grad_values, grad_rates = rule_pull((grad_mixed, incoming))
    grad_extended, grad_conv = mixer_pull((grad_query, grad_keys, grad_values))
    returned = passed_along(grad_extended[:, : width - 1, :], "cp", -1)
    grad_own = grad_extended[:, width - 1 :, :]
    keep_rows = seg_len - (width - 1)
    grad_own = jnp.concatenate(
        [grad_own[:, :keep_rows, :], grad_own[:, keep_rows:, :] + returned], axis=1
    )
    grad_projected = grad_own.astype(jnp.bfloat16)
    grad_logits = grad_rates * rates * (1.0 - rates)
    grad_qkv = weight_grad(normed_one, grad_projected)
    grad_beta = jnp.einsum(
        "sga,sgb->ab", normed_one.astype(jnp.float32), grad_logits, precision=lax.Precision.HIGHEST
    )
    grad_normed_one = rows_back(grad_projected, w_qkv)
    grad_normed_one = grad_normed_one + jnp.einsum(
        "sgb,ab->sga", grad_logits, w_beta.astype(jnp.float32), precision=lax.Precision.HIGHEST
    )
    grad_mixer, grad_from_first = norm_back(
        resid_in, scale_one, gain_one.astype(jnp.float32), grad_normed_one
    )
    grad_input = grad_middle + grad_from_first
    totals, grad_out_all = lax.psum((squares, grad_out), ("dp", "cp"))
    rms_values = jnp.sqrt(totals / (result.size * lax.axis_size(("dp", "cp"))))
    shares = (
        lax.psum_scatter(grad_mixer, ("dp", "cp"), scatter_dimension=0, tiled=True),
        lax.psum_scatter(grad_qkv, ("dp", "cp"), scatter_dimension=0, tiled=True),
        lax.psum_scatter(grad_conv, ("dp", "cp"), scatter_dimension=1, tiled=True),
        lax.psum_scatter(grad_beta, ("dp", "cp"), scatter_dimension=0, tiled=True),
        lax.psum_scatter(grad_proj, ("dp", "cp"), scatter_dimension=0, tiled=True),
        lax.psum_scatter(grad_ffn, ("dp", "cp"), scatter_dimension=0, tiled=True),
        lax.psum_scatter(grad_gateup, ("dp", "cp"), scatter_dimension=0, tiled=True),
        lax.psum_scatter(grad_down, ("dp", "cp"), scatter_dimension=0, tiled=True),
    )
    return (
        result.astype(jnp.bfloat16),
        grad_input,
        shares[0],
        shares[1],
        shares[2],
        shares[3],
        grad_out_all,
        shares[4],
        shares[5],
        shares[6],
        shares[7],
        rms_values,
    )


def solution(mesh):
    in_specs = (
        P("dp", "cp", None),
        P(("dp", "cp")),
        P(("dp", "cp"), None),
        P(None, ("dp", "cp")),
        P(("dp", "cp"), None),
        P(),
        P(("dp", "cp"), None),
        P(("dp", "cp")),
        P(("dp", "cp"), None),
        P(("dp", "cp"), None),
        P("dp", "cp", None),
    )
    out_specs = (
        P("dp", "cp", None),
        P("dp", "cp", None),
        P(("dp", "cp")),
        P(("dp", "cp"), None),
        P(None, ("dp", "cp")),
        P(("dp", "cp"), None),
        P(),
        P(("dp", "cp"), None),
        P(("dp", "cp")),
        P(("dp", "cp"), None),
        P(("dp", "cp"), None),
        P(),
    )
    return jax.shard_map(
        per_device, mesh=mesh, in_specs=in_specs, out_specs=out_specs, check_vma=False
    )
```

profile of v0, /device:TPU:0, one launch (start us, length us, event | category | flops | bytes accessed | tf_op | source)
XLA Modules:
  0.0 3483.3 jit_solution(9513841482243251967)
XLA Ops:
  11.2 42.6 %all-reduce.16 = (bf16[1024]{0:T(1024)(128)(2,1)S(1)}, bf16[1024]{0:T(1024)(128)(2,1)S(1)}) all-reduce(bf16[1024]{0:T(1024)(128)(2,1)S(1)} %dynamic-update-slice, bf16[1024]{0:T(1024)(128)(2,1)S(1)} %dynamic-update-slice.1), channel_id=1, replica_groups=mesh['dp'=8,'cp'=4] {'dp','cp'}, use_global_device_ids=true, to_apply=%add.11 | all-reduce | flops 2048 | bytes 8192
  53.8 66.5 %all-gather = bf16[32,96,4]{1,2,0:T(4,128)(2,1)S(1)} all-gather(bf16[1,96,4]{1,2,0:T(4,128)(2,1)} %bitcast.633), channel_id=1, replica_groups=mesh['dp'=8,'cp'=4] {'dp','cp'}, dimensions={0}, use_global_device_ids=true | all-gather | bytes 25344 | tf_op jit(solution)/shard_map/all_gather | solution.py:184
  120.4 64.9 %all-gather.1 = bf16[32,32,8]{1,2,0:T(8,128)(2,1)S(1)} all-gather(bf16[1,32,8]{1,2,0:T(8,128)(2,1)} %bitcast.632), channel_id=1, replica_groups=mesh['dp'=8,'cp'=4] {'dp','cp'}, dimensions={0}, use_global_device_ids=true | all-gather | bytes 16896 | tf_op jit(solution)/shard_map/all_gather | solution.py:185
  188.2 6.6 fusion.139
  223.1 396.6 %while.67 = (s32[]{:T(128)}, f32[2,8,128,128]{3,2,1,0:T(8,128)}, f32[2,8,128,128]{3,2,1,0:T(8,128)}, f32[4,2,64,8,128]{4,2,3,1,0:T(8,128)S(1)}, f32[4,2,64,8]{2,...) while((s32[]{:T(128)}, f32[2,8,128,128]{3,2,1,0:T(8,128)}, ...), condition=%wide.region_3.4_spmd.clone, body=%wide.region_2.3_spmd.clone.sunk | while | flops 1511804928 | bytes 29491888 | solution.py:122
  228.7 80.0 %custom-call.36 = f32[2,8,1,64,64]{3,4,2,1,0:T(8,128)} custom-call(f32[2,8,1,64,64]{4,3,2,1,0:T(8,128)} %fusion.418), custom_call_target="InvertDiagBlocksLowerTriangular" | custom-call | tf_op jit(solution)/shard_map/vmap()/while/body/eval_jaxpr/jit(_solve_triangular)/vmap()/triangular_solve | solution.py:97
  327.6 80.0 %custom-call.36 = f32[2,8,1,64,64]{3,4,2,1,0:T(8,128)} custom-call(f32[2,8,1,64,64]{4,3,2,1,0:T(8,128)} %fusion.418), custom_call_target="InvertDiagBlocksLowerTriangular" | custom-call | tf_op jit(solution)/shard_map/vmap()/while/body/eval_jaxpr/jit(_solve_triangular)/vmap()/triangular_solve | solution.py:97
  426.7 80.0 %custom-call.36 = f32[2,8,1,64,64]{3,4,2,1,0:T(8,128)} custom-call(f32[2,8,1,64,64]{4,3,2,1,0:T(8,128)} %fusion.418), custom_call_target="InvertDiagBlocksLowerTriangular" | custom-call | tf_op jit(solution)/shard_map/vmap()/while/body/eval_jaxpr/jit(_solve_triangular)/vmap()/triangular_solve | solution.py:97
  525.9 80.0 %custom-call.36 = f32[2,8,1,64,64]{3,4,2,1,0:T(8,128)} custom-call(f32[2,8,1,64,64]{4,3,2,1,0:T(8,128)} %fusion.418), custom_call_target="InvertDiagBlocksLowerTriangular" | custom-call | tf_op jit(solution)/shard_map/vmap()/while/body/eval_jaxpr/jit(_solve_triangular)/vmap()/triangular_solve | solution.py:97
  626.6 15.3 collective-permute-done.1
  650.7 20.9 collective-permute-done.2
  686.6 19.8 collective-permute-done.3
  707.9 389.3 %while.66 = (s32[]{:T(128)}, f32[2,8,128,128]{3,2,1,0:T(8,128)S(1)}, f32[4,2,64,8,128]{4,2,3,1,0:T(8,128)}, f32[4,2,8,128,128]{4,3,2,1,0:T(8,128)}, f32[4,2,64,8...) while((s32[]{:T(128)}, ...), condition=%wide.region_6.8_spmd.clone, body=%wide.region_5.7_spmd.clone.sunk | while | flops 1007644672 | bytes 15392125 | solution.py:79
  716.5 80.0 %custom-call.35 = f32[2,8,1,64,64]{3,4,2,1,0:T(8,128)} custom-call(f32[2,8,1,64,64]{4,3,2,1,0:T(8,128)} %fusion.402), custom_call_target="InvertDiagBlocksLowerTriangular" | custom-call | tf_op jit(solution)/shard_map/jvp(vmap())/while/body/eval_jaxpr/jit(_solve_triangular)/vmap()/triangular_solve/custom-call.0 | solution.py:57
  813.8 80.0 %custom-call.35 = f32[2,8,1,64,64]{3,4,2,1,0:T(8,128)} custom-call(f32[2,8,1,64,64]{4,3,2,1,0:T(8,128)} %fusion.402), custom_call_target="InvertDiagBlocksLowerTriangular" | custom-call | tf_op jit(solution)/shard_map/jvp(vmap())/while/body/eval_jaxpr/jit(_solve_triangular)/vmap()/triangular_solve/custom-call.0 | solution.py:57
  911.2 80.0 %custom-call.35 = f32[2,8,1,64,64]{3,4,2,1,0:T(8,128)} custom-call(f32[2,8,1,64,64]{4,3,2,1,0:T(8,128)} %fusion.402), custom_call_target="InvertDiagBlocksLowerTriangular" | custom-call | tf_op jit(solution)/shard_map/jvp(vmap())/while/body/eval_jaxpr/jit(_solve_triangular)/vmap()/triangular_solve/custom-call.0 | solution.py:57
  1008.5 80.0 %custom-call.35 = f32[2,8,1,64,64]{3,4,2,1,0:T(8,128)} custom-call(f32[2,8,1,64,64]{4,3,2,1,0:T(8,128)} %fusion.402), custom_call_target="InvertDiagBlocksLowerTriangular" | custom-call | tf_op jit(solution)/shard_map/jvp(vmap())/while/body/eval_jaxpr/jit(_solve_triangular)/vmap()/triangular_solve/custom-call.0 | solution.py:57
  1120.3 12.3 fusion.125
  1132.6 9.4 multiply_convert_fusion.1
  1142.0 12.1 fusion.123
  1154.1 8.0 multiply_reduce_fusion.8
  1172.3 387.0 %while.68 = (s32[]{:T(128)}, f32[2,8,128,128]{3,2,1,0:T(8,128)}, f32[4,2,64,8,128]{4,2,3,1,0:T(8,128)}, f32[4,2,64,8,128]{4,2,3,1,0:T(8,128)S(1)}, f32[4,2,64,8]...) while((s32[]{:T(128)}, f32[2,8,128,128]{3,2,1,0:T(8,128)}, ...), condition=%wide.region_12.15_spmd.clone, body=%wide.region_11.14_spmd.clone.sunk | while | flops 1008169024 | bytes 25289408 | solution.py:79
  1184.3 80.0 %custom-call.37 = f32[2,8,1,64,64]{3,4,2,1,0:T(8,128)} custom-call(f32[2,8,1,64,64]{4,3,2,1,0:T(8,128)} %fusion.438), custom_call_target="InvertDiagBlocksLowerTriangular" | custom-call | tf_op jit(solution)/shard_map/transpose(jvp(vmap()))/while/body/eval_jaxpr/checkpoint/jit(_solve_triangular)/vmap()/triangular_solve/custom-call.2 | solution.py:57
  1281.1 80.0 %custom-call.37 = f32[2,8,1,64,64]{3,4,2,1,0:T(8,128)} custom-call(f32[2,8,1,64,64]{4,3,2,1,0:T(8,128)} %fusion.438), custom_call_target="InvertDiagBlocksLowerTriangular" | custom-call | tf_op jit(solution)/shard_map/transpose(jvp(vmap()))/while/body/eval_jaxpr/checkpoint/jit(_solve_triangular)/vmap()/triangular_solve/custom-call.2 | solution.py:57
  1377.9 80.0 %custom-call.37 = f32[2,8,1,64,64]{3,4,2,1,0:T(8,128)} custom-call(f32[2,8,1,64,64]{4,3,2,1,0:T(8,128)} %fusion.438), custom_call_target="InvertDiagBlocksLowerTriangular" | custom-call | tf_op jit(solution)/shard_map/transpose(jvp(vmap()))/while/body/eval_jaxpr/checkpoint/jit(_solve_triangular)/vmap()/triangular_solve/custom-call.2 | solution.py:57
  1474.7 80.0 %custom-call.37 = f32[2,8,1,64,64]{3,4,2,1,0:T(8,128)} custom-call(f32[2,8,1,64,64]{4,3,2,1,0:T(8,128)} %fusion.438), custom_call_target="InvertDiagBlocksLowerTriangular" | custom-call | tf_op jit(solution)/shard_map/transpose(jvp(vmap()))/while/body/eval_jaxpr/checkpoint/jit(_solve_triangular)/vmap()/triangular_solve/custom-call.2 | solution.py:57
  1564.5 24.0 collective-permute-done.4
  1593.0 24.4 collective-permute-done.5
  1627.5 14.9 collective-permute-done.6
  1647.0 482.7 %while.65 = (s32[]{:T(128)}, f32[2,8,128,128]{3,2,1,0:T(8,128)S(1)}, f32[4,2,64,8,128]{4,3,2,0,1:T(8,128)}, f32[4,2,64,8,128]{4,3,2,0,1:T(8,128)}, f32[4,2,64,8,...) while((s32[]{:T(128)}, ...), condition=%wide.region_16.19_spmd, body=%wide.region_13.18_spmd.sunk | while | flops 2570284032 | bytes 76497808 | solution.py:79
  1656.8 79.3 %custom-call.34 = f32[2,8,1,64,64]{3,4,2,1,0:T(8,128)} custom-call(f32[2,8,1,64,64]{4,3,2,1,0:T(8,128)S(1)} %select_bitcast_fusion.6), custom_call_target="InvertDiagBlocksLowerTriangular" | custom-call | tf_op jit(solution)/shard_map/transpose(jvp(vmap()))/while/body/eval_jaxpr/checkpoint/jit(_solve_triangular)/vmap()/triangular_solve/custom-call.2 | solution.py:57
  1777.3 79.3 %custom-call.34 = f32[2,8,1,64,64]{3,4,2,1,0:T(8,128)} custom-call(f32[2,8,1,64,64]{4,3,2,1,0:T(8,128)S(1)} %select_bitcast_fusion.6), custom_call_target="InvertDiagBlocksLowerTriangular" | custom-call | tf_op jit(solution)/shard_map/transpose(jvp(vmap()))/while/body/eval_jaxpr/checkpoint/jit(_solve_triangular)/vmap()/triangular_solve/custom-call.2 | solution.py:57
  1897.8 79.3 %custom-call.34 = f32[2,8,1,64,64]{3,4,2,1,0:T(8,128)} custom-call(f32[2,8,1,64,64]{4,3,2,1,0:T(8,128)S(1)} %select_bitcast_fusion.6), custom_call_target="InvertDiagBlocksLowerTriangular" | custom-call | tf_op jit(solution)/shard_map/transpose(jvp(vmap()))/while/body/eval_jaxpr/checkpoint/jit(_solve_triangular)/vmap()/triangular_solve/custom-call.2 | solution.py:57
  2018.4 79.3 %custom-call.34 = f32[2,8,1,64,64]{3,4,2,1,0:T(8,128)} custom-call(f32[2,8,1,64,64]{4,3,2,1,0:T(8,128)S(1)} %select_bitcast_fusion.6), custom_call_target="InvertDiagBlocksLowerTriangular" | custom-call | tf_op jit(solution)/shard_map/transpose(jvp(vmap()))/while/body/eval_jaxpr/checkpoint/jit(_solve_triangular)/vmap()/triangular_solve/custom-call.2 | solution.py:57
  2158.9 8.1 add_add_fusion.1
  2167.0 15.8 multiply_reduce_fusion.5
  2192.3 6.3 broadcast_multiply_fusion
  2211.6 6.6 convolution_bitcast_fusion.2
  2218.3 9.6 convolution_bitcast_fusion.1
  2228.6 14.0 convolution_bitcast_fusion
  2247.0 37.5 %reduce-scatter.19.cloned.1.call-done = f32[96,4]{1,0:T(8,128)} async-done(((f32[3072,4]{1,0:T(8,128)}), f32[96,4]{1,0:T(8,128)}) %reduce-scatter.19.cloned.1.call-update) | async-done | bytes 1552
  2286.0 133.7 %reduce-scatter.21.cloned.1.call-done = f32[32,8]{1,0:T(8,128)} async-done(((f32[1024,8]{1,0:T(8,128)}), f32[32,8]{1,0:T(8,128)}) %reduce-scatter.21.cloned.1.call-update) | async-done | bytes 1040
  2421.1 9.4 fusion.150
  2430.6 37.8 %all-reduce.15 = (f32[1024]{0:T(1024)S(1)}, f32[128]{0:T(128)}, f32[1024]{0:T(1024)S(1)}, f32[3]{0:T(128)S(1)}) all-reduce(f32[1024]{0:T(1024)S(1)} %get-tuple-element.671, f32[128]{0:T(128)S(1)} %bitcast_reduce_fusion, f32[1024]{0:T(1024)S(1)} %copy-done.68, ...), channel_id=2, replica_groups=mesh['dp'=8,'cp'=4] {'dp','cp'}, use_global_device_ids=true, to_apply=%region_21.24.clone | all-reduce | flops 2179 | bytes 17432
  2473.5 93.7 %reduce-scatter.13.cloned.1.call-done = f32[32,1024]{1,0:T(8,128)} async-done(((f32[1024,1024]{1,0:T(8,128)}), f32[32,1024]{1,0:T(8,128)}) %reduce-scatter.13.cloned.1.call-update) | async-done | bytes 131088 | tf_op jit(solution)/shard_map/reduce_scatter | solution.py:294
  2567.2 161.4 %reduce-scatter.11.cloned.1.call-done = f32[32,3072]{1,0:T(8,128)} async-done(((f32[1024,3072]{1,0:T(8,128)}), f32[32,3072]{1,0:T(8,128)}) %reduce-scatter.11.cloned.1.call-update) | async-done | bytes 393232 | tf_op jit(solution)/shard_map/reduce_scatter | solution.py:291
  2728.7 253.0 %reduce-scatter.17.cloned.1.call-done = f32[88,1024]{1,0:T(8,128)} async-done(((f32[2816,1024]{1,0:T(8,128)}), f32[88,1024]{1,0:T(8,128)}) %reduce-scatter.17.cloned.1.call-update) | async-done | bytes 360464 | tf_op jit(solution)/shard_map/reduce_scatter | solution.py:297
  2981.6 494.6 %reduce-scatter.15.cloned.1.call-done = f32[32,5632]{1,0:T(8,128)} async-done(((f32[1024,5632]{1,0:T(8,128)}), f32[32,5632]{1,0:T(8,128)}) %reduce-scatter.15.cloned.1.call-update) | async-done | bytes 720912 | tf_op jit(solution)/shard_map/reduce_scatter | solution.py:296
  (664 shorter events, 564.4 us)
Async XLA Ops:
  7.2 180.4 %copy-start.29 = (bf16[2,256,1024]{2,1,0:T(8,128)(2,1)S(1)}, bf16[2,256,1024]{2,1,0:T(8,128)(2,1)}, u32[]{:S(2)}) copy-start(bf16[2,256,1024]{2,1,0:T(8,128)(2,1)} %param.23) | copy-start | bytes 3145732
  7.2 181.0 %all-gather.7.cloned.1.call-start = ((), (), s32[]{:S(2)}) async-start(), calls=%async_computation.6 | async-start | bytes 6488064 | tf_op jit(solution)/shard_map/all_gather | solution.py:183
  7.9 1107.1 %all-gather.9.cloned.1.call-start = ((), (), s32[]{:S(2)}) async-start(), calls=%async_computation.7 | async-start | bytes 2162688 | tf_op jit(solution)/shard_map/all_gather | solution.py:186
  8.7 1111.6 %all-gather.11.cloned.1.call-start = ((), (), s32[]{:S(2)}) async-start(), calls=%async_computation.8 | async-start | bytes 11894784 | tf_op jit(solution)/shard_map/all_gather | solution.py:188
  9.4 1123.2 %all-gather.13.cloned.1.call-start = ((), (), s32[]{:S(2)}) async-start(), calls=%async_computation.9 | async-start | bytes 5947392 | tf_op jit(solution)/shard_map/all_gather | solution.py:189
  53.8 141.0 %copy-start.40 = (f32[1024]{0:T(1024)}, f32[1024]{0:T(1024)S(1)}, u32[]{:S(2)}) copy-start(f32[1024]{0:T(1024)S(1)} %convert_element_type.123) | copy-start | bytes 12292
  185.5 9.3 copy-start.62
  187.6 7.2 copy-start.46
  188.1 13.1 copy-start.64
  188.1 18.5 copy-start.54
  188.1 18.5 copy-start.56
  188.1 18.5 copy-start.58
  188.1 18.5 copy-start.60
  196.8 7.0 collective-permute-start
  206.6 5.5 copy-start
  510.8 5.0 copy-start.14
  610.0 5.0 copy-start.14
  619.7 22.1 copy-start.15
  622.3 28.3 copy-start.69
  622.3 19.5 collective-permute-start.1
  645.2 26.4 collective-permute-start.2
  650.6 1634.0 %reduce-scatter.19.cloned.1.call-start = ((), (), s32[]{:S(2)}) async-start(), calls=%async_computation.14 | async-start | bytes 1622016
  650.7 511.4 %copy-start.42 = (f32[1024]{0:T(1024)}, f32[1024]{0:T(1024)S(1)}, u32[]{:S(2)}) copy-start(f32[1024]{0:T(1024)S(1)} %convert_element_type.133) | copy-start | bytes 12292
  650.7 29.1 copy-start.34
  675.4 30.9 collective-permute-start.3
  1120.2 41.9 %copy-start.44 = (f32[2,256]{1,0:T(2,128)}, f32[2,256]{1,0:T(2,128)S(1)}, u32[]{:S(2)}) copy-start(f32[2,256]{1,0:T(2,128)S(1)} %get-tuple-element.792) | copy-start | bytes 6148
  1120.3 12.3 copy-start.39
  1142.0 12.1 copy-start.36
  1142.0 12.1 copy-start.37
  1142.0 12.1 copy-start.70
  1142.0 12.1 copy-start.32
  1559.3 29.2 copy-start.13
  1562.8 25.8 collective-permute-start.4
  1591.7 31.1 copy-start.51
  1591.7 25.7 collective-permute-start.5
  1621.5 20.9 collective-permute-start.6
  1656.4 79.7 %copy-start.7 = (f32[2,8,64,64]{3,2,1,0:T(8,128)}, f32[2,8,64,64]{3,2,1,0:T(8,128)S(1)}, u32[]{:S(2)}) copy-start(f32[2,8,64,64]{3,2,1,0:T(8,128)S(1)} %fusion.377) | copy-start | bytes 786436 | tf_op jit(solution)/shard_map/transpose(jvp(vmap()))/while
  1777.0 79.7 %copy-start.7 = (f32[2,8,64,64]{3,2,1,0:T(8,128)}, f32[2,8,64,64]{3,2,1,0:T(8,128)S(1)}, u32[]{:S(2)}) copy-start(f32[2,8,64,64]{3,2,1,0:T(8,128)S(1)} %fusion.377) | copy-start | bytes 786436 | tf_op jit(solution)/shard_map/transpose(jvp(vmap()))/while
  1897.5 79.7 %copy-start.7 = (f32[2,8,64,64]{3,2,1,0:T(8,128)}, f32[2,8,64,64]{3,2,1,0:T(8,128)S(1)}, u32[]{:S(2)}) copy-start(f32[2,8,64,64]{3,2,1,0:T(8,128)S(1)} %fusion.377) | copy-start | bytes 786436 | tf_op jit(solution)/shard_map/transpose(jvp(vmap()))/while
  2018.1 79.7 %copy-start.7 = (f32[2,8,64,64]{3,2,1,0:T(8,128)}, f32[2,8,64,64]{3,2,1,0:T(8,128)S(1)}, u32[]{:S(2)}) copy-start(f32[2,8,64,64]{3,2,1,0:T(8,128)S(1)} %fusion.377) | copy-start | bytes 786436 | tf_op jit(solution)/shard_map/transpose(jvp(vmap()))/while
  2184.6 235.2 %reduce-scatter.21.cloned.1.call-start = ((), (), s32[]{:S(2)}) async-start(), calls=%async_computation.15 | async-start | bytes 540672
  2187.0 380.2 %reduce-scatter.13.cloned.1.call-start = ((), (), s32[]{:S(2)}) async-start(), calls=%async_computation.11 | async-start | bytes 4325376 | tf_op jit(solution)/shard_map/reduce_scatter | solution.py:294
  2191.5 537.1 %reduce-scatter.11.cloned.1.call-start = ((), (), s32[]{:S(2)}) async-start(), calls=%async_computation.10 | async-start | bytes 12976128 | tf_op jit(solution)/shard_map/reduce_scatter | solution.py:291
  2199.5 10.4 collective-permute-start.7
  2218.2 763.4 %reduce-scatter.17.cloned.1.call-start = ((), (), s32[]{:S(2)}) async-start(), calls=%async_computation.13 | async-start | bytes 11894784 | tf_op jit(solution)/shard_map/reduce_scatter | solution.py:297
  2227.9 1248.3 %reduce-scatter.15.cloned.1.call-start = ((), (), s32[]{:S(2)}) async-start(), calls=%async_computation.12 | async-start | bytes 23789568 | tf_op jit(solution)/shard_map/reduce_scatter | solution.py:296
  2421.1 9.5 copy-start.68
  2421.1 48.9 %copy-start.67 = (f32[2,256]{1,0:T(2,128)S(1)}, f32[2,256]{1,0:T(2,128)}, u32[]{:S(2)}) copy-start(f32[2,256]{1,0:T(2,128)} %get-tuple-element.789) | copy-start | bytes 6148
  (77 other events, 177.3 us)
Sparse Core Ops, SparseCore 0:
  10.9 72.5 all-gather.6
  86.4 55.0 all-gather.8
  144.3 89.5 all-gather.10
  650.7 66.2 all-gather.12
  2184.7 99.8 reduce-scatter.18
  2286.7 133.0 reduce-scatter.20
  2422.7 144.4 reduce-scatter.12
  2574.9 153.7 reduce-scatter.10
  2731.5 250.0 reduce-scatter.16
  2984.4 491.8 reduce-scatter.14
where the time goes:
time: 3500 us; the launch traced here: 3480 us
  other arithmetic  1370 us (39%)
  waiting for transfers between devices  1300 us (37%)
  matrix products  416 us (12%)
  blocking collectives  212 us (6%)
  local copies, waits for them, and re-layouts  149 us (4%)
    another operation x28, other arithmetic, group_step(): jax.scipy.linalg.solve_triangular(system, rate_heads[:, :, None] * (value...  958 us
    reduce_scatter x1, waiting for transfers between devices, per_device(): lax.psum_scatter(grad_gateup, ('dp', 'cp'), scatter_dimension=0, tiled=True)  495 us
    another operation x8, other arithmetic, group_map(): solved = jax.scipy.linalg.solve_triangular(system, stacked, lower=True)  320 us
    reduce_scatter x1, waiting for transfers between devices, per_device(): lax.psum_scatter(grad_down, ('dp', 'cp'), scatter_dimension=0, tiled=True)  253 us
    unnamed x12, waiting for transfers between devices  173 us
    reduce_scatter x1, waiting for transfers between devices, per_device(): lax.psum_scatter(grad_qkv, ('dp', 'cp'), scatter_dimension=0, tiled=True)  161 us
    ppermute x8, waiting for transfers between devices, passed_along(): return lax.ppermute(value, axis, pairs)  122 us
    reduce_scatter x1, waiting for transfers between devices, per_device(): lax.psum_scatter(grad_proj, ('dp', 'cp'), scatter_dimension=0, tiled=True)  93.7 us
  transfers between devices with their start and end apart: 18, of which 13 were waited for; matrix products, arithmetic and copies ran while one was open for 27% of the time, Pallas kernels for 0%

commit v1 on v0

v1 whole, which is shorter than its diff:
```python
import functools

import jax
import jax.numpy as jnp
from jax import lax
from jax.experimental import pallas as pl
from jax.experimental.pallas import tpu as pltpu
from jax.sharding import PartitionSpec as P

HEADS = 8
PAIR = 4

norm_eps = 1e-05
unit_eps = 1e-06
F32 = jnp.float32
BF16 = jnp.bfloat16


def halves(value):
    high = value.astype(BF16)
    return high, (value - high.astype(F32)).astype(BF16)


NN = (((1,), (0,)), ((), ()))
NT = (((1,), (1,)), ((), ()))
TN = (((0,), (0,)), ((), ()))


def mul(left, right, dims):
    return lax.dot_general(left, right, dims, preferred_element_type=F32)


def mul_split(left, right, dims):
    return (
        mul(left[0], right[0], dims) + mul(left[0], right[1], dims) + mul(left[1], right[0], dims)
    )


def mul_high(left, right, dims):
    left = (left,) if left.dtype == BF16 else halves(left)
    right = (right,) if right.dtype == BF16 else halves(right)
    total = mul(left[0], right[0], dims)
    if len(right) == 2:
        total = total + mul(left[0], right[1], dims)
    if len(left) == 2:
        total = total + mul(left[1], right[0], dims)
    return total


def shifted_down(rows, before, by):
    if by == 0:
        return rows
    rolled = pltpu.roll(rows, by, 0)
    top = pltpu.roll(before, by, 0)
    index = lax.broadcasted_iota(jnp.int32, before.shape, 0)
    first = jnp.where(index < by, top, rolled[: before.shape[0]])
    return jnp.concatenate([first, rolled[before.shape[0] :]], axis=0)


def shifted_up(rows, by):
    if by == 0:
        return rows
    count = rows.shape[0]
    index = lax.broadcasted_iota(jnp.int32, rows.shape, 0)
    return jnp.where(index < count - by, pltpu.roll(rows, count - by, 0), 0.0)


def conv_parts(rows, before, taps):
    width = taps.shape[0]
    conv = None
    for lag in range(width):
        term = taps[lag : lag + 1] * shifted_down(rows, before, width - 1 - lag)
        conv = term if conv is None else conv + term
    return conv


def unit_scale(active):
    return lax.rsqrt(jnp.sum(active * active, axis=-1, keepdims=True) + unit_eps)


def column_of(rates, head):
    index = lax.broadcasted_iota(jnp.int32, rates.shape, 1)
    return jnp.sum(jnp.where(index == head, rates, 0.0), axis=1, keepdims=True)


def row_of(rates, head):
    index = lax.broadcasted_iota(jnp.int32, rates.shape, 0)
    return jnp.sum(jnp.where(index == head, rates, 0.0), axis=0, keepdims=True)


def forward_kernel(
    q_ref, k_ref, v_ref, qb_ref, kb_ref, vb_ref, qt_ref, kt_ref, vt_ref, rates_ref, flipped_ref,
    inverse_ref, updates_ref, weights_ref, reach_ref, mixed_ref, transfer_ref, offset_ref,
):
    depth = transfer_ref.shape[-1]
    size = q_ref.shape[1]
    first = pl.program_id(1) * PAIR
    row = lax.broadcasted_iota(jnp.int32, (size, size), 0)
    col = lax.broadcasted_iota(jnp.int32, (size, size), 1)
    apart = row ^ col
    strict = row > col
    lower = row >= col
    eye = jnp.where(row == col, 1.0, 0.0)
    small_row = lax.broadcasted_iota(jnp.int32, (depth, depth), 0)
    small_col = lax.broadcasted_iota(jnp.int32, (depth, depth), 1)
    small_eye = jnp.where(small_row == small_col, 1.0, 0.0)
    systems, inverses, queries, keys, values, across = [], [], [], [], [], []
    for h in range(PAIR):
        lanes = slice(h * depth, (h + 1) * depth)

        def active(ref, before, taps):
            conv = conv_parts(
                ref[0, :, lanes].astype(F32),
                before[0, :, lanes].astype(F32),
                taps[:, lanes].astype(F32),
            )
            return conv * jax.nn.sigmoid(conv)

        q = active(q_ref, qb_ref, qt_ref)
        k = active(k_ref, kb_ref, kt_ref)
        v = active(v_ref, vb_ref, vt_ref)
        q = (q * unit_scale(q) * depth ** (-0.5)).astype(BF16)
        k = (k * unit_scale(k)).astype(BF16)
        queries.append(q)
        keys.append(k)
        values.append(v.astype(BF16))
        column = column_of(rates_ref[0], first + h)
        across.append(row_of(flipped_ref[0], first + h))
        system = jnp.where(strict, column * mul(k, k, NT), 0.0)
        systems.append(system)
        inverses.append(eye - jnp.where(apart == 1, system, 0.0))
    for level in range(1, size.bit_length() - 1):
        for h in range(PAIR):
            part = jnp.where((apart >> level) == 1, systems[h], 0.0)
            split = halves(inverses[h])
            half_way = mul_split(split, halves(part), NN)
            inverses[h] = inverses[h] - mul_split(halves(half_way), split, NN)
    for h in range(PAIR):
        inverse_ref[0, h] = inverses[h]
        joined = jnp.concatenate([values[h], keys[h]], axis=1)
        solved = mul_high(inverses[h] * across[h], joined, NN)
        updates_ref[0, h] = solved[:, :depth]
        weights_ref[0, h] = solved[:, depth:]
        scores = jnp.where(lower, mul(queries[h], keys[h], NT), 0.0)
        seen = mul_high(scores, solved, NN)
        mixed_ref[0, h] = seen[:, :depth]
        reach_ref[0, h] = queries[h].astype(F32) - seen[:, depth:]
        moved = mul_high(keys[h], solved, TN)
        offset_ref[0, h] = moved[:, :depth]
        transfer_ref[0, h] = small_eye - moved[:, depth:]


def specs_of(model, depth, size, reverse=False):
    wide = PAIR * depth
    blocks = model // wide
    rows = [pl.BlockSpec((1, size, wide), functools.partial(lambda part, s, g: (s, 0, part * blocks + g), part)) for part in range(3)]
    before = [pl.BlockSpec((1, 8, wide), functools.partial(lambda part, s, g: (s, 0, part * blocks + g), part)) for part in range(3)]
    return rows, before, wide, blocks


def forward_parts(projected, before, taps, rates, depth):
    seqs, size, model3 = projected.shape
    model = model3 // 3
    rows, prior, wide, blocks = specs_of(model, depth, size)
    tap_specs = [pl.BlockSpec((taps.shape[0], wide), functools.partial(lambda part, s, g: (0, part * blocks + g), part)) for part in range(3)]
    rate_spec = pl.BlockSpec((1, size, HEADS), lambda s, g: (s, 0, 0))
    flip_spec = pl.BlockSpec((1, HEADS, size), lambda s, g: (s, 0, 0))

    def out(*dims):
        return pl.BlockSpec((1, PAIR) + dims, lambda s, g: (s, g, 0, 0)), jax.ShapeDtypeStruct((seqs, HEADS) + dims, F32)

    outs = [out(size, size), out(size, depth), out(size, depth), out(size, depth), out(size, depth), out(depth, depth), out(depth, depth)]
    return pl.pallas_call(
        forward_kernel,
        grid=(seqs, HEADS // PAIR),
        in_specs=rows + prior + tap_specs + [rate_spec, flip_spec],
        out_specs=[o[0] for o in outs],
        out_shape=[o[1] for o in outs],
        compiler_params=pltpu.CompilerParams(vmem_limit_bytes=56 * 2**20),
        name="delta_forward",
    )(projected, projected, projected, before, before, before, taps, taps, taps, rates, jnp.swapaxes(rates, 1, 2))


def backward_kernel(
    q_ref, k_ref, v_ref, qb_ref, kb_ref, vb_ref, qt_ref, kt_ref, vt_ref, rates_ref,
    inverse_ref, updates_ref, weights_ref, state_ref, grad_ref, leaving_ref,
    rows_ref, prior_ref, taps_ref, rate_ref,
):
    depth = state_ref.shape[-1]
    size = q_ref.shape[1]
    first = pl.program_id(1) * PAIR
    row = lax.broadcasted_iota(jnp.int32, (size, size), 0)
    col = lax.broadcasted_iota(jnp.int32, (size, size), 1)
    strict = row > col
    lower = row >= col
    index8 = lax.broadcasted_iota(jnp.int32, (8, depth), 0)
    for h in range(PAIR):
        lanes = slice(h * depth, (h + 1) * depth)

        def load(ref, before, taps):
            return (
                ref[0, :, lanes].astype(F32),
                before[0, :, lanes].astype(F32),
                taps[:, lanes].astype(F32),
            )

        def active(parts):
            conv = conv_parts(*parts)
            gate = jax.nn.sigmoid(conv)
            return conv, gate, conv * gate

        raw = [load(q_ref, qb_ref, qt_ref), load(k_ref, kb_ref, kt_ref), load(v_ref, vb_ref, vt_ref)]
        acts = [active(parts) for parts in raw]
        q_scale = unit_scale(acts[0][2])
        k_scale = unit_scale(acts[1][2])
        q = (acts[0][2] * q_scale * depth ** (-0.5)).astype(BF16)
        k = (acts[1][2] * k_scale).astype(BF16)
        v = acts[2][2].astype(BF16)
        column = column_of(rates_ref[0], first + h)
        inverse = inverse_ref[0, h]
        state = state_ref[0, h]
        grad = grad_ref[0, h]
        leaving = leaving_ref[0, h]
        gram = jnp.where(strict, mul(k, k, NT), 0.0)
        scores = jnp.where(lower, mul(q, k, NT), 0.0)
        errors = updates_ref[0, h] - mul_high(weights_ref[0, h], state, NN)
        missed = v.astype(F32) - mul_high(k, state, NN) - mul_high(gram, errors, NN)
        grad_errors = mul_high(scores, grad, TN) + mul_high(k, leaving, NN)
        grad_right = mul_high(inverse, grad_errors, TN)
        grad_scores = jnp.where(lower, mul_high(grad, errors, NT), 0.0)
        grad_system = jnp.where(strict, -mul_high(grad_right, errors, NT), 0.0) * column
        grad_v = grad_right * column
        grad_q = mul_high(grad, state, NT) + mul_high(grad_scores, k, NN)
        grad_k = (
            mul_high(grad_scores, q, TN)
            + mul_high(errors, leaving, NT)
            - mul_high(grad_v, state, NT)
            + mul_high(grad_system, k, NN)
            + mul_high(grad_system, k, TN)
        )
        rate_ref[0, h] = jnp.sum(grad_right * missed, axis=1, keepdims=True)
        q_un, k_un = acts[0][2], acts[1][2]
        grad_q = (
            q_scale * grad_q
            - q_un * (q_scale * q_scale * q_scale * jnp.sum(grad_q * q_un, axis=1, keepdims=True))
        ) * depth ** (-0.5)
        grad_k = k_scale * grad_k - k_un * (
            k_scale * k_scale * k_scale * jnp.sum(grad_k * k_un, axis=1, keepdims=True)
        )
        for part, grad_act in enumerate((grad_q, grad_k, grad_v)):
            conv, gate, _ = acts[part]
            rows, before, taps = raw[part]
            width = taps.shape[0]
            grad_conv = grad_act * (gate * (1.0 + conv * (1.0 - gate)))
            total = None
            ahead = None
            for lag in range(width):
                by = width - 1 - lag
                tap = taps[lag : lag + 1]
                term = tap * shifted_up(grad_conv, by)
                total = term if total is None else total + term
                taps_ref[0, part, lag : lag + 1, lanes] = jnp.sum(
                    grad_conv * shifted_down(rows, before, by), axis=0, keepdims=True
                )
                if by:
                    early = jnp.where(index8 >= 8 - by, tap * pltpu.roll(grad_conv[:8], 8 - by, 0), 0.0)
                    ahead = early if ahead is None else ahead + early
            rows_ref[part, 0, :, lanes] = total
            prior_ref[0, part, :, lanes] = ahead


def backward_parts(projected, before, taps, rates, inverse, updates, weights, state, grad, leaving, depth):
    seqs, size, model3 = projected.shape
    model = model3 // 3
    width = taps.shape[0]
    rows, prior, wide, blocks = specs_of(model, depth, size)
    tap_specs = [pl.BlockSpec((width, wide), functools.partial(lambda part, s, g: (0, part * blocks + g), part)) for part in range(3)]
    rate_spec = pl.BlockSpec((1, size, HEADS), lambda s, g: (s, 0, 0))

    def heads(*dims):
        return pl.BlockSpec((1, PAIR) + dims, lambda s, g: (s, g, 0, 0))

    return pl.pallas_call(
        backward_kernel,
        grid=(seqs, HEADS // PAIR),
        in_specs=rows + prior + tap_specs + [rate_spec, heads(size, size), heads(size, depth), heads(size, depth), heads(depth, depth), heads(size, depth), heads(depth, depth)],
        out_specs=[
            pl.BlockSpec((3, 1, size, wide), lambda s, g: (0, s, 0, g)),
            pl.BlockSpec((1, 3, 8, wide), lambda s, g: (s, 0, 0, g)),
            pl.BlockSpec((1, 3, width, wide), lambda s, g: (s, 0, 0, g)),
            heads(size, 1),
        ],
        out_shape=[
            jax.ShapeDtypeStruct((3, seqs, size, model), F32),
            jax.ShapeDtypeStruct((seqs, 3, 8, model), F32),
            jax.ShapeDtypeStruct((seqs, 3, width, model), F32),
            jax.ShapeDtypeStruct((seqs, HEADS, size, 1), F32),
        ],
        compiler_params=pltpu.CompilerParams(vmem_limit_bytes=56 * 2**20),
        name="delta_backward",
    )(projected, projected, projected, before, before, before, taps, taps, taps, rates, inverse, updates, weights, state, grad, leaving)


def passed_along(value, axis, by):
    peers = lax.axis_size(axis)
    pairs = [(i, i + by) for i in range(peers) if 0 <= i + by < peers]
    return lax.ppermute(value, axis, pairs)


def apply_map(transfer, state, offset):
    return jnp.einsum("shij,shjk->shik", transfer, state, precision=lax.Precision.HIGH) + offset


def rows_times(left, right):
    return jnp.einsum("sga,ab->sgb", left, right, preferred_element_type=F32)


def rows_back(grad, weight):
    return jnp.einsum("sgb,ab->sga", grad, weight, preferred_element_type=F32)


def weight_grad(left, right):
    return jnp.einsum("sga,sgb->ab", left, right, preferred_element_type=F32)


def norm_back(rows, scale, gain, grad):
    weighted = grad * gain
    gain_grad = jnp.sum(grad * rows * scale, axis=tuple(range(rows.ndim - 1)))
    width = rows.shape[-1]
    row_grad = scale * weighted - rows * scale**3 * (
        jnp.sum(weighted * rows, axis=-1, keepdims=True) / width
    )
    return (gain_grad, row_grad)


BOTH = ("dp", "cp")


def per_device(
    block_input, mixer_gain, qkv_weight, conv_taps, beta_weight, out_gain,
    proj_weight, ffn_gain, gate_up, down_weight, cotangent,
):
    seqs, seg_len, model = block_input.shape
    width = conv_taps.shape[0]
    depth = model // HEADS
    peers = lax.axis_size(BOTH)
    share = model // peers
    tap_share = conv_taps.shape[1]
    small = jnp.concatenate(
        [mixer_gain, ffn_gain, beta_weight.reshape(-1), conv_taps.reshape(-1)]
    )
    small = jnp.pad(small, (0, 1024 - small.size)).reshape(8, 128)
    small = lax.all_gather(small, BOTH, axis=0, tiled=False).reshape(peers, 1024)
    w_qkv = lax.all_gather(qkv_weight, BOTH, axis=0, tiled=True)
    w_proj = lax.all_gather(proj_weight, BOTH, axis=0, tiled=True)
    w_gateup = lax.all_gather(gate_up, BOTH, axis=0, tiled=True)
    w_down = lax.all_gather(down_weight, BOTH, axis=0, tiled=True)
    gain_one = small[:, :share].reshape(-1)
    gain_two = small[:, share : 2 * share].reshape(-1)
    at = 2 * share
    w_beta = small[:, at : at + share * HEADS].reshape(model, HEADS)
    at += share * HEADS
    taps = small[:, at : at + width * tap_share].reshape(peers, width, tap_share)
    taps = jnp.swapaxes(taps, 0, 1).reshape(width, peers * tap_share)

    gain_outf = out_gain.astype(F32)
    resid_in = block_input.astype(F32)
    scale_one = lax.rsqrt(jnp.mean(resid_in * resid_in, axis=-1, keepdims=True) + norm_eps)
    normed_one = (resid_in * scale_one * gain_one.astype(F32)).astype(BF16)
    projected = rows_times(normed_one, w_qkv).astype(BF16)
    tail = projected[:, seg_len - (width - 1) :, :]
    before = jnp.pad(passed_along(tail, "cp", 1), ((0, 0), (8 - (width - 1), 0), (0, 0)))
    rates = jax.nn.sigmoid(rows_times(normed_one, w_beta))
    inverse, updates, weights, reach, alone, transfer, offset = forward_parts(
        projected, before, taps, rates, depth
    )
    carried = jnp.zeros_like(offset)
    for step in range(lax.axis_size("cp") - 1):
        sent = offset if step == 0 else apply_map(transfer, carried, offset)
        carried = passed_along(sent.astype(BF16), "cp", 1).astype(F32)
    mixed = alone + jnp.einsum("shtd,shde->shte", reach, carried, precision=lax.Precision.HIGH)
    scale_mix = lax.rsqrt(jnp.mean(mixed * mixed, axis=-1, keepdims=True) + norm_eps)
    mixed_low = jnp.swapaxes(mixed * scale_mix * gain_outf, 1, 2).reshape(seqs, seg_len, model).astype(BF16)
    attn = rows_times(mixed_low, w_proj)
    middle = resid_in + attn
    scale_two = lax.rsqrt(jnp.mean(middle * middle, axis=-1, keepdims=True) + norm_eps)
    gain_twof = gain_two.astype(F32)
    normed_two = (middle * scale_two * gain_twof).astype(BF16)
    gates = rows_times(normed_two, w_gateup)
    half = gates.shape[-1] // 2
    gate_part = gates[..., :half]
    up_part = gates[..., half:]
    hidden = (jax.nn.silu(gate_part) * up_part).astype(BF16)
    ffn_out = rows_times(hidden, w_down)
    result = middle + ffn_out
    squares = jnp.stack(
        [jnp.sum(result * result), jnp.sum(attn * attn), jnp.sum(ffn_out * ffn_out)]
    )
    upstream = cotangent.astype(F32)
    grad_down = weight_grad(hidden, cotangent).astype(BF16)
    grad_hidden = rows_back(cotangent, w_down)
    sigma = jax.nn.sigmoid(gate_part)
    grad_gate = grad_hidden * up_part * (sigma * (1.0 + gate_part * (1.0 - sigma)))
    grad_up = grad_hidden * (gate_part * sigma)
    grad_gates = jnp.concatenate([grad_gate, grad_up], axis=-1).astype(BF16)
    grad_gateup = weight_grad(normed_two, grad_gates).astype(BF16)
    grad_normed_two = rows_back(grad_gates, w_gateup)
    grad_ffn, grad_from_norm = norm_back(middle, scale_two, gain_twof, grad_normed_two)
    grad_middle = upstream + grad_from_norm
    grad_attn = grad_middle.astype(BF16)
    grad_proj = weight_grad(mixed_low, grad_attn).astype(BF16)
    grad_normed_mix = rows_back(grad_attn, w_proj).astype(BF16).astype(F32)
    grad_normed_mix = jnp.swapaxes(grad_normed_mix.reshape(seqs, seg_len, HEADS, depth), 1, 2)
    grad_out, grad_mixed = norm_back(mixed, scale_mix, gain_outf, grad_normed_mix)
    local_part = jnp.einsum("shtd,shte->shde", reach, grad_mixed, precision=lax.Precision.HIGH)
    flipped = jnp.swapaxes(transfer, -1, -2)
    incoming = jnp.zeros_like(local_part)
    for step in range(lax.axis_size("cp") - 1):
        sent = local_part if step == 0 else apply_map(flipped, incoming, local_part)
        incoming = passed_along(sent.astype(BF16), "cp", -1).astype(F32)
    grad_rows, grad_prior, grad_taps, grad_rates = backward_parts(
        projected, before, taps, rates, inverse, updates, weights, carried, grad_mixed, incoming, depth
    )
    returned = passed_along(grad_prior, "cp", -1)
    grad_rows = jnp.concatenate(
        [
            grad_rows[:, :, : seg_len - 8],
            grad_rows[:, :, seg_len - 8 :] + jnp.swapaxes(returned, 0, 1),
        ],
        axis=2,
    ).astype(BF16)
    grad_projected = jnp.moveaxis(grad_rows, 0, 2).reshape(seqs, seg_len, 3 * model)
    grad_rates = jnp.swapaxes(grad_rates[..., 0], 1, 2)
    grad_logits = grad_rates * rates * (1.0 - rates)
    grad_qkv = weight_grad(normed_one, grad_projected).astype(BF16)
    grad_beta = jnp.einsum("sga,sgb->ab", normed_one.astype(F32), grad_logits, precision=lax.Precision.HIGH)
    grad_normed_one = rows_back(grad_projected, w_qkv)
    grad_normed_one = grad_normed_one + jnp.einsum(
        "sgb,ab->sga", grad_logits, w_beta.astype(F32), precision=lax.Precision.HIGH
    )
    grad_mixer, grad_from_first = norm_back(resid_in, scale_one, gain_one.astype(F32), grad_normed_one)
    grad_input = grad_middle + grad_from_first
    grad_conv = jnp.moveaxis(jnp.sum(grad_taps, axis=0), 0, 1).reshape(width, 3 * model)
    grad_conv = jnp.swapaxes(grad_conv.reshape(width, peers, tap_share), 0, 1).reshape(-1)
    pieces = [grad_mixer, grad_ffn, grad_beta.reshape(-1), grad_conv, squares, grad_out]
    sizes = [p.size for p in pieces]
    packed = jnp.concatenate(pieces)
    packed = jnp.pad(packed, (0, -packed.size % 1024)).reshape(-1, 128)
    packed = lax.psum(packed, BOTH).reshape(-1)
    ends = [sum(sizes[: i + 1]) for i in range(len(sizes))]
    starts = [0] + ends[:-1]
    me = lax.axis_index(BOTH)

    def mine(i):
        own = sizes[i] // peers
        return lax.dynamic_slice(packed[starts[i] : ends[i]], (me * own,), (own,))

    rms_values = jnp.sqrt(packed[starts[4] : ends[4]] / (result.size * peers))

    def scattered(grad):
        return lax.psum_scatter(grad, BOTH, scatter_dimension=0, tiled=True).astype(F32)

    return (
        result.astype(BF16),
        grad_input,
        mine(0),
        scattered(grad_qkv),
        mine(3).reshape(width, tap_share),
        mine(2).reshape(share, HEADS),
        packed[starts[5] : ends[5]],
        scattered(grad_proj),
        mine(1),
        scattered(grad_gateup),
        scattered(grad_down),
        rms_values,
    )


def solution(mesh):
    both = P(BOTH)
    rows = P(BOTH, None)
    tokens = P("dp", "cp", None)
    taps = P(None, BOTH)
    in_specs = (tokens, both, rows, taps, rows, P(), rows, both, rows, rows, tokens)
    out_specs = (tokens, tokens, both, rows, taps, rows, P(), rows, both, rows, rows, P())
    return jax.shard_map(
        per_device, mesh=mesh, in_specs=in_specs, out_specs=out_specs, check_vma=False
    )
```

time: 3500 us -> 1280 us (0.37)
  other arithmetic: 1370 us -> 29.7 us
  waiting for transfers between devices: 1300 us -> 921 us
  matrix products: 416 us -> 110 us
  blocking collectives: 212 us -> 71.2 us
  local copies, waits for them, and re-layouts: 149 us -> 39.2 us
  Pallas kernels: 0 us -> 72.7 us
    another operation x42 -> x2, other arithmetic: 1280 us -> 1.8 us  [the longest x28 958 us: group_step(): jax.scipy.linalg.solve_triangular(system, rate_heads[:, :, None] * (value...]
    reduce_scatter x4, waiting for transfers between devices: 1000 us -> 657 us  [scattered(): lax.psum_scatter(grad, BOTH, scatter_dimension=0, tiled=True).astype(F32)]
    dot_general x153 -> x21, matrix products: 377 us -> 110 us  [the longest x5 33 us: rows_times(): return jnp.einsum('sga,ab->sgb', left, right, preferred_element_type=F32)]
    unnamed x12 -> x9, waiting for transfers between devices: 173 us -> 2.66 us
    all_gather x4, waiting for transfers between devices: 0.04 us -> 88.4 us  [the longest x1 56.2 us: per_device(): w_down = lax.all_gather(down_weight, BOTH, axis=0, tiled=True)]
    psum x0 -> x1, waiting for transfers between devices: none -> 85.9 us  [per_device(): packed = lax.psum(packed, BOTH).reshape(-1)]
    unnamed x2 -> x0, blocking collectives: 80.4 us -> none
    pallas_call x0 -> x2, Pallas kernels: none -> 72.7 us  [the longest x1 36.9 us: forward_parts(): pl.pallas_call(forward_kernel, grid=(seqs, HEADS // PAIR), in_specs=rows...]
  transfers between devices with their start and end apart: 18 -> 17, of which waited for: 13 -> 13; matrix products, arithmetic and copies ran while one was open for 27% -> 8% of each run, Pallas kernels for 0% -> 3%
where the time goes in v1:
time: 1280 us
  waiting for transfers between devices  921 us (72%)
  matrix products  110 us (9%)
  Pallas kernels  72.7 us (6%)
  blocking collectives  71.2 us (6%)
  local copies, waits for them, and re-layouts  39.2 us (3%)
  other arithmetic  29.7 us (2%)
  starting transfers between devices  21.7 us (2%)
  between operations  14.7 us (1%)
    reduce_scatter x4, waiting for transfers between devices, scattered(): lax.psum_scatter(grad, BOTH, scatter_dimension=0, tiled=True).astype(F32)  657 us
    ppermute x8, waiting for transfers between devices, passed_along(): return lax.ppermute(value, axis, pairs)  86.6 us
    psum x1, waiting for transfers between devices, per_device(): packed = lax.psum(packed, BOTH).reshape(-1)  85.9 us
    all_gather x1, blocking collectives, per_device(): lax.all_gather(small, BOTH, axis=0, tiled=False).reshape(peers, 1024)  71.2 us
    all_gather x1, waiting for transfers between devices, per_device(): w_down = lax.all_gather(down_weight, BOTH, axis=0, tiled=True)  56.2 us
    pallas_call x1, Pallas kernels, forward_parts(): pl.pallas_call(forward_kernel, grid=(seqs, HEADS // PAIR), in_specs=rows...  36.9 us
    pallas_call x1, Pallas kernels, backward_parts(): pl.pallas_call(backward_kernel, grid=(seqs, HEADS // PAIR), in_specs=rows...  35.8 us
    dot_general x5, matrix products, rows_times(): return jnp.einsum('sga,ab->sgb', left, right, preferred_element_type=F32)  33 us
  transfers between devices with their start and end apart: 17, of which 13 were waited for; matrix products, arithmetic and copies ran while one was open for 8% of the time, Pallas kernels for 3%

profile of v1, /device:TPU:0, one launch (start us, length us, event | category | flops | bytes accessed | tf_op | source)
XLA Modules:
  0.0 1279.9 jit_solution(5370641147095533491)
XLA Ops:
  12.4 71.2 %all_gather.15 = bf16[32,8,128]{2,1,0:T(8,128)(2,1)S(1)} all-gather(bf16[1,8,128]{2,1,0:T(8,128)(2,1)S(1)} %fusion.64), channel_id=1, replica_groups=mesh['dp'=8,'cp'=4] {'dp','cp'}, dimensions={0}, use_global_device_ids=true | all-gather | bytes 67584 | tf_op jit(solution)/shard_map/all_gather | solution.py:353
  85.2 6.7 fusion.13.q_ref.k_ref.v_ref
  92.7 2.2 collective-permute-start
  98.5 36.9 %delta_forward.1 = (f32[2,8,256,256]{3,2,1,0:T(8,128)}, f32[2,8,256,128]{3,2,1,0:T(8,128)}, f32[2,8,256,128]{3,2,1,0:T(8,128)}, f32[2,8,256,128]{3,2,1,0:T(8,128...) custom-call(bf16[2,256,3072]{2,1,0:T(8,128)(2,1)} %copy-done, ...), custom_call_target="tpu_custom_call" | custom-call | tf_op jit(solution)/shard_map/delta_forward/pallas_call | solution.py:173
  136.9 3.4 collective-permute-start.1
  140.3 10.8 collective-permute-done.1
  152.8 4.6 collective-permute-start.2
  157.4 14.8 %collective-permute-done.2 = bf16[2,8,128,128]{3,2,1,0:T(8,128)(2,1)S(1)} collective-permute-done((bf16[2,8,128,128]{3,2,1,0:T(8,128)(2,1)S(1)}, bf16[2,8,128,128]{3,2,1,0:T(8,128)(2,1)S(1)}, u32[]{:S(2)}, u32[]{:S(2)}) %collective-permute-start.2) | collective-permute-done | bytes 524320 | tf_op jit(solution)/shard_map/ppermute | solution.py:307
  173.5 5.4 collective-permute-start.3
  179.0 20.7 %collective-permute-done.3 = bf16[2,8,128,128]{3,2,1,0:T(8,128)(2,1)} collective-permute-done((bf16[2,8,128,128]{3,2,1,0:T(8,128)(2,1)}, bf16[2,8,128,128]{3,2,1,0:T(8,128)(2,1)}, u32[]{:S(2)}, u32[]{:S(2)}) %collective-permute-start.3) | collective-permute-done | bytes 524320 | tf_op jit(solution)/shard_map/ppermute | solution.py:307
  199.7 1.9 fusion.71
  203.9 2.3 copy.105
  206.1 6.4 multiply_reduce_fusion.6
  212.5 32.2 %all-gather.9.cloned.1.call-done = bf16[1024,5632]{1,0:T(8,128)(2,1)} async-done(((bf16[32,5632]{1,0:T(8,128)(2,1)}), bf16[1024,5632]{1,0:T(8,128)(2,1)}) %all-gather.9.cloned.1.call-update) | async-done | bytes 11534352 | tf_op jit(solution)/shard_map/all_gather | solution.py:356
  244.7 12.2 fusion.2
  256.9 56.2 %all-gather.11.cloned.1.call-done = bf16[2816,1024]{1,0:T(8,128)(2,1)} async-done(((bf16[88,1024]{1,0:T(8,128)(2,1)}), bf16[2816,1024]{1,0:T(8,128)(2,1)}) %all-gather.11.cloned.1.call-update) | async-done | bytes 5767184 | tf_op jit(solution)/shard_map/all_gather | solution.py:357
  313.1 11.8 multiply_convert_fusion.1
  324.9 11.4 fusion
  336.3 7.2 multiply_reduce_fusion
  345.5 2.6 fusion.34
  348.1 2.9 copy.107
  351.0 2.9 copy.108
  353.9 2.6 fusion.26
  356.6 1.9 multiply_subtract_fusion.grad_ref
  358.5 2.0 fusion.70
  361.8 15.0 %collective-permute-done.4 = bf16[2,8,128,128]{3,2,1,0:T(8,128)(2,1)S(1)} collective-permute-done((bf16[2,8,128,128]{3,2,1,0:T(8,128)(2,1)S(1)}, bf16[2,8,128,128]{3,2,1,0:T(8,128)(2,1)S(1)}, u32[]{:S(2)}, u32[]{:S(2)}) %collective-permute-start.4) | collective-permute-done | bytes 524320 | tf_op jit(solution)/shard_map/ppermute | solution.py:307
  378.9 14.2 %collective-permute-done.5 = bf16[2,8,128,128]{3,2,1,0:T(8,128)(2,1)S(1)} collective-permute-done((bf16[2,8,128,128]{3,2,1,0:T(8,128)(2,1)S(1)}, bf16[2,8,128,128]{3,2,1,0:T(8,128)(2,1)S(1)}, u32[]{:S(2)}, u32[]{:S(2)}) %collective-permute-start.5) | collective-permute-done | bytes 524320 | tf_op jit(solution)/shard_map/ppermute | solution.py:307
  395.1 2.2 convert_element_type.141.state_ref
  397.2 11.2 collective-permute-done.6
  409.5 35.8 %delta_backward.1 = (f32[3,2,256,1024]{3,2,1,0:T(8,128)}, f32[2,3,8,1024]{3,2,1,0:T(8,128)}, f32[2,3,4,1024]{3,2,1,0:T(4,128)}, f32[2,8,256,1]{3,2,1,0:T(8,128)}) custom-call(bf16[2,256,3072]{2,1,0:T(8,128)(2,1)} %copy-done, bf16[2,256,3072]{2,1,0:T(8,128)(2,1)} %copy-done, bf16[2,256,3072]{2,1,0:T(8,128)(2,1)} %copy-done, ...), custom_call_target="tpu_custom_call" | custom-call | tf_op jit(solution)/shard_map/delta_backward/pallas_call | solution.py:283
  445.3 5.0 slice.113
  452.0 3.8 copy.116
  455.7 2.0 convolution_bitcast_fusion
  459.4 4.0 maximum_bitcast_fusion
  463.4 4.7 copy.114
  468.1 6.6 fusion.4
  474.7 2.6 fusion.24
  477.3 2.0 concatenate.17
  480.1 3.9 bitcast_convert_fusion.3
  484.0 7.6 bitcast_convert_fusion.1
  491.9 7.8 bitcast_convert_fusion.2
  499.8 12.2 bitcast_convert_fusion
  512.1 3.5 fusion.21
  515.5 85.9 %all-reduce.5.cloned.1.call-done = f32[184,128]{1,0:T(8,128)} async-done(((f32[184,128]{1,0:T(8,128)}), f32[184,128]{1,0:T(8,128)}) %all-reduce.5.cloned.1.call-update) | async-done | bytes 94224 | tf_op jit(solution)/shard_map/psum | solution.py:449
  608.9 133.5 %reduce-scatter.7.cloned.1.call-done = bf16[32,1024]{1,0:T(8,128)(2,1)} async-done(((bf16[1024,1024]{1,0:T(8,128)(2,1)}), bf16[32,1024]{1,0:T(8,128)(2,1)}) %reduce-scatter.7.cloned.1.call-update) | async-done | bytes 65552 | tf_op jit(solution)/shard_map/reduce_scatter | solution.py:461
  743.9 117.6 %reduce-scatter.5.cloned.1.call-done = bf16[32,3072]{1,0:T(8,128)(2,1)} async-done(((bf16[1024,3072]{1,0:T(8,128)(2,1)}), bf16[32,3072]{1,0:T(8,128)(2,1)}) %reduce-scatter.5.cloned.1.call-update) | async-done | bytes 196624 | tf_op jit(solution)/shard_map/reduce_scatter | solution.py:461
  863.2 156.4 %reduce-scatter.11.cloned.1.call-done = bf16[88,1024]{1,0:T(8,128)(2,1)} async-done(((bf16[2816,1024]{1,0:T(8,128)(2,1)}), bf16[88,1024]{1,0:T(8,128)(2,1)}) %reduce-scatter.11.cloned.1.call-update) | async-done | bytes 180240 | tf_op jit(solution)/shard_map/reduce_scatter | solution.py:461
  1021.3 250.0 %reduce-scatter.9.cloned.1.call-done = bf16[32,5632]{1,0:T(8,128)(2,1)} async-done(((bf16[1024,5632]{1,0:T(8,128)(2,1)}), bf16[32,5632]{1,0:T(8,128)(2,1)}) %reduce-scatter.9.cloned.1.call-update) | async-done | bytes 360464 | tf_op jit(solution)/shard_map/reduce_scatter | solution.py:461
  (140 shorter events, 44.9 us)
Async XLA Ops:
  7.2 77.7 %copy-start.4 = (bf16[2,256,1024]{2,1,0:T(8,128)(2,1)S(1)}, bf16[2,256,1024]{2,1,0:T(8,128)(2,1)}, u32[]{:S(2)}) copy-start(bf16[2,256,1024]{2,1,0:T(8,128)(2,1)} %param.11) | copy-start | bytes 3145732
  7.2 78.0 %all-gather.5.cloned.1.call-start = ((), (), s32[]{:S(2)}) async-start(), calls=%async_computation.4 | async-start | bytes 6488064 | tf_op jit(solution)/shard_map/all_gather | solution.py:354
  7.9 198.2 %all-gather.7.cloned.1.call-start = ((), (), s32[]{:S(2)}) async-start(), calls=%async_computation.5 | async-start | bytes 2162688 | tf_op jit(solution)/shard_map/all_gather | solution.py:355
  8.7 236.0 %all-gather.9.cloned.1.call-start = ((), (), s32[]{:S(2)}) async-start(), calls=%async_computation.6 | async-start | bytes 11894784 | tf_op jit(solution)/shard_map/all_gather | solution.py:356
  9.4 303.7 %all-gather.11.cloned.1.call-start = ((), (), s32[]{:S(2)}) async-start(), calls=%async_computation.7 | async-start | bytes 5947392 | tf_op jit(solution)/shard_map/all_gather | solution.py:357
  10.0 591.4 %all-reduce.5.cloned.1.call-start = ((), (), s32[]{:S(2)}) async-start(), calls=%async_computation.8 | async-start | bytes 188416 | tf_op jit(solution)/shard_map/psum | solution.py:449
  85.2 9.7 copy-start.5
  85.2 9.7 copy-start.20
  91.9 6.6 copy-start
  92.7 4.4 collective-permute-start
  95.4 3.1 copy-start.13
  135.4 15.7 %copy-start.3 = (f32[2,8,128,128]{3,2,1,0:T(8,128)S(1)}, f32[2,8,128,128]{3,2,1,0:T(8,128)}, u32[]{:S(2)}) copy-start(f32[2,8,128,128]{3,2,1,0:T(8,128)} %get-tuple-element.25) | copy-start | bytes 3145732
  135.4 36.8 %copy-start.7 = (f32[2,8,128,128]{3,2,1,0:T(8,128)S(1)}, f32[2,8,128,128]{3,2,1,0:T(8,128)}, u32[]{:S(2)}) copy-start(f32[2,8,128,128]{3,2,1,0:T(8,128)} %get-tuple-element.26) | copy-start | bytes 3145732
  136.9 14.2 %collective-permute-start.1 = (bf16[2,8,128,128]{3,2,1,0:T(8,128)(2,1)S(1)}, bf16[2,8,128,128]{3,2,1,0:T(8,128)(2,1)S(1)}, u32[]{:S(2)}, u32[]{:S(2)}) collective-permute-start(bf16[2,8,128,128]{3,2,1,0:T(8,128)(2,1)S(1)} %convert_element_type.128), channel_id=1, source_target_pairs={{0,1},{1,2},{2,3},{4,5},{5,6},{6,7},{8,9},{9,10},{10,11},{12,13},{... | collective-permute-start | bytes 1572872 | tf_op jit(solution)/shard_map/ppermute | solution.py:307
  152.8 26.1 %copy-start.23 = (bf16[128]{0:T(256)(128)(2,1)S(1)}, bf16[128]{0:T(256)(128)(2,1)}, u32[]{:S(2)}) copy-start(bf16[128]{0:T(256)(128)(2,1)} %param.16) | copy-start | bytes 772
  152.8 46.9 %copy-start.11 = (f32[2,8,256,128]{3,2,1,0:T(8,128)S(1)}, f32[2,8,256,128]{3,2,1,0:T(8,128)}, u32[]{:S(2)}) copy-start(f32[2,8,256,128]{3,2,1,0:T(8,128)} %get-tuple-element.24) | copy-start | bytes 6291460
  152.8 19.4 %collective-permute-start.2 = (bf16[2,8,128,128]{3,2,1,0:T(8,128)(2,1)S(1)}, bf16[2,8,128,128]{3,2,1,0:T(8,128)(2,1)S(1)}, u32[]{:S(2)}, u32[]{:S(2)}) collective-permute-start(bf16[2,8,128,128]{3,2,1,0:T(8,128)(2,1)S(1)} %fusion.37), channel_id=1, source_target_pairs={{0,1},{1,2},{2,3},{4,5},{5,6},{6,7},{8,9},{9,10},{10,11},{12,13},{... | collective-permute-start | bytes 1572872 | tf_op jit(solution)/shard_map/ppermute | solution.py:307
  173.5 26.2 %collective-permute-start.3 = (bf16[2,8,128,128]{3,2,1,0:T(8,128)(2,1)}, bf16[2,8,128,128]{3,2,1,0:T(8,128)(2,1)}, u32[]{:S(2)}, u32[]{:S(2)}) collective-permute-start(bf16[2,8,128,128]{3,2,1,0:T(8,128)(2,1)} %fusion.38), channel_id=1, source_target_pairs={{0,1},{1,2},{2,3},{4,5},{5,6},{6,7},{8,9},{9,10},{10,11},{12,13},{... | collective-permute-start | bytes 1572872 | tf_op jit(solution)/shard_map/ppermute | solution.py:307
  199.7 1.9 copy-start.15
  313.1 23.2 %slice-start = ((s8[5767168]{0:T(1024)(128)(4,1)}), s8[4194304]{0:T(1024)(128)(4,1)S(1)}, s32[]{:S(2)}) async-start(s8[5767168]{0:T(1024)(128)(4,1)} %bitcast.139), calls=%async_computation.13 | async-start | bytes 8388608
  324.9 11.4 copy-start.24
  324.9 11.4 copy-start.10
  324.9 11.4 slice-start.1
  336.3 7.2 copy-start.18
  343.5 1.9 copy-start.17
  344.1 1.3 copy-start.8
  353.9 2.7 copy-start.2
  356.6 2.0 copy-start.12
  358.5 2.0 copy-start.1
  360.5 16.3 %collective-permute-start.4 = (bf16[2,8,128,128]{3,2,1,0:T(8,128)(2,1)S(1)}, bf16[2,8,128,128]{3,2,1,0:T(8,128)(2,1)S(1)}, u32[]{:S(2)}, u32[]{:S(2)}) collective-permute-start(bf16[2,8,128,128]{3,2,1,0:T(8,128)(2,1)S(1)} %get-tuple-element.99), channel_id=1, source_target_pairs={{1,0},{2,1},{3,2},{5,4},{6,5},{7,6},{9,8},{10,9},{11,10},{13,12},{... | collective-permute-start | bytes 1572872 | tf_op jit(solution)/shard_map/ppermute | solution.py:307
  377.6 15.5 %collective-permute-start.5 = (bf16[2,8,128,128]{3,2,1,0:T(8,128)(2,1)S(1)}, bf16[2,8,128,128]{3,2,1,0:T(8,128)(2,1)S(1)}, u32[]{:S(2)}, u32[]{:S(2)}) collective-permute-start(bf16[2,8,128,128]{3,2,1,0:T(8,128)(2,1)S(1)} %fusion.39), channel_id=1, source_target_pairs={{1,0},{2,1},{3,2},{5,4},{6,5},{7,6},{9,8},{10,9},{11,10},{13,12},{... | collective-permute-start | bytes 1572872 | tf_op jit(solution)/shard_map/ppermute | solution.py:307
  393.8 14.6 %collective-permute-start.6 = (bf16[2,8,128,128]{3,2,1,0:T(8,128)(2,1)S(1)}, bf16[2,8,128,128]{3,2,1,0:T(8,128)(2,1)S(1)}, u32[]{:S(2)}, u32[]{:S(2)}) collective-permute-start(bf16[2,8,128,128]{3,2,1,0:T(8,128)(2,1)S(1)} %fusion.40), channel_id=1, source_target_pairs={{1,0},{2,1},{3,2},{5,4},{6,5},{7,6},{9,8},{10,9},{11,10},{13,12},{... | collective-permute-start | bytes 1572872 | tf_op jit(solution)/shard_map/ppermute | solution.py:307
  445.3 6.7 copy-start.16
  450.3 5.4 copy-start.6
  450.3 5.4 copy-start.14
  450.3 8.1 collective-permute-start.7
  455.7 2.3 copy-start.22
  468.1 6.6 copy-start.19
  468.1 6.6 copy-start.21
  474.7 5.3 copy-start.9
  480.0 262.4 %reduce-scatter.7.cloned.1.call-start = ((), (), s32[]{:S(2)}) async-start(), calls=%async_computation.10 | async-start | bytes 2162688 | tf_op jit(solution)/shard_map/reduce_scatter | solution.py:461
  484.0 377.5 %reduce-scatter.5.cloned.1.call-start = ((), (), s32[]{:S(2)}) async-start(), calls=%async_computation.9 | async-start | bytes 6488064 | tf_op jit(solution)/shard_map/reduce_scatter | solution.py:461
  491.6 527.9 %reduce-scatter.11.cloned.1.call-start = ((), (), s32[]{:S(2)}) async-start(), calls=%async_computation.12 | async-start | bytes 5947392 | tf_op jit(solution)/shard_map/reduce_scatter | solution.py:461
  499.8 771.5 %reduce-scatter.9.cloned.1.call-start = ((), (), s32[]{:S(2)}) async-start(), calls=%async_computation.11 | async-start | bytes 11894784 | tf_op jit(solution)/shard_map/reduce_scatter | solution.py:461
Sparse Core Ops, SparseCore 0:
  10.9 71.7 all-gather.4
  85.7 55.5 all-gather.6
  144.1 100.5 all-gather.8
  247.4 65.6 all-gather.10
  480.1 121.2 all-reduce.4
  603.5 138.7 reduce-scatter.6
  748.9 112.4 reduce-scatter.4
  863.8 155.7 reduce-scatter.10
  1021.9 249.3 reduce-scatter.8

commit v2 on v1

--- a/solution.py
+++ b/solution.py
@@ -301,6 +301,123 @@
     )(projected, projected, projected, before, before, before, taps, taps, taps, rates, inverse, updates, weights, state, grad, leaving)
 
 
+BOTH = ("dp", "cp")
+
+
+class Grid:
+    def __init__(self):
+        self.cp = lax.axis_size("cp")
+        group = lax.axis_size("dp")
+        self.core = 2 if group % 2 == 0 else 1
+        self.lo = 2 if group // self.core % 2 == 0 else 1
+        self.hi = group // self.core // self.lo
+        self.sizes = (self.hi, self.lo, self.core, self.cp)
+
+    def place(self):
+        member = lax.axis_index("dp")
+        return (
+            member // (self.lo * self.core),
+            member // self.core % self.lo,
+            member % self.core,
+            lax.axis_index("cp"),
+        )
+
+    def swap(self, value, axis, by):
+        step = [1] * 4
+        for later in range(3):
+            step[2 - later] = step[3 - later] * self.sizes[3 - later]
+        pairs = []
+        for device in range(step[0] * self.sizes[0]):
+            here = device // step[axis] % self.sizes[axis]
+            pairs.append((device, device + ((here ^ by) - here) * step[axis]))
+        return lax.ppermute(value, BOTH, pairs)
+
+    def others(self, value, axis):
+        return [self.swap(value, axis, by) for by in range(1, self.sizes[axis])]
+
+
+HI, LO, CORE, SEG = range(4)
+
+
+def cut_of(columns):
+    return columns // 256 * 128
+
+
+def place_kernel(spot, own_left, own_right, other_left, other_right, *outs):
+    core = spot[2]
+    for away, left, right in ((0, own_left, own_right), (1, other_left, other_right)):
+        if away >= outs[0].shape[2]:
+            continue
+        row = jnp.concatenate([left[0, 0, 0], right[0, 0, 0]], axis=1)
+        at = 0
+        for out in outs:
+            wide = out.shape[-1]
+            out[0, 0, core ^ away, 0] = row[:, at : at + wide]
+            at += wide
+
+
+def gathered(grid, shard, widths):
+    r, total = shard.shape
+    cut = cut_of(total)
+    parts = [shard] + grid.others(shard, SEG)
+    own = []
+    for start, stop, axes in ((0, cut, (LO, HI)), (cut, total, (HI, LO))):
+        value = jnp.stack([part[:, start:stop] for part in parts])
+        for axis in axes:
+            value = jnp.stack([value] + grid.others(value, axis))
+        own.append(value)
+    other = [grid.swap(value, CORE, 1) if grid.core == 2 else value for value in own]
+
+    def source(wide, order):
+        def index(a, b, c, spot):
+            first, second = a ^ spot[0], b ^ spot[1]
+            return (first, second, c ^ spot[3], 0, 0) if order == 0 else (second, first, c ^ spot[3], 0, 0)
+
+        return pl.BlockSpec((1, 1, 1, r, wide), index)
+
+    sources = [source(cut, 0), source(total - cut, 1)]
+    outs = pl.pallas_call(
+        place_kernel,
+        grid_spec=pltpu.PrefetchScalarGridSpec(
+            num_scalar_prefetch=1,
+            grid=(grid.hi, grid.lo, grid.cp),
+            in_specs=sources + sources,
+            out_specs=[
+                pl.BlockSpec((1, 1, grid.core, 1, r, wide), lambda a, b, c, spot: (a, b, 0, c, 0, 0))
+                for wide in widths
+            ],
+        ),
+        out_shape=[jax.ShapeDtypeStruct(grid.sizes + (r, wide), shard.dtype) for wide in widths],
+        name="place_rows",
+    )(jnp.stack(grid.place()), *own, *other)
+    return [out.reshape(-1, out.shape[-1]) for out in outs]
+
+
+def summed_share(grid, value):
+    hi, lo, core, seg = grid.place()
+    columns = value.shape[-1]
+    value = value.reshape(grid.sizes + (-1, columns))
+
+    def pick(array, index, axis):
+        return lax.dynamic_index_in_dim(array, index, axis, keepdims=False)
+
+    def stage(array, axis, dim, here):
+        total = pick(array, here, dim).astype(F32)
+        for by in range(1, grid.sizes[axis]):
+            total = total + grid.swap(pick(array, here ^ by, dim), axis, by).astype(F32)
+        return total
+
+    value = stage(value, CORE, 2, core).astype(BF16)
+    cut = cut_of(columns)
+    left, right = value[..., :cut], value[..., cut:]
+    left = stage(left, LO, 1, lo).astype(BF16)
+    right = stage(right, HI, 0, hi).astype(BF16)
+    left = stage(left, HI, 0, hi)
+    right = stage(right, LO, 0, lo)
+    joined = jnp.concatenate([left, right], axis=-1).astype(BF16)
+    return stage(joined, SEG, 0, seg)
+
+
 def passed_along(value, axis, by):
     peers = lax.axis_size(axis)
     pairs = [(i, i + by) for i in range(peers) if 0 <= i + by < peers]
@@ -331,9 +448,6 @@
         jnp.sum(weighted * rows, axis=-1, keepdims=True) / width
     )
     return (gain_grad, row_grad)
-
-
-BOTH = ("dp", "cp")
 
 
 def per_device(
@@ -346,15 +460,16 @@
     peers = lax.axis_size(BOTH)
     share = model // peers
     tap_share = conv_taps.shape[1]
+    grid = Grid()
     small = jnp.concatenate(
         [mixer_gain, ffn_gain, beta_weight.reshape(-1), conv_taps.reshape(-1)]
     )
-    small = jnp.pad(small, (0, 1024 - small.size)).reshape(8, 128)
-    small = lax.all_gather(small, BOTH, axis=0, tiled=False).reshape(peers, 1024)
-    w_qkv = lax.all_gather(qkv_weight, BOTH, axis=0, tiled=True)
-    w_proj = lax.all_gather(proj_weight, BOTH, axis=0, tiled=True)
-    w_gateup = lax.all_gather(gate_up, BOTH, axis=0, tiled=True)
-    w_down = lax.all_gather(down_weight, BOTH, axis=0, tiled=True)
+    small = jnp.pad(small, (0, share * 128 - small.size)).reshape(share, 128)
+    w_qkv, small = gathered(grid, jnp.concatenate([qkv_weight, small], axis=1), (3 * model, 128))
+    small = small.reshape(peers, share * 128)
+    (w_proj,) = gathered(grid, proj_weight, (model,))
+    (w_gateup,) = gathered(grid, gate_up, gate_up.shape[1:])
+    (w_down,) = gathered(grid, down_weight, (model,))
     gain_one = small[:, :share].reshape(-1)
     gain_two = small[:, share : 2 * share].reshape(-1)
     at = 2 * share
@@ -442,36 +557,29 @@
     grad_input = grad_middle + grad_from_first
     grad_conv = jnp.moveaxis(jnp.sum(grad_taps, axis=0), 0, 1).reshape(width, 3 * model)
     grad_conv = jnp.swapaxes(grad_conv.reshape(width, peers, tap_share), 0, 1).reshape(-1)
-    pieces = [grad_mixer, grad_ffn, grad_beta.reshape(-1), grad_conv, squares, grad_out]
-    sizes = [p.size for p in pieces]
-    packed = jnp.concatenate(pieces)
-    packed = jnp.pad(packed, (0, -packed.size % 1024)).reshape(-1, 128)
-    packed = lax.psum(packed, BOTH).reshape(-1)
-    ends = [sum(sizes[: i + 1]) for i in range(len(sizes))]
-    starts = [0] + ends[:-1]
-    me = lax.axis_index(BOTH)
-
-    def mine(i):
-        own = sizes[i] // peers
-        return lax.dynamic_slice(packed[starts[i] : ends[i]], (me * own,), (own,))
-
-    rms_values = jnp.sqrt(packed[starts[4] : ends[4]] / (result.size * peers))
-
-    def scattered(grad):
-        return lax.psum_scatter(grad, BOTH, scatter_dimension=0, tiled=True).astype(F32)
+    sums = lax.psum(jnp.concatenate([squares, grad_out]), BOTH)
+    rms_values = jnp.sqrt(sums[:3] / (result.size * peers))
+    pieces = [grad_mixer, grad_ffn, grad_beta, grad_conv]
+    pieces = jnp.concatenate([piece.reshape(peers, -1) for piece in pieces], axis=1)
+    pieces = jnp.pad(pieces, ((0, 0), (0, share * 128 - pieces.shape[1])))
+    grad_qkv = jnp.concatenate([grad_qkv, pieces.astype(BF16).reshape(model, 128)], axis=1)
+    share_qkv = summed_share(grid, grad_qkv)
+    own = share_qkv[:, 3 * model :].reshape(-1)
+    share_qkv = share_qkv[:, : 3 * model]
+    ends = [share, 2 * share, 2 * share + share * HEADS, 2 * share + share * HEADS + width * tap_share]
 
     return (
         result.astype(BF16),
         grad_input,
-        mine(0),
-        scattered(grad_qkv),
-        mine(3).reshape(width, tap_share),
-        mine(2).reshape(share, HEADS),
-        packed[starts[5] : ends[5]],
-        scattered(grad_proj),
-        mine(1),
-        scattered(grad_gateup),
-        scattered(grad_down),
+        own[: ends[0]],
+        share_qkv,
+        own[ends[2] : ends[3]].reshape(width, tap_share),
+        own[ends[1] : ends[2]].reshape(share, HEADS),
+        sums[3:],
+        summed_share(grid, grad_proj),
+        own[ends[0] : ends[1]],
+        summed_share(grid, grad_gateup),
+        summed_share(grid, grad_down),
         rms_values,
     )
 

time: 1280 us -> 719 us (0.56)
  waiting for transfers between devices: 921 us -> 207 us
  starting transfers between devices: 21.7 us -> 111 us
  Pallas kernels: 72.7 us -> 121 us
  other arithmetic: 29.7 us -> 72.4 us
  blocking collectives: 71.2 us -> 40.4 us
    reduce_scatter x4 -> x0, waiting for transfers between devices: 657 us -> none  [scattered(): lax.psum_scatter(grad, BOTH, scatter_dimension=0, tiled=True).astype(F32)]
    ppermute x0 -> x68, waiting for transfers between devices: none -> 188 us  [swap(): return lax.ppermute(value, BOTH, pairs)]
    ppermute x0 -> x68, starting transfers between devices: none -> 90.4 us  [swap(): return lax.ppermute(value, BOTH, pairs)]
    all_gather x4 -> x0, waiting for transfers between devices: 88.4 us -> none  [the longest x1 56.2 us: per_device(): w_down = lax.all_gather(down_weight, BOTH, axis=0, tiled=True)]
    psum x1 -> x0, waiting for transfers between devices: 85.9 us -> none  [per_device(): packed = lax.psum(packed, BOTH).reshape(-1)]
    all_gather x1 -> x0, blocking collectives: 71.2 us -> none  [per_device(): lax.all_gather(small, BOTH, axis=0, tiled=False).reshape(peers, 1024)]
    ppermute x8, waiting for transfers between devices: 86.6 us -> 19.4 us  [passed_along(): return lax.ppermute(value, axis, pairs)]
    pallas_call x0 -> x4, Pallas kernels: none -> 48.8 us  [gathered(): pl.pallas_call(place_kernel, grid_spec=pltpu.PrefetchScalarGridSpec(num_s...]
  transfers between devices with their start and end apart: 17 -> 76, of which waited for: 13 -> 34; matrix products, arithmetic and copies ran while one was open for 8% -> 20% of each run, Pallas kernels for 3% -> 15%
where the time goes in v2:
time: 719 us; the launch traced here: 709 us
  waiting for transfers between devices  207 us (29%)
  Pallas kernels  121 us (17%)
  starting transfers between devices  111 us (15%)
  matrix products  102 us (14%)
  other arithmetic  72.4 us (10%)
  local copies, waits for them, and re-layouts  51.6 us (7%)
  blocking collectives  40.4 us (6%)
    ppermute x68, waiting for transfers between devices, swap(): return lax.ppermute(value, BOTH, pairs)  188 us
    ppermute x68, starting transfers between devices, swap(): return lax.ppermute(value, BOTH, pairs)  90.4 us
    pallas_call x4, Pallas kernels, gathered(): pl.pallas_call(place_kernel, grid_spec=pltpu.PrefetchScalarGridSpec(num_s...  48.8 us
    psum x1, blocking collectives, per_device(): sums = lax.psum(jnp.concatenate([squares, grad_out]), BOTH)  40.4 us
    pallas_call x1, Pallas kernels, forward_parts(): pl.pallas_call(forward_kernel, grid=(seqs, HEADS // PAIR), in_specs=rows...  36.9 us
    pallas_call x1, Pallas kernels, backward_parts(): pl.pallas_call(backward_kernel, grid=(seqs, HEADS // PAIR), in_specs=rows...  35.8 us
    dot_general x5, matrix products, rows_times(): return jnp.einsum('sga,ab->sgb', left, right, preferred_element_type=F32)  34.4 us
    dot_general x4, matrix products, rows_back(): return jnp.einsum('sgb,ab->sga', grad, weight, preferred_element_type=F32)  33 us
  transfers between devices with their start and end apart: 76, of which 34 were waited for; matrix products, arithmetic and copies ran while one was open for 20% of the time, Pallas kernels for 15%

profile of v2, /device:TPU:0, one launch (start us, length us, event | category | flops | bytes accessed | tf_op | source)
XLA Modules:
  0.0 709.1 jit_solution(1562290952934502152)
XLA Ops:
  4.1 5.1 collective-permute-start.2
  9.8 3.7 collective-permute-start.15
  18.9 6.4 collective-permute-done.15
  25.3 6.7 collective-permute-start.13
  37.0 10.8 %collective-permute-done.33 = bf16[88,1024]{1,0:T(8,128)(2,1)S(1)} collective-permute-done((bf16[88,1024]{1,0:T(8,128)(2,1)S(1)}, bf16[88,1024]{1,0:T(8,128)(2,1)S(1)}, u32[]{:S(2)}, u32[]{:S(2)}) %collective-permute-start.33) | collective-permute-done | bytes 180256 | tf_op jit(solution)/shard_map/ppermute | solution.py:333
  47.8 9.2 %collective-permute-start.32 = (bf16[88,1024]{1,0:T(8,128)(2,1)S(1)}, bf16[88,1024]{1,0:T(8,128)(2,1)S(1)}, u32[]{:S(2)}, u32[]{:S(2)}) collective-permute-start(bf16[88,1024]{1,0:T(8,128)(2,1)S(1)} %copy-done.42), channel_id=1, source_target_pairs={{0,2},{1,3},{2,0},{3,1},{4,6},{5,7},{6,4},{7,5},{8,10},{9,11},{10,... | collective-permute-start | bytes 540680 | tf_op jit(solution)/shard_map/ppermute | solution.py:333
  57.0 5.7 collective-permute-done.32
  65.6 3.5 collective-permute-done.31
  81.6 9.6 %collective-permute-done.3 = bf16[4,32,1536]{2,1,0:T(8,128)(2,1)S(1)} collective-permute-done((bf16[4,32,1536]{2,1,0:T(8,128)(2,1)S(1)}, bf16[4,32,1536]{2,1,0:T(8,128)(2,1)S(1)}, u32[]{:S(2)}, u32[]{:S(2)}) %collective-permute-start.3) | collective-permute-done | bytes 393248 | tf_op jit(solution)/shard_map/ppermute | solution.py:333
  94.3 15.6 %collective-permute-done.4 = bf16[2,4,32,1536]{3,2,1,0:T(8,128)(2,1)S(1)} collective-permute-done((bf16[2,4,32,1536]{3,2,1,0:T(8,128)(2,1)S(1)}, bf16[2,4,32,1536]{3,2,1,0:T(8,128)(2,1)S(1)}, u32[]{:S(2)}, u32[]{:S(2)}) %collective-permute-start.4) | collective-permute-done | bytes 786464 | tf_op jit(solution)/shard_map/ppermute | solution.py:333
  122.0 10.2 %collective-permute-done.25 = bf16[4,32,2816]{2,1,0:T(8,128)(2,1)S(1)} collective-permute-done((bf16[4,32,2816]{2,1,0:T(8,128)(2,1)S(1)}, bf16[4,32,2816]{2,1,0:T(8,128)(2,1)S(1)}, u32[]{:S(2)}, u32[]{:S(2)}) %collective-permute-start.25) | collective-permute-done | bytes 720928 | tf_op jit(solution)/shard_map/ppermute | solution.py:333
  138.7 12.1 %place_rows.4 = (bf16[2,2,2,4,32,3072]{5,4,3,2,1,0:T(8,128)(2,1)}, bf16[2,2,2,4,32,128]{5,4,3,2,1,0:T(8,128)(2,1)}) custom-call(s32[4]{0:T(128)} %pad_add_fusion.spot, bf16[2,2,4,32,1536]{4,3,2,1,0:T(8,128)(2,1)} %copy-done.16, bf16[2,2,4,32,1664]{4,3,2,1,0:T(8,128)(2,1)} %copy-done.15, bf16[2,2,4,32,1536]{4,3,2,1,0:T(8,128)(2,1)} %copy-done.30, ...), custom_call_target="tpu_custom_call" | custom-call | tf_op jit(solution)/shard_map/place_rows/pallas_call | solution.py:379
  152.0 6.6 convolution_convert_fusion.q_ref.k_ref.v_ref
  170.2 36.9 %delta_forward.1 = (f32[2,8,256,256]{3,2,1,0:T(8,128)}, f32[2,8,256,128]{3,2,1,0:T(8,128)}, f32[2,8,256,128]{3,2,1,0:T(8,128)}, f32[2,8,256,128]{3,2,1,0:T(8,128...) custom-call(bf16[2,256,3072]{2,1,0:T(8,128)(2,1)} %copy-done, ...), custom_call_target="tpu_custom_call" | custom-call | tf_op jit(solution)/shard_map/delta_forward/pallas_call | solution.py:173
  220.7 4.6 collective-permute-start.11
  232.3 4.7 collective-permute-done.11
  239.0 5.2 collective-permute-start.12
  244.2 9.6 %place_rows.5 = bf16[2,2,2,4,32,1024]{5,4,3,2,1,0:T(8,128)(2,1)} custom-call(s32[4]{0:T(128)} %pad_add_fusion.spot, bf16[2,2,4,32,512]{4,3,2,1,0:T(8,128)(2,1)} %copy-done.25, bf16[2,2,4,32,512]{4,3,2,1,0:T(8,128)(2,1)} %copy-done.26, bf16[2,2,4,32,512]{4,3,2,1,0:T(8,128)(2,1)} %copy-done.38, bf16[2,2,4,32,512]{4,3,2,1,0:T(8,128)(2,1)} %copy-done.39), custom_call_target="tpu_custom_call" | custom-call | tf_op jit(solution)/shard_map/place_rows/pallas_call | solution.py:379
  253.9 11.9 %place_rows.7 = bf16[2,2,2,4,88,1024]{5,4,3,2,1,0:T(8,128)(2,1)} custom-call(s32[4]{0:T(128)} %pad_add_fusion.spot, bf16[2,2,4,88,512]{4,3,2,1,0:T(8,128)(2,1)} %pad_maximum_fusion.9.own_left, bf16[2,2,4,88,512]{4,3,2,1,0:T(8,128)(2,1)} %pad_maximum_fusion.10.own_right, bf16[2,2,4,88,512]{4,3,2,1,0:T(8,128)(2,1)} %collective-permute-done.38.other_left, ...), custom_call_target="tpu_custom_call" | custom-call | tf_op jit(solution)/shard_map/place_rows/pallas_call | solution.py:379
  274.4 5.4 multiply_reduce_fusion.6
  279.8 15.2 %place_rows.6 = bf16[2,2,2,4,32,5632]{5,4,3,2,1,0:T(8,128)(2,1)} custom-call(s32[4]{0:T(128)} %pad_add_fusion.spot, bf16[2,2,4,32,2816]{4,3,2,1,0:T(8,128)(2,1)} %pad_maximum_fusion.3.own_left, bf16[2,2,4,32,2816]{4,3,2,1,0:T(8,128)(2,1)} %pad_maximum_fusion.4.own_right, bf16[2,2,4,32,2816]{4,3,2,1,0:T(8,128)(2,1)} %collective-permute-done.29.other_left, ...), custom_call_target="tpu_custom_call" | custom-call | tf_op jit(solution)/shard_map/place_rows/pallas_call | solution.py:379
  295.0 12.4 %fusion.72 = f32[2,256,5632]{2,1,0:T(8,128)} fusion(bf16[1024,5632,1]{1,0,2:T(8,128)(2,1)} %bitcast.397, f32[2,256,1024]{2,1,0:T(8,128)} %get-tuple-element.85, f32[1024]{0:T(1024)S(1)} %reshape.239, f32[2,256]{1,0:T(2,128)S(1)} %get-tuple-element.178), kind=kOutput, calls=%fused_computation.204 | convolution fusion | flops 5907152896 | bytes 25171968 | tf_op jit(solution)/shard_map/sga,ab->sgb/dot_general | solution.py:432
  307.4 11.7 %fusion.4 = (bf16[2,256,2816]{2,1,0:T(8,128)(2,1)}, bf16[2,256,2816]{2,1,0:T(8,128)(2,1)}, bf16[2,256,2816]{2,1,0:T(8,128)(2,1)}) fusion(f32[2,256,5632]{2,1,0:T(8,128)} %fusion.72, bf16[2816,1024,1]{1,0,2:T(8,128)(2,1)} %bitcast.406, bf16[2,256,1024]{2,1,0:T(8,128)(2,1)S(1)} %copy-done.31), kind=kOutput, calls=%fused_computation.18 | convolution fusion | flops 2974416896 | bytes 27000832 | tf_op jit(solution)/shard_map/sgb,ab->sga/dot_general | solution.py:436
  319.2 9.5 %fusion.7 = f32[2,256,1024]{2,1,0:T(8,128)} fusion(bf16[1024,5632,1]{1,0,2:T(8,128)(2,1)S(1)} %bitcast.400, bf16[2,256,2816]{2,1,0:T(8,128)(2,1)} %get-tuple-element.89, bf16[2,256,2816]{2,1,0:T(8,128)(2,1)} %get-tuple-element.88), kind=kOutput, calls=%fused_computation.32 | convolution fusion | flops 5917114368 | bytes 19398656 | tf_op jit(solution)/shard_map/sgb,ab->sga/dot_general | solution.py:436
  328.7 9.5 %multiply_reduce_fusion.2 = (f32[]{:T(128)}, f32[]{:T(128)}, f32[2,256]{1,0:T(2,128)S(1)}, bf16[1024]{0:T(1024)(128)(2,1)S(1)}, bf16[2,256,1024]{2,1,0:T(8,128)(2,1)}) fusion(f32[2,256,1024]{2,1,0:T(8,128)S(1)} %copy-done.11, f32[2,256,1024]{2,1,0:T(8,128)} %fusion.7, f32[1024]{0:T(1024)S(1)} %reshape.239, f32[2,256]{1,0:T(2,128)S(1)} %get-tuple-element.178, ...), kind=kOutput, calls=%fused_computation.62 | convolution fusion | flops 2959079936 | bytes 13903880 | tf_op jit(solution)/shard_map/sga,ab->sgb/dot_general | solution.py:432
  345.9 9.3 %bitcast_convert_fusion = bf16[1024,5632]{1,0:T(8,128)(2,1)} fusion(bf16[2,256,2816]{2,1,0:T(8,128)(2,1)S(1)} %copy-done.57, bf16[2,256,2816]{2,1,0:T(8,128)(2,1)S(1)} %copy-done.56, f32[2,256,1024]{2,1,0:T(8,128)S(1)} %copy-done.11, f32[1024]{0:T(1024)S(1)} %reshape.239, f32[2,256]{1,0:T(2,128)S(1)} %get-tuple-element.178), kind=kOutput, calls=%fused_computation | convolution fusion | flops 5924454400 | bytes 19404800 | tf_op jit(solution)/shard_map/sga,sgb->ab/dot_general | solution.py:440
  374.6 5.0 bitcast_convert_fusion.2
  380.6 3.8 dynamic-slice_bitcast_fusion.1
  386.6 40.4 %psum.7 = f32[131]{0:T(256)} all-reduce(f32[131]{0:T(256)S(1)} %pad_maximum_fusion.28), channel_id=1, replica_groups=mesh['dp'=8,'cp'=4] {'dp','cp'}, use_global_device_ids=true, to_apply=%region_13.14 | all-reduce | flops 131 | bytes 1048 | tf_op jit(solution)/shard_map/psum | solution.py:560
  434.5 9.5 %collective-permute-done.41 = bf16[2,8,128,128]{3,2,1,0:T(8,128)(2,1)S(1)} collective-permute-done((bf16[2,8,128,128]{3,2,1,0:T(8,128)(2,1)S(1)}, bf16[2,8,128,128]{3,2,1,0:T(8,128)(2,1)S(1)}, u32[]{:S(2)}, u32[]{:S(2)}) %collective-permute-start.41) | collective-permute-done | bytes 524320 | tf_op jit(solution)/shard_map/ppermute | solution.py:424
  448.3 5.7 collective-permute-done.55
  459.8 35.8 %delta_backward.1 = (f32[3,2,256,1024]{3,2,1,0:T(8,128)}, f32[2,3,8,1024]{3,2,1,0:T(8,128)}, f32[2,3,4,1024]{3,2,1,0:T(4,128)}, f32[2,8,256,1]{3,2,1,0:T(8,128)}) custom-call(bf16[2,256,3072]{2,1,0:T(8,128)(2,1)} %copy-done, bf16[2,256,3072]{2,1,0:T(8,128)(2,1)} %copy-done, bf16[2,256,3072]{2,1,0:T(8,128)(2,1)} %copy-done, ...), custom_call_target="tpu_custom_call" | custom-call | tf_op jit(solution)/shard_map/delta_backward/pallas_call | solution.py:283
  495.6 4.6 copy.134
  500.2 5.0 slice.337
  518.9 9.2 %fusion.22 = (bf16[1024]{0:T(1024)(128)(2,1)}, f32[2,256]{1,0:T(2,128)}, f32[2,256,1024]{2,1,0:T(8,128)S(1)}) fusion(bf16[2,256,1024]{2,1,0:T(8,128)(2,1)} %param.11, f32[2,256]{1,0:T(2,128)} %copy-done.49, f32[1024]{0:T(1024)} %copy-done.45, f32[2,256,1024]{2,1,0:T(8,128)} %fusion.80, bf16[2,256,3072]{1,2,0:T(8,128)(2,1)} %bitcast.411, ...), kind=kOutput, calls=%fused_computation.53 | convolution fusion | flops 3225418240 | bytes 14690304 | tf_op jit(solution)/shard_map/sgb,ab->sga/dot_general | solution.py:436
  530.4 6.3 bitcast_convert_fusion.1
  537.0 4.1 fusion.2
  546.8 4.3 collective-permute-done.59
  556.1 4.0 collective-permute-done.69
  561.9 10.4 %collective-permute-done.71 = bf16[2,4,88,512]{3,2,1,0:T(8,128)(2,1)S(1)} collective-permute-done((bf16[2,4,88,512]{3,2,1,0:T(8,128)(2,1)S(1)}, bf16[2,4,88,512]{3,2,1,0:T(8,128)(2,1)S(1)}, u32[]{:S(2)}, u32[]{:S(2)}) %collective-permute-start.71) | collective-permute-done | bytes 720928 | tf_op jit(solution)/shard_map/ppermute | solution.py:333
  572.9 6.2 collective-permute-done.70
  590.7 5.9 collective-permute-done.74
  601.5 6.0 fusion
  610.9 10.0 %collective-permute-done.45 = bf16[2,4,32,1536]{3,2,1,0:T(8,128)(2,1)} collective-permute-done((bf16[2,4,32,1536]{3,2,1,0:T(8,128)(2,1)}, bf16[2,4,32,1536]{3,2,1,0:T(8,128)(2,1)}, u32[]{:S(2)}, u32[]{:S(2)}) %collective-permute-start.45) | collective-permute-done | bytes 786464 | tf_op jit(solution)/shard_map/ppermute | solution.py:333
  625.8 31.1 %collective-permute-done.46 = bf16[4,32,1536]{2,1,0:T(8,128)(2,1)S(1)} collective-permute-done((bf16[4,32,1536]{2,1,0:T(8,128)(2,1)S(1)}, bf16[4,32,1536]{2,1,0:T(8,128)(2,1)S(1)}, u32[]{:S(2)}, u32[]{:S(2)}) %collective-permute-start.46) | collective-permute-done | bytes 393248 | tf_op jit(solution)/shard_map/ppermute | solution.py:333
  667.7 6.9 collective-permute-done.50
  685.1 6.6 collective-permute-done.67
  691.7 15.0 %collective-permute-done.66 = bf16[32,5632]{1,0:T(8,128)(2,1)S(1)} collective-permute-done((bf16[32,5632]{1,0:T(8,128)(2,1)S(1)}, bf16[32,5632]{1,0:T(8,128)(2,1)S(1)}, u32[]{:S(2)}, u32[]{:S(2)}) %collective-permute-start.66) | collective-permute-done | bytes 360480 | tf_op jit(solution)/shard_map/ppermute | solution.py:333
  (420 shorter events, 219.8 us)
Async XLA Ops:
  4.1 71.5 %collective-permute-start.2 = (bf16[32,3200]{1,0:T(8,128)(2,1)S(1)}, bf16[32,3200]{1,0:T(8,128)(2,1)S(1)}, u32[]{:S(2)}, u32[]{:S(2)}) collective-permute-start(bf16[32,3200]{1,0:T(8,128)(2,1)S(1)} %pad_maximum_fusion.23), channel_id=1, source_target_pairs={{0,3},{1,2},{2,1},{3,0},{4,7},{5,6},{6,5},{7,4},{8,11},{9,10},{10,... | collective-permute-start | bytes 614408 | tf_op jit(solution)/shard_map/ppermute | solution.py:333
  9.2 68.4 %collective-permute-start.1 = (bf16[32,3200]{1,0:T(8,128)(2,1)S(1)}, bf16[32,3200]{1,0:T(8,128)(2,1)S(1)}, u32[]{:S(2)}, u32[]{:S(2)}) collective-permute-start(bf16[32,3200]{1,0:T(8,128)(2,1)S(1)} %pad_maximum_fusion.23), channel_id=1, source_target_pairs={{0,2},{1,3},{2,0},{3,1},{4,6},{5,7},{6,4},{7,5},{8,10},{9,11},{10,... | collective-permute-start | bytes 614408 | tf_op jit(solution)/shard_map/ppermute | solution.py:333
  9.2 70.0 %collective-permute-start = (bf16[32,3200]{1,0:T(8,128)(2,1)S(1)}, bf16[32,3200]{1,0:T(8,128)(2,1)S(1)}, u32[]{:S(2)}, u32[]{:S(2)}) collective-permute-start(bf16[32,3200]{1,0:T(8,128)(2,1)S(1)} %pad_maximum_fusion.23), channel_id=1, source_target_pairs={{0,1},{1,0},{2,3},{3,2},{4,5},{5,4},{6,7},{7,6},{8,9},{9,8},{10,11... | collective-permute-start | bytes 614408 | tf_op jit(solution)/shard_map/ppermute | solution.py:333
  9.8 15.5 %collective-permute-start.15 = (bf16[32,1024]{1,0:T(8,128)(2,1)}, bf16[32,1024]{1,0:T(8,128)(2,1)S(1)}, u32[]{:S(2)}, u32[]{:S(2)}) collective-permute-start(bf16[32,1024]{1,0:T(8,128)(2,1)} %param.17), channel_id=1, source_target_pairs={{0,3},{1,2},{2,1},{3,0},{4,7},{5,6},{6,5},{7,4},{8,11},{9,10},{10,... | collective-permute-start | bytes 196616 | tf_op jit(solution)/shard_map/ppermute | solution.py:333
  13.6 18.7 %collective-permute-start.14 = (bf16[32,1024]{1,0:T(8,128)(2,1)}, bf16[32,1024]{1,0:T(8,128)(2,1)S(1)}, u32[]{:S(2)}, u32[]{:S(2)}) collective-permute-start(bf16[32,1024]{1,0:T(8,128)(2,1)} %param.17), channel_id=1, source_target_pairs={{0,2},{1,3},{2,0},{3,1},{4,6},{5,7},{6,4},{7,5},{8,10},{9,11},{10,... | collective-permute-start | bytes 196616 | tf_op jit(solution)/shard_map/ppermute | solution.py:333
  32.3 48.7 %collective-permute-start.24 = (bf16[32,5632]{1,0:T(8,128)(2,1)S(1)}, bf16[32,5632]{1,0:T(8,128)(2,1)S(1)}, u32[]{:S(2)}, u32[]{:S(2)}) collective-permute-start(bf16[32,5632]{1,0:T(8,128)(2,1)S(1)} %copy-done.40), channel_id=1, source_target_pairs={{0,3},{1,2},{2,1},{3,0},{4,7},{5,6},{6,5},{7,4},{8,11},{9,10},{10,... | collective-permute-start | bytes 1081352 | tf_op jit(solution)/shard_map/ppermute | solution.py:333
  74.1 19.5 %collective-permute-start.23 = (bf16[32,5632]{1,0:T(8,128)(2,1)S(1)}, bf16[32,5632]{1,0:T(8,128)(2,1)S(1)}, u32[]{:S(2)}, u32[]{:S(2)}) collective-permute-start(bf16[32,5632]{1,0:T(8,128)(2,1)S(1)} %copy-done.40), channel_id=1, source_target_pairs={{0,2},{1,3},{2,0},{3,1},{4,6},{5,7},{6,4},{7,5},{8,10},{9,11},{10,... | collective-permute-start | bytes 1081352 | tf_op jit(solution)/shard_map/ppermute | solution.py:333
  75.6 37.7 %collective-permute-start.22 = (bf16[32,5632]{1,0:T(8,128)(2,1)S(1)}, bf16[32,5632]{1,0:T(8,128)(2,1)S(1)}, u32[]{:S(2)}, u32[]{:S(2)}) collective-permute-start(bf16[32,5632]{1,0:T(8,128)(2,1)S(1)} %copy-done.40), channel_id=1, source_target_pairs={{0,1},{1,0},{2,3},{3,2},{4,5},{5,4},{6,7},{7,6},{8,9},{9,8},{10,11... | collective-permute-start | bytes 1081352 | tf_op jit(solution)/shard_map/ppermute | solution.py:333
  77.6 36.5 %collective-permute-start.18 = (bf16[4,32,512]{2,1,0:T(8,128)(2,1)S(1)}, bf16[4,32,512]{2,1,0:T(8,128)(2,1)S(1)}, u32[]{:S(2)}, u32[]{:S(2)}) collective-permute-start(bf16[4,32,512]{2,1,0:T(8,128)(2,1)S(1)} %get-tuple-element.160), channel_id=1, source_target_pairs={{0,16},{1,17},{2,18},{3,19},{4,20},{5,21},{6,22},{7,23},{8,24},{9,... | collective-permute-start | bytes 393224 | tf_op jit(solution)/shard_map/ppermute | solution.py:333
  91.2 26.3 %collective-permute-start.34 = (bf16[4,88,512]{2,1,0:T(8,128)(2,1)S(1)}, bf16[4,88,512]{2,1,0:T(8,128)(2,1)S(1)}, u32[]{:S(2)}, u32[]{:S(2)}) collective-permute-start(bf16[4,88,512]{2,1,0:T(8,128)(2,1)S(1)} %get-tuple-element.133), channel_id=1, source_target_pairs={{0,8},{1,9},{2,10},{3,11},{4,12},{5,13},{6,14},{7,15},{8,0},{9,1},... | collective-permute-start | bytes 1081352 | tf_op jit(solution)/shard_map/ppermute | solution.py:333
  92.8 17.1 %collective-permute-start.4 = (bf16[2,4,32,1536]{3,2,1,0:T(8,128)(2,1)S(1)}, bf16[2,4,32,1536]{3,2,1,0:T(8,128)(2,1)S(1)}, u32[]{:S(2)}, u32[]{:S(2)}) collective-permute-start(bf16[2,4,32,1536]{3,2,1,0:T(8,128)(2,1)S(1)} %get-tuple-element.112), channel_id=1, source_target_pairs={{0,16},{1,17},{2,18},{3,19},{4,20},{5,21},{6,22},{7,23},{8,24},{9,... | collective-permute-start | bytes 2359304 | tf_op jit(solution)/shard_map/ppermute | solution.py:333
  93.5 19.6 %collective-permute-start.6 = (bf16[2,4,32,1664]{3,2,1,0:T(8,128)(2,1)S(1)}, bf16[2,4,32,1664]{3,2,1,0:T(8,128)(2,1)S(1)}, u32[]{:S(2)}, u32[]{:S(2)}) collective-permute-start(bf16[2,4,32,1664]{3,2,1,0:T(8,128)(2,1)S(1)} %get-tuple-element.107), channel_id=1, source_target_pairs={{0,8},{1,9},{2,10},{3,11},{4,12},{5,13},{6,14},{7,15},{8,0},{9,1},... | collective-permute-start | bytes 2555912 | tf_op jit(solution)/shard_map/ppermute | solution.py:333
  113.1 21.4 %collective-permute-start.7 = (bf16[2,2,4,32,1536]{4,3,2,1,0:T(8,128)(2,1)S(1)}, bf16[2,2,4,32,1536]{4,3,2,1,0:T(8,128)(2,1)S(1)}, u32[]{:S(2)}, u32[]{:S(2)}) collective-permute-start(bf16[2,2,4,32,1536]{4,3,2,1,0:T(8,128)(2,1)S(1)} %pad_maximum_fusion.6.own_left), channel_id=1, source_target_pairs={{0,4},{1,5},{2,6},{3,7},{4,0},{5,1},{6,2},{7,3},{8,12},{9,13},{10,... | collective-permute-start | bytes 4718600 | tf_op jit(solution)/shard_map/ppermute | solution.py:333
  113.3 22.7 %collective-permute-start.8 = (bf16[2,2,4,32,1664]{4,3,2,1,0:T(8,128)(2,1)S(1)}, bf16[2,2,4,32,1664]{4,3,2,1,0:T(8,128)(2,1)S(1)}, u32[]{:S(2)}, u32[]{:S(2)}) collective-permute-start(bf16[2,2,4,32,1664]{4,3,2,1,0:T(8,128)(2,1)S(1)} %pad_maximum_fusion.5.own_right), channel_id=1, source_target_pairs={{0,4},{1,5},{2,6},{3,7},{4,0},{5,1},{6,2},{7,3},{8,12},{9,13},{10,... | collective-permute-start | bytes 5111816 | tf_op jit(solution)/shard_map/ppermute | solution.py:333
  114.1 18.1 %collective-permute-start.25 = (bf16[4,32,2816]{2,1,0:T(8,128)(2,1)S(1)}, bf16[4,32,2816]{2,1,0:T(8,128)(2,1)S(1)}, u32[]{:S(2)}, u32[]{:S(2)}) collective-permute-start(bf16[4,32,2816]{2,1,0:T(8,128)(2,1)S(1)} %get-tuple-element.123), channel_id=1, source_target_pairs={{0,8},{1,9},{2,10},{3,11},{4,12},{5,13},{6,14},{7,15},{8,0},{9,1},... | collective-permute-start | bytes 2162696 | tf_op jit(solution)/shard_map/ppermute | solution.py:333
  117.5 47.9 %collective-permute-start.17 = (bf16[2,4,32,512]{3,2,1,0:T(8,128)(2,1)}, bf16[2,4,32,512]{3,2,1,0:T(8,128)(2,1)}, u32[]{:S(2)}, u32[]{:S(2)}) collective-permute-start(bf16[2,4,32,512]{3,2,1,0:T(8,128)(2,1)} %get-tuple-element.150), channel_id=1, source_target_pairs={{0,16},{1,17},{2,18},{3,19},{4,20},{5,21},{6,22},{7,23},{8,24},{9,... | collective-permute-start | bytes 786440 | tf_op jit(solution)/shard_map/ppermute | solution.py:333
  119.2 39.4 %collective-permute-start.27 = (bf16[4,32,2816]{2,1,0:T(8,128)(2,1)}, bf16[4,32,2816]{2,1,0:T(8,128)(2,1)}, u32[]{:S(2)}, u32[]{:S(2)}) collective-permute-start(bf16[4,32,2816]{2,1,0:T(8,128)(2,1)} %get-tuple-element.121), channel_id=1, source_target_pairs={{0,16},{1,17},{2,18},{3,19},{4,20},{5,21},{6,22},{7,23},{8,24},{9,... | collective-permute-start | bytes 2162696 | tf_op jit(solution)/shard_map/ppermute | solution.py:333
  132.2 81.4 %collective-permute-start.35 = (bf16[2,4,88,512]{3,2,1,0:T(8,128)(2,1)}, bf16[2,4,88,512]{3,2,1,0:T(8,128)(2,1)}, u32[]{:S(2)}, u32[]{:S(2)}) collective-permute-start(bf16[2,4,88,512]{3,2,1,0:T(8,128)(2,1)} %get-tuple-element.119), channel_id=1, source_target_pairs={{0,16},{1,17},{2,18},{3,19},{4,20},{5,21},{6,22},{7,23},{8,24},{9,... | collective-permute-start | bytes 2162696 | tf_op jit(solution)/shard_map/ppermute | solution.py:333
  134.5 81.7 %collective-permute-start.37 = (bf16[2,4,88,512]{3,2,1,0:T(8,128)(2,1)}, bf16[2,4,88,512]{3,2,1,0:T(8,128)(2,1)}, u32[]{:S(2)}, u32[]{:S(2)}) collective-permute-start(bf16[2,4,88,512]{3,2,1,0:T(8,128)(2,1)} %get-tuple-element.117), channel_id=1, source_target_pairs={{0,8},{1,9},{2,10},{3,11},{4,12},{5,13},{6,14},{7,15},{8,0},{9,1},... | collective-permute-start | bytes 2162696 | tf_op jit(solution)/shard_map/ppermute | solution.py:333
  137.2 83.5 %collective-permute-start.26 = (bf16[2,4,32,2816]{3,2,1,0:T(8,128)(2,1)}, bf16[2,4,32,2816]{3,2,1,0:T(8,128)(2,1)}, u32[]{:S(2)}, u32[]{:S(2)}) collective-permute-start(bf16[2,4,32,2816]{3,2,1,0:T(8,128)(2,1)} %get-tuple-element.103), channel_id=1, source_target_pairs={{0,16},{1,17},{2,18},{3,19},{4,20},{5,21},{6,22},{7,23},{8,24},{9,... | collective-permute-start | bytes 4325384 | tf_op jit(solution)/shard_map/ppermute | solution.py:333
  165.4 43.2 %collective-permute-start.19 = (bf16[2,4,32,512]{3,2,1,0:T(8,128)(2,1)}, bf16[2,4,32,512]{3,2,1,0:T(8,128)(2,1)S(1)}, u32[]{:S(2)}, u32[]{:S(2)}) collective-permute-start(bf16[2,4,32,512]{3,2,1,0:T(8,128)(2,1)} %get-tuple-element.148), channel_id=1, source_target_pairs={{0,8},{1,9},{2,10},{3,11},{4,12},{5,13},{6,14},{7,15},{8,0},{9,1},... | collective-permute-start | bytes 786440 | tf_op jit(solution)/shard_map/ppermute | solution.py:333
  166.0 62.5 %collective-permute-start.28 = (bf16[2,4,32,2816]{3,2,1,0:T(8,128)(2,1)}, bf16[2,4,32,2816]{3,2,1,0:T(8,128)(2,1)}, u32[]{:S(2)}, u32[]{:S(2)}) collective-permute-start(bf16[2,4,32,2816]{3,2,1,0:T(8,128)(2,1)} %get-tuple-element.101), channel_id=1, source_target_pairs={{0,8},{1,9},{2,10},{3,11},{4,12},{5,13},{6,14},{7,15},{8,0},{9,1},... | collective-permute-start | bytes 4325384 | tf_op jit(solution)/shard_map/ppermute | solution.py:333
  213.6 18.3 %collective-permute-start.20 = (bf16[2,2,4,32,512]{4,3,2,1,0:T(8,128)(2,1)S(1)}, bf16[2,2,4,32,512]{4,3,2,1,0:T(8,128)(2,1)S(1)}, u32[]{:S(2)}, u32[]{:S(2)}) collective-permute-start(bf16[2,2,4,32,512]{4,3,2,1,0:T(8,128)(2,1)S(1)} %pad_maximum_fusion.17.own_left), channel_id=1, source_target_pairs={{0,4},{1,5},{2,6},{3,7},{4,0},{5,1},{6,2},{7,3},{8,12},{9,13},{10,... | collective-permute-start | bytes 1572872 | tf_op jit(solution)/shard_map/ppermute | solution.py:333
  216.2 37.7 %collective-permute-start.38 = (bf16[2,2,4,88,512]{4,3,2,1,0:T(8,128)(2,1)}, bf16[2,2,4,88,512]{4,3,2,1,0:T(8,128)(2,1)}, u32[]{:S(2)}, u32[]{:S(2)}) collective-permute-start(bf16[2,2,4,88,512]{4,3,2,1,0:T(8,128)(2,1)} %pad_maximum_fusion.9.own_left), channel_id=1, source_target_pairs={{0,4},{1,5},{2,6},{3,7},{4,0},{5,1},{6,2},{7,3},{8,12},{9,13},{10,... | collective-permute-start | bytes 4325384 | tf_op jit(solution)/shard_map/ppermute | solution.py:333
  220.2 33.6 %collective-permute-start.39 = (bf16[2,2,4,88,512]{4,3,2,1,0:T(8,128)(2,1)}, bf16[2,2,4,88,512]{4,3,2,1,0:T(8,128)(2,1)}, u32[]{:S(2)}, u32[]{:S(2)}) collective-permute-start(bf16[2,2,4,88,512]{4,3,2,1,0:T(8,128)(2,1)} %pad_maximum_fusion.10.own_right), channel_id=1, source_target_pairs={{0,4},{1,5},{2,6},{3,7},{4,0},{5,1},{6,2},{7,3},{8,12},{9,13},{10,... | collective-permute-start | bytes 4325384 | tf_op jit(solution)/shard_map/ppermute | solution.py:333
  220.7 16.2 %collective-permute-start.11 = (bf16[2,8,128,128]{3,2,1,0:T(8,128)(2,1)S(1)}, bf16[2,8,128,128]{3,2,1,0:T(8,128)(2,1)S(1)}, u32[]{:S(2)}, u32[]{:S(2)}) collective-permute-start(bf16[2,8,128,128]{3,2,1,0:T(8,128)(2,1)S(1)} %fusion.33), channel_id=1, source_target_pairs={{0,1},{1,2},{2,3},{4,5},{5,6},{6,7},{8,9},{9,10},{10,11},{12,13},{... | collective-permute-start | bytes 1572872 | tf_op jit(solution)/shard_map/ppermute | solution.py:424
  231.9 47.9 %collective-permute-start.29 = (bf16[2,2,4,32,2816]{4,3,2,1,0:T(8,128)(2,1)}, bf16[2,2,4,32,2816]{4,3,2,1,0:T(8,128)(2,1)}, u32[]{:S(2)}, u32[]{:S(2)}) collective-permute-start(bf16[2,2,4,32,2816]{4,3,2,1,0:T(8,128)(2,1)} %pad_maximum_fusion.3.own_left), channel_id=1, source_target_pairs={{0,4},{1,5},{2,6},{3,7},{4,0},{5,1},{6,2},{7,3},{8,12},{9,13},{10,... | collective-permute-start | bytes 8650760 | tf_op jit(solution)/shard_map/ppermute | solution.py:333
  236.9 42.9 %collective-permute-start.30 = (bf16[2,2,4,32,2816]{4,3,2,1,0:T(8,128)(2,1)}, bf16[2,2,4,32,2816]{4,3,2,1,0:T(8,128)(2,1)}, u32[]{:S(2)}, u32[]{:S(2)}) collective-permute-start(bf16[2,2,4,32,2816]{4,3,2,1,0:T(8,128)(2,1)} %pad_maximum_fusion.4.own_right), channel_id=1, source_target_pairs={{0,4},{1,5},{2,6},{3,7},{4,0},{5,1},{6,2},{7,3},{8,12},{9,13},{10,... | collective-permute-start | bytes 8650760 | tf_op jit(solution)/shard_map/ppermute | solution.py:333
  239.0 26.8 %collective-permute-start.12 = (bf16[2,8,128,128]{3,2,1,0:T(8,128)(2,1)}, bf16[2,8,128,128]{3,2,1,0:T(8,128)(2,1)}, u32[]{:S(2)}, u32[]{:S(2)}) collective-permute-start(bf16[2,8,128,128]{3,2,1,0:T(8,128)(2,1)} %fusion.34), channel_id=1, source_target_pairs={{0,1},{1,2},{2,3},{4,5},{5,6},{6,7},{8,9},{9,10},{10,11},{12,13},{... | collective-permute-start | bytes 1572872 | tf_op jit(solution)/shard_map/ppermute | solution.py:424
  368.8 58.2 %collective-permute-start.40 = (bf16[2,8,128,128]{3,2,1,0:T(8,128)(2,1)}, bf16[2,8,128,128]{3,2,1,0:T(8,128)(2,1)}, u32[]{:S(2)}, u32[]{:S(2)}) collective-permute-start(bf16[2,8,128,128]{3,2,1,0:T(8,128)(2,1)} %get-tuple-element.179), channel_id=1, source_target_pairs={{1,0},{2,1},{3,2},{5,4},{6,5},{7,6},{9,8},{10,9},{11,10},{13,12},{... | collective-permute-start | bytes 1572872 | tf_op jit(solution)/shard_map/ppermute | solution.py:424
  370.2 60.1 %collective-permute-start.52 = (bf16[2,2,4,32,1024]{4,3,2,1,0:T(8,128)(2,1)S(1)}, bf16[2,2,4,32,1024]{4,3,2,1,0:T(8,128)(2,1)}, u32[]{:S(2)}, u32[]{:S(2)}) collective-permute-start(bf16[2,2,4,32,1024]{4,3,2,1,0:T(8,128)(2,1)S(1)} %dynamic-slice_bitcast_fusion.4), channel_id=1, source_target_pairs={{0,4},{1,5},{2,6},{3,7},{4,0},{5,1},{6,2},{7,3},{8,12},{9,13},{10,... | collective-permute-start | bytes 3145736 | tf_op jit(solution)/shard_map/ppermute | solution.py:333
  380.3 221.2 %collective-permute-start.60 = (bf16[2,2,4,32,5632]{4,3,2,1,0:T(8,128)(2,1)}, bf16[2,2,4,32,5632]{4,3,2,1,0:T(8,128)(2,1)}, u32[]{:S(2)}, u32[]{:S(2)}) collective-permute-start(bf16[2,2,4,32,5632]{4,3,2,1,0:T(8,128)(2,1)} %dynamic-slice_bitcast_fusion), channel_id=1, source_target_pairs={{0,4},{1,5},{2,6},{3,7},{4,0},{5,1},{6,2},{7,3},{8,12},{9,13},{10,... | collective-permute-start | bytes 17301512 | tf_op jit(solution)/shard_map/ppermute | solution.py:333
  384.4 152.6 %collective-permute-start.68 = (bf16[2,2,4,88,1024]{4,3,2,1,0:T(8,128)(2,1)}, bf16[2,2,4,88,1024]{4,3,2,1,0:T(8,128)(2,1)}, u32[]{:S(2)}, u32[]{:S(2)}) collective-permute-start(bf16[2,2,4,88,1024]{4,3,2,1,0:T(8,128)(2,1)} %dynamic-slice_bitcast_fusion.1), channel_id=1, source_target_pairs={{0,4},{1,5},{2,6},{3,7},{4,0},{5,1},{6,2},{7,3},{8,12},{9,13},{10,... | collective-permute-start | bytes 8650760 | tf_op jit(solution)/shard_map/ppermute | solution.py:333
  432.2 15.9 %collective-permute-start.53 = (bf16[2,4,32,512]{3,2,1,0:T(8,128)(2,1)S(1)}, bf16[2,4,32,512]{3,2,1,0:T(8,128)(2,1)S(1)}, u32[]{:S(2)}, u32[]{:S(2)}) collective-permute-start(bf16[2,4,32,512]{3,2,1,0:T(8,128)(2,1)S(1)} %dynamic-slice_bitcast_fusion.16), channel_id=1, source_target_pairs={{0,8},{1,9},{2,10},{3,11},{4,12},{5,13},{6,14},{7,15},{8,0},{9,1},... | collective-permute-start | bytes 786440 | tf_op jit(solution)/shard_map/ppermute | solution.py:333
  454.8 88.5 %collective-permute-start.56 = (bf16[4,32,512]{2,1,0:T(8,128)(2,1)}, bf16[4,32,512]{2,1,0:T(8,128)(2,1)}, u32[]{:S(2)}, u32[]{:S(2)}) collective-permute-start(bf16[4,32,512]{2,1,0:T(8,128)(2,1)} %dynamic-slice_bitcast_fusion.17), channel_id=1, source_target_pairs={{0,8},{1,9},{2,10},{3,11},{4,12},{5,13},{6,14},{7,15},{8,0},{9,1},... | collective-permute-start | bytes 393224 | tf_op jit(solution)/shard_map/ppermute | solution.py:333
  536.9 60.5 %collective-permute-start.44 = (bf16[2,2,4,32,3200]{4,3,2,1,0:T(8,128)(2,1)S(1)}, bf16[2,2,4,32,3200]{4,3,2,1,0:T(8,128)(2,1)S(1)}, u32[]{:S(2)}, u32[]{:S(2)}) collective-permute-start(bf16[2,2,4,32,3200]{4,3,2,1,0:T(8,128)(2,1)S(1)} %fusion.9), channel_id=1, source_target_pairs={{0,4},{1,5},{2,6},{3,7},{4,0},{5,1},{6,2},{7,3},{8,12},{9,13},{10,... | collective-permute-start | bytes 9830408 | tf_op jit(solution)/shard_map/ppermute | solution.py:333
  541.5 18.6 %collective-permute-start.69 = (bf16[2,4,88,512]{3,2,1,0:T(8,128)(2,1)S(1)}, bf16[2,4,88,512]{3,2,1,0:T(8,128)(2,1)S(1)}, u32[]{:S(2)}, u32[]{:S(2)}) collective-permute-start(bf16[2,4,88,512]{3,2,1,0:T(8,128)(2,1)S(1)} %dynamic-slice_bitcast_fusion.8), channel_id=1, source_target_pairs={{0,8},{1,9},{2,10},{3,11},{4,12},{5,13},{6,14},{7,15},{8,0},{9,1},... | collective-permute-start | bytes 2162696 | tf_op jit(solution)/shard_map/ppermute | solution.py:333
  553.3 19.0 %collective-permute-start.71 = (bf16[2,4,88,512]{3,2,1,0:T(8,128)(2,1)S(1)}, bf16[2,4,88,512]{3,2,1,0:T(8,128)(2,1)S(1)}, u32[]{:S(2)}, u32[]{:S(2)}) collective-permute-start(bf16[2,4,88,512]{3,2,1,0:T(8,128)(2,1)S(1)} %dynamic-slice_bitcast_fusion.7), channel_id=1, source_target_pairs={{0,16},{1,17},{2,18},{3,19},{4,20},{5,21},{6,22},{7,23},{8,24},{9,... | collective-permute-start | bytes 2162696 | tf_op jit(solution)/shard_map/ppermute | solution.py:333
  560.4 18.7 %collective-permute-start.70 = (bf16[4,88,512]{2,1,0:T(8,128)(2,1)S(1)}, bf16[4,88,512]{2,1,0:T(8,128)(2,1)S(1)}, u32[]{:S(2)}, u32[]{:S(2)}) collective-permute-start(bf16[4,88,512]{2,1,0:T(8,128)(2,1)S(1)} %dynamic-slice_bitcast_fusion.14), channel_id=1, source_target_pairs={{0,16},{1,17},{2,18},{3,19},{4,20},{5,21},{6,22},{7,23},{8,24},{9,... | collective-permute-start | bytes 1081352 | tf_op jit(solution)/shard_map/ppermute | solution.py:333
  598.7 25.3 %collective-permute-start.47 = (bf16[2,4,32,1664]{3,2,1,0:T(8,128)(2,1)S(1)}, bf16[2,4,32,1664]{3,2,1,0:T(8,128)(2,1)}, u32[]{:S(2)}, u32[]{:S(2)}) collective-permute-start(bf16[2,4,32,1664]{3,2,1,0:T(8,128)(2,1)S(1)} %dynamic-slice_bitcast_fusion.5), channel_id=1, source_target_pairs={{0,16},{1,17},{2,18},{3,19},{4,20},{5,21},{6,22},{7,23},{8,24},{9,... | collective-permute-start | bytes 2555912 | tf_op jit(solution)/shard_map/ppermute | solution.py:333
  600.1 20.8 %collective-permute-start.45 = (bf16[2,4,32,1536]{3,2,1,0:T(8,128)(2,1)}, bf16[2,4,32,1536]{3,2,1,0:T(8,128)(2,1)}, u32[]{:S(2)}, u32[]{:S(2)}) collective-permute-start(bf16[2,4,32,1536]{3,2,1,0:T(8,128)(2,1)} %dynamic-slice_bitcast_fusion.6), channel_id=1, source_target_pairs={{0,8},{1,9},{2,10},{3,11},{4,12},{5,13},{6,14},{7,15},{8,0},{9,1},... | collective-permute-start | bytes 2359304 | tf_op jit(solution)/shard_map/ppermute | solution.py:333
  608.4 53.9 %collective-permute-start.61 = (bf16[2,4,32,2816]{3,2,1,0:T(8,128)(2,1)S(1)}, bf16[2,4,32,2816]{3,2,1,0:T(8,128)(2,1)S(1)}, u32[]{:S(2)}, u32[]{:S(2)}) collective-permute-start(bf16[2,4,32,2816]{3,2,1,0:T(8,128)(2,1)S(1)} %dynamic-slice_bitcast_fusion.3), channel_id=1, source_target_pairs={{0,8},{1,9},{2,10},{3,11},{4,12},{5,13},{6,14},{7,15},{8,0},{9,1},... | collective-permute-start | bytes 4325384 | tf_op jit(solution)/shard_map/ppermute | solution.py:333
  609.2 55.0 %collective-permute-start.63 = (bf16[2,4,32,2816]{3,2,1,0:T(8,128)(2,1)S(1)}, bf16[2,4,32,2816]{3,2,1,0:T(8,128)(2,1)S(1)}, u32[]{:S(2)}, u32[]{:S(2)}) collective-permute-start(bf16[2,4,32,2816]{3,2,1,0:T(8,128)(2,1)S(1)} %dynamic-slice_bitcast_fusion.2), channel_id=1, source_target_pairs={{0,16},{1,17},{2,18},{3,19},{4,20},{5,21},{6,22},{7,23},{8,24},{9,... | collective-permute-start | bytes 4325384 | tf_op jit(solution)/shard_map/ppermute | solution.py:333
  622.2 34.6 %collective-permute-start.46 = (bf16[4,32,1536]{2,1,0:T(8,128)(2,1)S(1)}, bf16[4,32,1536]{2,1,0:T(8,128)(2,1)S(1)}, u32[]{:S(2)}, u32[]{:S(2)}) collective-permute-start(bf16[4,32,1536]{2,1,0:T(8,128)(2,1)S(1)} %dynamic-slice_bitcast_fusion.12), channel_id=1, source_target_pairs={{0,16},{1,17},{2,18},{3,19},{4,20},{5,21},{6,22},{7,23},{8,24},{9,... | collective-permute-start | bytes 1179656 | tf_op jit(solution)/shard_map/ppermute | solution.py:333
  625.4 32.3 %collective-permute-start.48 = (bf16[4,32,1664]{2,1,0:T(8,128)(2,1)S(1)}, bf16[4,32,1664]{2,1,0:T(8,128)(2,1)S(1)}, u32[]{:S(2)}, u32[]{:S(2)}) collective-permute-start(bf16[4,32,1664]{2,1,0:T(8,128)(2,1)S(1)} %dynamic-slice_bitcast_fusion.11), channel_id=1, source_target_pairs={{0,8},{1,9},{2,10},{3,11},{4,12},{5,13},{6,14},{7,15},{8,0},{9,1},... | collective-permute-start | bytes 1277960 | tf_op jit(solution)/shard_map/ppermute | solution.py:333
  659.5 15.2 %collective-permute-start.49 = (bf16[32,3200]{1,0:T(8,128)(2,1)S(1)}, bf16[32,3200]{1,0:T(8,128)(2,1)S(1)}, u32[]{:S(2)}, u32[]{:S(2)}) collective-permute-start(bf16[32,3200]{1,0:T(8,128)(2,1)S(1)} %get-tuple-element.108), channel_id=1, source_target_pairs={{0,1},{1,0},{2,3},{3,2},{4,5},{5,4},{6,7},{7,6},{8,9},{9,8},{10,11... | collective-permute-start | bytes 614408 | tf_op jit(solution)/shard_map/ppermute | solution.py:333
  680.6 26.1 %collective-permute-start.66 = (bf16[32,5632]{1,0:T(8,128)(2,1)S(1)}, bf16[32,5632]{1,0:T(8,128)(2,1)S(1)}, u32[]{:S(2)}, u32[]{:S(2)}) collective-permute-start(bf16[32,5632]{1,0:T(8,128)(2,1)S(1)} %get-tuple-element.98), channel_id=1, source_target_pairs={{0,2},{1,3},{2,0},{3,1},{4,6},{5,7},{6,4},{7,5},{8,10},{9,11},{10,... | collective-permute-start | bytes 1081352 | tf_op jit(solution)/shard_map/ppermute | solution.py:333
  680.6 26.1 %collective-permute-start.65 = (bf16[32,5632]{1,0:T(8,128)(2,1)S(1)}, bf16[32,5632]{1,0:T(8,128)(2,1)}, u32[]{:S(2)}, u32[]{:S(2)}) collective-permute-start(bf16[32,5632]{1,0:T(8,128)(2,1)S(1)} %get-tuple-element.97), channel_id=1, source_target_pairs={{0,1},{1,0},{2,3},{3,2},{4,5},{5,4},{6,7},{7,6},{8,9},{9,8},{10,11... | collective-permute-start | bytes 1081352 | tf_op jit(solution)/shard_map/ppermute | solution.py:333
  (90 other events, 1009.0 us)

commit v3 on v1

--- a/solution.py
+++ b/solution.py
@@ -143,52 +143,67 @@
         weights_ref[0, h] = solved[:, depth:]
         scores = jnp.where(lower, mul(queries[h], keys[h], NT), 0.0)
         seen = mul_high(scores, solved, NN)
-        mixed_ref[0, h] = seen[:, :depth]
-        reach_ref[0, h] = queries[h].astype(F32) - seen[:, depth:]
+        lanes = slice(h * depth, (h + 1) * depth)
+        mixed_ref[0, :, lanes] = seen[:, :depth]
+        reach_ref[0, :, lanes] = queries[h].astype(F32) - seen[:, depth:]
         moved = mul_high(keys[h], solved, TN)
         offset_ref[0, h] = moved[:, :depth]
         transfer_ref[0, h] = small_eye - moved[:, depth:]
 
 
-def specs_of(model, depth, size, reverse=False):
+def cost(microseconds):
+    return pl.CostEstimate(flops=int(microseconds * 1.15e9), bytes_accessed=2**20, transcendentals=0)
+
+
+def specs_of(model, depth, size, width, base=0, seq=None):
     wide = PAIR * depth
     blocks = model // wide
-    rows = [pl.BlockSpec((1, size, wide), functools.partial(lambda part, s, g: (s, 0, part * blocks + g), part)) for part in range(3)]
-    before = [pl.BlockSpec((1, 8, wide), functools.partial(lambda part, s, g: (s, 0, part * blocks + g), part)) for part in range(3)]
-    return rows, before, wide, blocks
+
+    def three(rows, batched):
+        def index(part, s, g):
+            column = part * blocks + base + g
+            if not batched:
+                return (0, column)
+            return (s if seq is None else seq, 0, column)
+
+        block = (1, rows, wide) if batched else (rows, wide)
+        return [pl.BlockSpec(block, functools.partial(index, part)) for part in range(3)]
+
+    return three(size, True) + three(8, True) + three(width, False), wide
 
 
 def forward_parts(projected, before, taps, rates, depth):
     seqs, size, model3 = projected.shape
     model = model3 // 3
-    rows, prior, wide, blocks = specs_of(model, depth, size)
-    tap_specs = [pl.BlockSpec((taps.shape[0], wide), functools.partial(lambda part, s, g: (0, part * blocks + g), part)) for part in range(3)]
+    token_specs, wide = specs_of(model, depth, size, taps.shape[0])
     rate_spec = pl.BlockSpec((1, size, HEADS), lambda s, g: (s, 0, 0))
     flip_spec = pl.BlockSpec((1, HEADS, size), lambda s, g: (s, 0, 0))
 
     def out(*dims):
         return pl.BlockSpec((1, PAIR) + dims, lambda s, g: (s, g, 0, 0)), jax.ShapeDtypeStruct((seqs, HEADS) + dims, F32)
 
-    outs = [out(size, size), out(size, depth), out(size, depth), out(size, depth), out(size, depth), out(depth, depth), out(depth, depth)]
+    flat = pl.BlockSpec((1, size, wide), lambda s, g: (s, 0, g)), jax.ShapeDtypeStruct((seqs, size, model), F32)
+    outs = [out(size, size), out(size, depth), out(size, depth), flat, flat, out(depth, depth), out(depth, depth)]
     return pl.pallas_call(
         forward_kernel,
         grid=(seqs, HEADS // PAIR),
-        in_specs=rows + prior + tap_specs + [rate_spec, flip_spec],
+        in_specs=token_specs + [rate_spec, flip_spec],
         out_specs=[o[0] for o in outs],
         out_shape=[o[1] for o in outs],
         compiler_params=pltpu.CompilerParams(vmem_limit_bytes=56 * 2**20),
+        cost_estimate=cost(37),
         name="delta_forward",
     )(projected, projected, projected, before, before, before, taps, taps, taps, rates, jnp.swapaxes(rates, 1, 2))
 
 
 def backward_kernel(
-    q_ref, k_ref, v_ref, qb_ref, kb_ref, vb_ref, qt_ref, kt_ref, vt_ref, rates_ref,
-    inverse_ref, updates_ref, weights_ref, state_ref, grad_ref, leaving_ref,
-    rows_ref, prior_ref, taps_ref, rate_ref,
+    base, fresh, q_ref, k_ref, v_ref, qb_ref, kb_ref, vb_ref, qt_ref, kt_ref, vt_ref, rates_ref,
+    inverse_ref, updates_ref, weights_ref, state_ref, grad_ref, leaving_ref, *refs
 ):
+    rows_ref, last_ref, prior_ref, taps_ref, rate_ref = refs[0 if fresh else 5 :]
     depth = state_ref.shape[-1]
     size = q_ref.shape[1]
-    first = pl.program_id(1) * PAIR
+    first = base * PAIR
     row = lax.broadcasted_iota(jnp.int32, (size, size), 0)
     col = lax.broadcasted_iota(jnp.int32, (size, size), 1)
     strict = row > col
@@ -219,7 +234,7 @@
         column = column_of(rates_ref[0], first + h)
         inverse = inverse_ref[0, h]
         state = state_ref[0, h]
-        grad = grad_ref[0, h]
+        grad = grad_ref[0, :, lanes]
         leaving = leaving_ref[0, h]
         gram = jnp.where(strict, mul(k, k, NT), 0.0)
         scores = jnp.where(lower, mul(q, k, NT), 0.0)
@@ -254,51 +269,405 @@
             grad_conv = grad_act * (gate * (1.0 + conv * (1.0 - gate)))
             total = None
             ahead = None
+            spot = slice((part * PAIR + h) * depth, (part * PAIR + h + 1) * depth)
             for lag in range(width):
                 by = width - 1 - lag
                 tap = taps[lag : lag + 1]
                 term = tap * shifted_up(grad_conv, by)
                 total = term if total is None else total + term
-                taps_ref[0, part, lag : lag + 1, lanes] = jnp.sum(
+                taps_ref[0, lag : lag + 1, spot] = jnp.sum(
                     grad_conv * shifted_down(rows, before, by), axis=0, keepdims=True
                 )
                 if by:
                     early = jnp.where(index8 >= 8 - by, tap * pltpu.roll(grad_conv[:8], 8 - by, 0), 0.0)
                     ahead = early if ahead is None else ahead + early
-            rows_ref[part, 0, :, lanes] = total
-            prior_ref[0, part, :, lanes] = ahead
-
-
-def backward_parts(projected, before, taps, rates, inverse, updates, weights, state, grad, leaving, depth):
+            rows_ref[0, :, spot] = total.astype(BF16)
+            last_ref[0, :, spot] = total[size - 8 :]
+            prior_ref[0, :, spot] = ahead
+
+
+def backward_parts(seq, base, held, projected, before, taps, rates, inverse, updates, weights, state, grad, leaving, depth):
     seqs, size, model3 = projected.shape
     model = model3 // 3
     width = taps.shape[0]
-    rows, prior, wide, blocks = specs_of(model, depth, size)
-    tap_specs = [pl.BlockSpec((width, wide), functools.partial(lambda part, s, g: (0, part * blocks + g), part)) for part in range(3)]
-    rate_spec = pl.BlockSpec((1, size, HEADS), lambda s, g: (s, 0, 0))
+    token_specs, wide = specs_of(model, depth, size, width, base, seq)
+    rate_spec = pl.BlockSpec((1, size, HEADS), lambda s, g: (seq, 0, 0))
 
     def heads(*dims):
-        return pl.BlockSpec((1, PAIR) + dims, lambda s, g: (s, g, 0, 0))
-
+        return pl.BlockSpec((1, PAIR) + dims, lambda s, g: (seq, base, 0, 0))
+
+    def out(rows, kind):
+        return pl.BlockSpec((1, rows, 3 * wide), lambda s, g: (seq, 0, 0)), jax.ShapeDtypeStruct((seqs, rows, 3 * wide), kind)
+
+    rate_out = pl.BlockSpec((1, PAIR, size, 1), lambda s, g: (seq, 0, 0, 0)), jax.ShapeDtypeStruct((seqs, PAIR, size, 1), F32)
+    outs = [out(size, BF16), out(8, F32), out(8, F32), out(width, F32), rate_out]
+    in_specs = token_specs + [rate_spec, heads(size, size), heads(size, depth), heads(size, depth), heads(depth, depth), pl.BlockSpec((1, size, wide), lambda s, g: (seq, 0, base)), heads(depth, depth)]
+    count = len(in_specs)
     return pl.pallas_call(
-        backward_kernel,
+        functools.partial(backward_kernel, base, not held),
+        grid=(1, 1),
+        in_specs=in_specs + [pl.BlockSpec(memory_space=pl.ANY)] * len(held),
+        out_specs=[o[0] for o in outs],
+        out_shape=[o[1] for o in outs],
+        input_output_aliases={count + i: i for i in range(len(held))},
+        compiler_params=pltpu.CompilerParams(vmem_limit_bytes=56 * 2**20),
+        cost_estimate=cost(10),
+        name="delta_backward",
+    )(projected, projected, projected, before, before, before, taps, taps, taps, rates, inverse, updates, weights, state, grad, leaving, *held)
+
+
+def mix_kernel(alone_ref, reach_ref, state_ref, gain_ref, mixed_ref, low_ref):
+    depth = state_ref.shape[-1]
+    for h in range(PAIR):
+        lanes = slice(h * depth, (h + 1) * depth)
+        mixed = alone_ref[0, :, lanes] + mul_high(reach_ref[0, :, lanes], state_ref[0, h], NN)
+        scale = lax.rsqrt(jnp.mean(mixed * mixed, axis=-1, keepdims=True) + norm_eps)
+        mixed_ref[0, :, lanes] = mixed
+        low_ref[0, :, lanes] = (mixed * scale * gain_ref[...]).astype(BF16)
+
+
+def mix(alone, reach, state, gain):
+    seqs, size, model = alone.shape
+    depth = state.shape[-1]
+    wide = PAIR * depth
+    flat = pl.BlockSpec((1, size, wide), lambda s, g: (s, 0, g))
+    return pl.pallas_call(
+        mix_kernel,
         grid=(seqs, HEADS // PAIR),
-        in_specs=rows + prior + tap_specs + [rate_spec, heads(size, size), heads(size, depth), heads(size, depth), heads(depth, depth), heads(size, depth), heads(depth, depth)],
-        out_specs=[
-            pl.BlockSpec((3, 1, size, wide), lambda s, g: (0, s, 0, g)),
-            pl.BlockSpec((1, 3, 8, wide), lambda s, g: (s, 0, 0, g)),
-            pl.BlockSpec((1, 3, width, wide), lambda s, g: (s, 0, 0, g)),
-            heads(size, 1),
+        in_specs=[flat, flat, pl.BlockSpec((1, PAIR, depth, depth), lambda s, g: (s, g, 0, 0)), pl.BlockSpec((1, depth), lambda s, g: (0, 0))],
+        out_specs=[flat, flat],
+        out_shape=[jax.ShapeDtypeStruct(alone.shape, F32), jax.ShapeDtypeStruct(alone.shape, BF16)],
+        cost_estimate=cost(5),
+        name="mix_heads",
+    )(alone, reach, state, gain.reshape(1, depth))
+
+
+def mix_back_kernel(mixed_ref, reach_ref, gain_ref, grad_ref, back_ref, local_ref, out_ref):
+    depth = local_ref.shape[-1]
+    total = None
+    for h in range(PAIR):
+        lanes = slice(h * depth, (h + 1) * depth)
+        mixed = mixed_ref[0, :, lanes]
+        grad = grad_ref[0, :, lanes].astype(F32)
+        scale = lax.rsqrt(jnp.mean(mixed * mixed, axis=-1, keepdims=True) + norm_eps)
+        weighted = grad * gain_ref[...]
+        part = jnp.sum(grad * mixed * scale, axis=0, keepdims=True)
+        total = part if total is None else total + part
+        back = scale * weighted - mixed * (scale * scale * scale) * (
+            jnp.mean(weighted * mixed, axis=-1, keepdims=True)
+        )
+        back_ref[0, :, lanes] = back
+        local_ref[0, h] = mul_high(reach_ref[0, :, lanes], back, TN)
+    out_ref[0, 0] = jnp.broadcast_to(total, out_ref.shape[2:])
+
+
+def mix_back(mixed, reach, gain, grad):
+    seqs, size, model = mixed.shape
+    depth = gain.size
+    wide = PAIR * depth
+    flat = pl.BlockSpec((1, size, wide), lambda s, g: (s, 0, g))
+    back, local, total = pl.pallas_call(
+        mix_back_kernel,
+        grid=(seqs, HEADS // PAIR),
+        in_specs=[flat, flat, pl.BlockSpec((1, depth), lambda s, g: (0, 0)), flat],
+        out_specs=[flat, pl.BlockSpec((1, PAIR, depth, depth), lambda s, g: (s, g, 0, 0)), pl.BlockSpec((1, 1, 8, depth), lambda s, g: (s, g, 0, 0))],
+        out_shape=[
+            jax.ShapeDtypeStruct(mixed.shape, F32),
+            jax.ShapeDtypeStruct((seqs, HEADS, depth, depth), F32),
+            jax.ShapeDtypeStruct((seqs, HEADS // PAIR, 8, depth), F32),
         ],
+        cost_estimate=cost(6),
+        name="mix_heads_back",
+    )(mixed, reach, gain.reshape(1, depth), grad)
+    return back, local, jnp.sum(total[:, :, 0], axis=(0, 1))
+
+
+BOTH = ("dp", "cp")
+
+
+class Grid:
+    def __init__(self):
+        self.cp = lax.axis_size("cp")
+        group = lax.axis_size("dp")
+        self.core = 2 if group % 2 == 0 else 1
+        self.lo = 2 if group // self.core % 2 == 0 else 1
+        self.hi = group // self.core // self.lo
+        self.sizes = (self.hi, self.lo, self.core, self.cp)
+
+    def place(self):
+        member = lax.axis_index("dp")
+        return (
+            member // (self.lo * self.core),
+            member // self.core % self.lo,
+            member % self.core,
+            lax.axis_index("cp"),
+        )
+
+    def swap(self, value, axis, by):
+        step = [1] * 4
+        for later in range(3):
+            step[2 - later] = step[3 - later] * self.sizes[3 - later]
+        pairs = []
+        for device in range(step[0] * self.sizes[0]):
+            here = device // step[axis] % self.sizes[axis]
+            pairs.append((device, device + ((here ^ by) - here) * step[axis]))
+        return lax.ppermute(value, BOTH, pairs)
+
+    def others(self, value, axis):
+        return [self.swap(value, axis, by) for by in range(1, self.sizes[axis])]
+
+
+HI, LO, CORE, SEG = range(4)
+
+
+def cut_of(columns):
+    return columns // 256 * 128
+
+
+def place_kernel(cuts, spot, own_left, own_right, other_left, other_right, *outs):
+    core = spot[2]
+    for away, left, right in ((0, own_left, own_right), (1, other_left, other_right)):
+        if away >= outs[0].shape[2]:
+            continue
+        row = jnp.concatenate([left[0, 0, 0], right[0, 0, 0]], axis=1)
+        for out, (top, bottom, first, last) in zip(outs, cuts):
+            out[0, 0, core ^ away, 0] = row[top:bottom, first:last]
+
+
+def tied(value, *needed):
+    return lax.optimization_barrier((value, needed))[0] if needed else value
+
+
+class Gather:
+    def __init__(self, grid, shard):
+        self.grid = grid
+        self.shape = shard.shape
+        self.cut = cut_of(shard.shape[1])
+        self.mine = shard
+        self.sent = [shard]
+        self.got = grid.others(shard, SEG)
+
+    def exchange(self, axes):
+        self.got = [self.grid.others(piece, axis) for piece, axis in zip(self.sent, axes)]
+
+    def first(self, *needed):
+        parts = tied([self.mine] + self.got, *needed)
+        self.sent = [
+            jnp.stack([part[:, : self.cut] for part in parts]),
+            jnp.stack([part[:, self.cut :] for part in parts]),
+        ]
+        self.exchange((LO, HI))
+
+    def second(self, *needed):
+        sent, got = tied((self.sent, self.got), *needed)
+        self.sent = [jnp.stack([piece] + more) for piece, more in zip(sent, got)]
+        self.exchange((HI, LO))
+
+    def third(self, *needed):
+        sent, got = tied((self.sent, self.got), *needed)
+        self.own = [
+            jnp.stack([piece] + more, axis=axis)
+            for piece, more, axis in zip(sent, got, (0, 1))
+        ]
+        self.sent = self.own
+        self.other = [
+            self.grid.swap(piece, CORE, 1) if self.grid.core == 2 else piece for piece in self.own
+        ]
+
+    def placed(self, cuts, *needed):
+        grid, (r, total), cut = self.grid, self.shape, self.cut
+        own, other = tied((self.own, self.other), *needed)
+
+        def source(wide):
+            return pl.BlockSpec(
+                (1, 1, 1, r, wide), lambda a, b, c, spot: (a ^ spot[0], b ^ spot[1], c ^ spot[3], 0, 0)
+            )
+
+        shapes = [(bottom - top, right - left) for top, bottom, left, right in cuts]
+        sources = [source(cut), source(total - cut)]
+        outs = pl.pallas_call(
+            functools.partial(place_kernel, cuts),
+            grid_spec=pltpu.PrefetchScalarGridSpec(
+                num_scalar_prefetch=1,
+                grid=(grid.hi, grid.lo, grid.cp),
+                in_specs=sources + sources,
+                out_specs=[
+                    pl.BlockSpec((1, 1, grid.core, 1) + shape, lambda a, b, c, spot: (a, b, 0, c, 0, 0))
+                    for shape in shapes
+                ],
+            ),
+            out_shape=[jax.ShapeDtypeStruct(grid.sizes + shape, BF16) for shape in shapes],
+            cost_estimate=cost(14),
+            name="place_rows",
+        )(jnp.stack(grid.place()), *own, *other)
+        return [out.reshape(-1, out.shape[-1]) for out in outs]
+
+
+class Share:
+    def __init__(self, grid, values=None, keep=None, send=None):
+        self.grid = grid
+        self.spots = grid.place()
+        self.halved = values is None
+        if self.halved:
+            self.spots = (0, 0, 0, 0)
+        else:
+            core = self.spots[2]
+            values = [value.reshape(grid.sizes + (-1, value.shape[-1])) for value in values]
+
+            def side(index):
+                parts = [lax.dynamic_index_in_dim(value, index, 2, keepdims=False) for value in values]
+                return parts[0] if len(parts) == 1 else jnp.concatenate(parts, axis=-2)
+
+            keep, send = [side(core)], [side(core ^ 1)]
+        self.sent = send
+        self.terms = [
+            [k, grid.swap(s, CORE, 1)] if grid.core == 2 else [k] for k, s in zip(keep, send)
+        ]
+
+    def begin(self, *moves):
+        self.terms = []
+        self.sent = []
+        for array, axis, dim in moves:
+            here = self.spots[axis]
+
+            def pick(index):
+                return lax.dynamic_index_in_dim(array, index, dim, keepdims=False)
+
+            sent = [pick(here ^ by) for by in range(1, self.grid.sizes[axis])]
+            self.sent += sent
+            self.terms.append(
+                [pick(here)] + [self.grid.swap(term, axis, by + 1) for by, term in enumerate(sent)]
+            )
+
+    def summed(self, kind, *needed):
+        totals = []
+        for terms in tied(self.terms, *needed):
+            total = terms[0].astype(F32)
+            for term in terms[1:]:
+                total = total + term.astype(F32)
+            totals.append(total.astype(kind))
+        return totals
+
+    def first(self, *needed):
+        totals = self.summed(BF16, *needed)
+        if not self.halved:
+            (value,) = totals
+            cut = cut_of(value.shape[-1])
+            totals = [value[..., :cut], value[..., cut:]]
+        left, right = totals
+        self.begin((left, LO, 1), (right, HI, 0))
+
+    def second(self, *needed):
+        left, right = self.summed(BF16, *needed)
+        self.begin((left, HI, 0), (right, LO, 0))
+
+    def third(self, *needed):
+        left, right = self.summed(BF16, *needed)
+        self.begin((jnp.concatenate([left, right], axis=-1), SEG, 0))
+
+    def result(self, *needed):
+        return self.summed(F32, *needed)[0]
+
+
+def all_sum(grid, value):
+    for axis in (CORE, LO, HI, SEG):
+        by = 1
+        while by < grid.sizes[axis]:
+            value = value + grid.swap(value, axis, by)
+            by *= 2
+    return value
+
+
+def natural_rows(grid, spot, own, other):
+    rows = []
+    for a in range(grid.hi):
+        for b in range(grid.lo):
+            for k in range(grid.core):
+                for c in range(grid.cp):
+                    index = (a ^ spot[0], b ^ spot[1], c ^ spot[3])
+                    mine, theirs = own[index], other[index]
+                    rows.append(jnp.where(spot[2] == k, mine, theirs))
+    return jnp.concatenate(rows, axis=0)
+
+
+def scatter_rows(grid, spot, value, keep, send):
+    r = keep.shape[-2]
+    for a in range(grid.hi):
+        for b in range(grid.lo):
+            for c in range(grid.cp):
+                index = (a ^ spot[0], b ^ spot[1], c ^ spot[3])
+                at = ((a * grid.lo + b) * grid.core * grid.cp + c) * r
+                lower = value[at : at + r]
+                at += grid.cp * r
+                upper = value[at : at + r]
+                keep[index] = jnp.where(spot[2] == 0, lower, upper)
+                send[index] = jnp.where(spot[2] == 0, upper, lower)
+
+
+def feed_kernel(
+    grid, spot, rows_ref, flipped_ref, cot_ref, og_ref, ou_ref, tg_ref, tu_ref, down_ref,
+    out_ref, back_ref, grad_down_ref, kg_ref, sg_ref, ku_ref, su_ref,
+):
+    rows, cot = rows_ref[...], cot_ref[...]
+    w_gate = natural_rows(grid, spot, og_ref, tg_ref)
+    w_up = natural_rows(grid, spot, ou_ref, tu_ref)
+    down = down_ref[...]
+    gate = mul(rows, w_gate, NN)
+    up = mul(rows, w_up, NN)
+    sigma = jax.nn.sigmoid(gate)
+    act = gate * sigma
+    hidden = (act * up).astype(BF16)
+    grad_hidden = mul(cot, down, NT)
+    grad_gate = (grad_hidden * up * (sigma * (1.0 + gate * (1.0 - sigma)))).astype(BF16)
+    grad_up = (grad_hidden * act).astype(BF16)
+    out = mul(hidden, down, NN)
+    back = mul(grad_gate, w_gate, NT) + mul(grad_up, w_up, NT)
+
+    @pl.when(pl.program_id(0) == 0)
+    def _():
+        out_ref[...] = out
+        back_ref[...] = back
+
+    @pl.when(pl.program_id(0) > 0)
+    def _():
+        out_ref[...] += out
+        back_ref[...] += back
+
+    grad_down_ref[...] = mul(hidden, cot, TN).astype(BF16)
+    flipped = flipped_ref[...]
+    scatter_rows(grid, spot, mul(flipped, grad_gate, NN).astype(BF16), kg_ref, sg_ref)
+    scatter_rows(grid, spot, mul(flipped, grad_up, NN).astype(BF16), ku_ref, su_ref)
+
+
+def feed_forward(grid, rows, cot, gather, w_down):
+    tokens, model = rows.shape
+    half = w_down.shape[0]
+    tile = 256
+    r = gather.shape[0]
+    lead = (grid.hi, grid.lo, grid.cp, r)
+    whole = pl.BlockSpec((tokens, model), lambda j, spot: (0, 0))
+    piece = pl.BlockSpec(lead + (tile,), lambda j, spot: (0, 0, 0, 0, j))
+    down = pl.BlockSpec((tile, model), lambda j, spot: (j, 0))
+    share = jax.ShapeDtypeStruct(lead + (half,), BF16)
+    out, back, grad_down, kg, sg, ku, su = pl.pallas_call(
+        functools.partial(feed_kernel, grid),
+        grid_spec=pltpu.PrefetchScalarGridSpec(
+            num_scalar_prefetch=1,
+            grid=(half // tile,),
+            in_specs=[whole, pl.BlockSpec((model, tokens), lambda j, spot: (0, 0)), whole] + [piece] * 4 + [down],
+            out_specs=[whole, whole, down] + [piece] * 4,
+        ),
         out_shape=[
-            jax.ShapeDtypeStruct((3, seqs, size, model), F32),
-            jax.ShapeDtypeStruct((seqs, 3, 8, model), F32),
-            jax.ShapeDtypeStruct((seqs, 3, width, model), F32),
-            jax.ShapeDtypeStruct((seqs, HEADS, size, 1), F32),
+            jax.ShapeDtypeStruct((tokens, model), F32),
+            jax.ShapeDtypeStruct((tokens, model), F32),
+            jax.ShapeDtypeStruct((half, model), BF16),
+            share, share, share, share,
         ],
-        compiler_params=pltpu.CompilerParams(vmem_limit_bytes=56 * 2**20),
-        name="delta_backward",
-    )(projected, projected, projected, before, before, before, taps, taps, taps, rates, inverse, updates, weights, state, grad, leaving)
+        compiler_params=pltpu.CompilerParams(vmem_limit_bytes=58 * 2**20),
+        cost_estimate=cost(33),
+        name="feed_forward",
+    )(jnp.stack(grid.place()), rows, rows.T, cot, *gather.own, *gather.other, w_down)
+    return out, back, grad_down, (kg, ku), (sg, su)
 
 
 def passed_along(value, axis, by):
@@ -331,9 +700,6 @@
         jnp.sum(weighted * rows, axis=-1, keepdims=True) / width
     )
     return (gain_grad, row_grad)
-
-
-BOTH = ("dp", "cp")
 
 
 def per_device(
@@ -346,15 +712,25 @@
     peers = lax.axis_size(BOTH)
     share = model // peers
     tap_share = conv_taps.shape[1]
+    hops = lax.axis_size("cp") - 1
+    grid = Grid()
+
+    even = -(-share // 16) * 16
+    down_share = down_weight.shape[0]
+    mats = jnp.concatenate([jnp.pad(proj_weight, ((0, even - share), (0, 0))), down_weight], axis=0)
     small = jnp.concatenate(
         [mixer_gain, ffn_gain, beta_weight.reshape(-1), conv_taps.reshape(-1)]
     )
-    small = jnp.pad(small, (0, 1024 - small.size)).reshape(8, 128)
-    small = lax.all_gather(small, BOTH, axis=0, tiled=False).reshape(peers, 1024)
-    w_qkv = lax.all_gather(qkv_weight, BOTH, axis=0, tiled=True)
-    w_proj = lax.all_gather(proj_weight, BOTH, axis=0, tiled=True)
-    w_gateup = lax.all_gather(gate_up, BOTH, axis=0, tiled=True)
-    w_down = lax.all_gather(down_weight, BOTH, axis=0, tiled=True)
+    small = jnp.pad(small, (0, share * 128 - small.size)).reshape(share, 128)
+    get_qkv = Gather(grid, jnp.concatenate([qkv_weight, small], axis=1))
+    get_gateup = Gather(grid, tied(gate_up, *get_qkv.got))
+    get_qkv.first()
+    get_qkv.second()
+    get_qkv.third()
+    w_qkv, small = get_qkv.placed(((0, share, 0, 3 * model), (0, share, 3 * model, 3 * model + 128)))
+    get_gateup.first(w_qkv)
+    get_mats = Gather(grid, tied(mats, *get_gateup.sent))
+    small = small.reshape(peers, share * 128)
     gain_one = small[:, :share].reshape(-1)
     gain_two = small[:, share : 2 * share].reshape(-1)
     at = 2 * share
@@ -367,112 +743,151 @@
     resid_in = block_input.astype(F32)
     scale_one = lax.rsqrt(jnp.mean(resid_in * resid_in, axis=-1, keepdims=True) + norm_eps)
     normed_one = (resid_in * scale_one * gain_one.astype(F32)).astype(BF16)
+    normed_one = tied(normed_one, *get_gateup.sent, *get_mats.sent)
     projected = rows_times(normed_one, w_qkv).astype(BF16)
     tail = projected[:, seg_len - (width - 1) :, :]
     before = jnp.pad(passed_along(tail, "cp", 1), ((0, 0), (8 - (width - 1), 0), (0, 0)))
     rates = jax.nn.sigmoid(rows_times(normed_one, w_beta))
+    get_gateup.second(projected)
+    get_mats.first(projected)
+    projected = tied(projected, *get_gateup.sent, *get_mats.sent)
     inverse, updates, weights, reach, alone, transfer, offset = forward_parts(
         projected, before, taps, rates, depth
     )
-    carried = jnp.zeros_like(offset)
-    for step in range(lax.axis_size("cp") - 1):
-        sent = offset if step == 0 else apply_map(transfer, carried, offset)
-        carried = passed_along(sent.astype(BF16), "cp", 1).astype(F32)
-    mixed = alone + jnp.einsum("shtd,shde->shte", reach, carried, precision=lax.Precision.HIGH)
-    scale_mix = lax.rsqrt(jnp.mean(mixed * mixed, axis=-1, keepdims=True) + norm_eps)
-    mixed_low = jnp.swapaxes(mixed * scale_mix * gain_outf, 1, 2).reshape(seqs, seg_len, model).astype(BF16)
+    carried = jnp.zeros(offset.shape, BF16)
+    for step in range(hops):
+        sent = offset if step == 0 else apply_map(transfer, carried.astype(F32), offset)
+        sent = sent.astype(BF16)
+        carried = passed_along(sent, "cp", 1)
+        if step == 0:
+            get_mats.second(sent)
+            get_gateup.third(sent)
+            carried = tied(carried, *get_mats.sent, *get_gateup.sent)
+        if step == 2:
+            get_mats.third(sent)
+            w_proj, w_down = get_mats.placed(((0, share, 0, model), (even, even + down_share, 0, model)), sent)
+            carried = tied(carried, w_down, w_proj)
+    mixed, mixed_low = mix(alone, reach, carried, gain_outf)
+
     attn = rows_times(mixed_low, w_proj)
     middle = resid_in + attn
     scale_two = lax.rsqrt(jnp.mean(middle * middle, axis=-1, keepdims=True) + norm_eps)
     gain_twof = gain_two.astype(F32)
     normed_two = (middle * scale_two * gain_twof).astype(BF16)
-    gates = rows_times(normed_two, w_gateup)
-    half = gates.shape[-1] // 2
-    gate_part = gates[..., :half]
-    up_part = gates[..., half:]
-    hidden = (jax.nn.silu(gate_part) * up_part).astype(BF16)
-    ffn_out = rows_times(hidden, w_down)
+    tokens = seqs * seg_len
+    ffn_out, grad_normed_two, grad_down, keep, send = feed_forward(
+        grid, normed_two.reshape(tokens, model), cotangent.reshape(tokens, model), get_gateup, w_down
+    )
+    ffn_out = ffn_out.reshape(middle.shape)
+    grad_normed_two = grad_normed_two.reshape(middle.shape)
+    put_gateup = Share(grid, keep=keep, send=send)
     result = middle + ffn_out
     squares = jnp.stack(
         [jnp.sum(result * result), jnp.sum(attn * attn), jnp.sum(ffn_out * ffn_out)]
     )
     upstream = cotangent.astype(F32)
-    grad_down = weight_grad(hidden, cotangent).astype(BF16)
-    grad_hidden = rows_back(cotangent, w_down)
-    sigma = jax.nn.sigmoid(gate_part)
-    grad_gate = grad_hidden * up_part * (sigma * (1.0 + gate_part * (1.0 - sigma)))
-    grad_up = grad_hidden * (gate_part * sigma)
-    grad_gates = jnp.concatenate([grad_gate, grad_up], axis=-1).astype(BF16)
-    grad_gateup = weight_grad(normed_two, grad_gates).astype(BF16)
-    grad_normed_two = rows_back(grad_gates, w_gateup)
     grad_ffn, grad_from_norm = norm_back(middle, scale_two, gain_twof, grad_normed_two)
     grad_middle = upstream + grad_from_norm
     grad_attn = grad_middle.astype(BF16)
     grad_proj = weight_grad(mixed_low, grad_attn).astype(BF16)
-    grad_normed_mix = rows_back(grad_attn, w_proj).astype(BF16).astype(F32)
-    grad_normed_mix = jnp.swapaxes(grad_normed_mix.reshape(seqs, seg_len, HEADS, depth), 1, 2)
-    grad_out, grad_mixed = norm_back(mixed, scale_mix, gain_outf, grad_normed_mix)
-    local_part = jnp.einsum("shtd,shte->shde", reach, grad_mixed, precision=lax.Precision.HIGH)
+    put_mats = Share(grid, [grad_proj, grad_down])
+    grad_normed_mix = rows_back(tied(grad_attn, grad_proj), w_proj).astype(BF16)
+
+    grad_mixed, local_part, grad_out = mix_back(mixed, reach, gain_outf, grad_normed_mix)
     flipped = jnp.swapaxes(transfer, -1, -2)
-    incoming = jnp.zeros_like(local_part)
-    for step in range(lax.axis_size("cp") - 1):
-        sent = local_part if step == 0 else apply_map(flipped, incoming, local_part)
-        incoming = passed_along(sent.astype(BF16), "cp", -1).astype(F32)
-    grad_rows, grad_prior, grad_taps, grad_rates = backward_parts(
-        projected, before, taps, rates, inverse, updates, weights, carried, grad_mixed, incoming, depth
-    )
-    returned = passed_along(grad_prior, "cp", -1)
-    grad_rows = jnp.concatenate(
-        [
-            grad_rows[:, :, : seg_len - 8],
-            grad_rows[:, :, seg_len - 8 :] + jnp.swapaxes(returned, 0, 1),
-        ],
-        axis=2,
-    ).astype(BF16)
-    grad_projected = jnp.moveaxis(grad_rows, 0, 2).reshape(seqs, seg_len, 3 * model)
-    grad_rates = jnp.swapaxes(grad_rates[..., 0], 1, 2)
+    incoming = jnp.zeros(local_part.shape, BF16)
+    for step in range(hops):
+        sent = local_part if step == 0 else apply_map(flipped, incoming.astype(F32), local_part)
+        sent = sent.astype(BF16)
+        incoming = passed_along(sent, "cp", -1)
+        if step == 0:
+            put_gateup.first(sent)
+            incoming = tied(incoming, *put_gateup.sent)
+        if step == 1:
+            put_mats.first(sent)
+            incoming = tied(incoming, *put_mats.sent)
+    puts = []
+    grad_rows = []
+    grad_rates = []
+    grad_taps = []
+    arrays = (projected, before, taps, rates, inverse, updates, weights, carried, grad_mixed)
+
+    def fixed(held):
+        rows, last, prior = held[:3]
+        returned = passed_along(prior, "cp", -1)
+        return lax.dynamic_update_slice(rows, (last + returned).astype(BF16), (0, seg_len - 8, 0))
+
+    for base in range(HEADS // PAIR):
+        held = ()
+        for seq in range(seqs):
+            held = backward_parts(seq, base, held, *arrays, incoming, depth)
+            if (base, seq) == (0, 0):
+                put_gateup.second(held[0])
+                incoming = tied(incoming, *put_gateup.sent)
+            if (base, seq) == (0, seqs - 1):
+                put_mats.second(held[0])
+                incoming = tied(incoming, *put_mats.sent)
+                rows_early = fixed(held)
+            if (base, seq) == (1, 0):
+                put_gateup.third(held[0])
+                rows_early = tied(rows_early, held[0])
+                puts.append(Share(grid, [weight_grad(normed_one, rows_early).astype(BF16)]))
+                incoming = tied(incoming, *put_gateup.sent, *puts[0].sent)
+        grad_rates.append(held[4][..., 0])
+        grad_taps.append(jnp.sum(held[3], axis=0))
+        grad_rows.append(rows_early if base == 0 else fixed(held))
+    puts[0].first(held[0])
+    puts.append(None)
+    grad_rates = jnp.swapaxes(jnp.concatenate(grad_rates, axis=1), 1, 2)
     grad_logits = grad_rates * rates * (1.0 - rates)
-    grad_qkv = weight_grad(normed_one, grad_projected).astype(BF16)
     grad_beta = jnp.einsum("sga,sgb->ab", normed_one.astype(F32), grad_logits, precision=lax.Precision.HIGH)
-    grad_normed_one = rows_back(grad_projected, w_qkv)
+    wide = PAIR * depth
+    grad_conv = jnp.stack([part.reshape(width, 3, wide) for part in grad_taps], axis=2).reshape(width, 3 * model)
+    grad_conv = jnp.swapaxes(grad_conv.reshape(width, peers, tap_share), 0, 1)
+    pieces = [grad_ffn, grad_beta, grad_conv]
+    pieces = jnp.concatenate([piece.reshape(peers, -1) for piece in pieces], axis=1)
+    pieces = jnp.pad(pieces, ((0, 0), (0, share * 128 - pieces.shape[1]))).astype(BF16)
+    late = weight_grad(normed_one, tied(grad_rows[1], *puts[0].sent)).astype(BF16)
+    puts[1] = Share(grid, [jnp.concatenate([late, pieces.reshape(model, 128)], axis=1)])
+    grad_rows = tied(grad_rows, *puts[1].sent)
+    columns = [rows[..., part * wide : (part + 1) * wide] for part in range(3) for rows in grad_rows]
+    grad_normed_one = rows_back(jnp.concatenate(columns, axis=-1), w_qkv)
+    puts[1].first(grad_normed_one)
+    puts[0].second(grad_normed_one)
+    put_mats.third(grad_normed_one)
+    grad_normed_one = tied(grad_normed_one, *puts[0].sent, *puts[1].sent, *put_mats.sent)
     grad_normed_one = grad_normed_one + jnp.einsum(
         "sgb,ab->sga", grad_logits, w_beta.astype(F32), precision=lax.Precision.HIGH
     )
     grad_mixer, grad_from_first = norm_back(resid_in, scale_one, gain_one.astype(F32), grad_normed_one)
     grad_input = grad_middle + grad_from_first
-    grad_conv = jnp.moveaxis(jnp.sum(grad_taps, axis=0), 0, 1).reshape(width, 3 * model)
-    grad_conv = jnp.swapaxes(grad_conv.reshape(width, peers, tap_share), 0, 1).reshape(-1)
-    pieces = [grad_mixer, grad_ffn, grad_beta.reshape(-1), grad_conv, squares, grad_out]
-    sizes = [p.size for p in pieces]
-    packed = jnp.concatenate(pieces)
-    packed = jnp.pad(packed, (0, -packed.size % 1024)).reshape(-1, 128)
-    packed = lax.psum(packed, BOTH).reshape(-1)
-    ends = [sum(sizes[: i + 1]) for i in range(len(sizes))]
-    starts = [0] + ends[:-1]
-    me = lax.axis_index(BOTH)
-
-    def mine(i):
-        own = sizes[i] // peers
-        return lax.dynamic_slice(packed[starts[i] : ends[i]], (me * own,), (own,))
-
-    rms_values = jnp.sqrt(packed[starts[4] : ends[4]] / (result.size * peers))
-
-    def scattered(grad):
-        return lax.psum_scatter(grad, BOTH, scatter_dimension=0, tiled=True).astype(F32)
-
+    flat = jnp.concatenate([squares, grad_out, grad_mixer])
+    flat = jnp.pad(flat, (0, -flat.size % 1024)).reshape(-1, 128)
+    sums = all_sum(grid, flat).reshape(-1)
+    puts[1].second(grad_input)
+    puts[0].third(grad_input)
+    puts[1].third()
+    shares = [put.result() for put in puts]
+    own = shares[1][:, 3 * wide :].reshape(-1)
+    shares[1] = shares[1][:, : 3 * wide]
+    share_qkv = jnp.stack([part.reshape(share, 3, wide) for part in shares], axis=2).reshape(share, 3 * model)
+    share_mats = put_mats.result()
+    ends = [share, share + share * HEADS, share + share * HEADS + width * tap_share]
+    at = 3 + depth
+    mixer_share = lax.dynamic_slice(sums[at : at + model], (lax.axis_index(BOTH) * share,), (share,))
     return (
         result.astype(BF16),
         grad_input,
-        mine(0),
-        scattered(grad_qkv),
-        mine(3).reshape(width, tap_share),
-        mine(2).reshape(share, HEADS),
-        packed[starts[5] : ends[5]],
-        scattered(grad_proj),
-        mine(1),
-        scattered(grad_gateup),
-        scattered(grad_down),
-        rms_values,
+        mixer_share,
+        share_qkv,
+        own[ends[1] : ends[2]].reshape(width, tap_share),
+        own[ends[0] : ends[1]].reshape(share, HEADS),
+        sums[3 : 3 + depth],
+        share_mats[:share],
+        own[: ends[0]],
+        put_gateup.result(),
+        share_mats[share:],
+        jnp.sqrt(sums[:3] / (result.size * peers)),
     )
 
 

time: 1280 us -> 560 us (0.44)
  waiting for transfers between devices: 921 us -> 107 us
  Pallas kernels: 72.7 us -> 159 us
  starting transfers between devices: 21.7 us -> 104 us
  matrix products: 110 us -> 34.3 us
  blocking collectives: 71.2 us -> 0 us
  other arithmetic: 29.7 us -> 82.1 us
  local copies, waits for them, and re-layouts: 39.2 us -> 63.2 us
    reduce_scatter x4 -> x0, waiting for transfers between devices: 657 us -> none  [scattered(): lax.psum_scatter(grad, BOTH, scatter_dimension=0, tiled=True).astype(F32)]
    all_gather x4 -> x0, waiting for transfers between devices: 88.4 us -> none  [the longest x1 56.2 us: per_device(): w_down = lax.all_gather(down_weight, BOTH, axis=0, tiled=True)]
    pallas_call x2 -> x10, Pallas kernels: 72.7 us -> 159 us  [the longest x4 44.8 us: backward_parts(): pl.pallas_call(functools.partial(backward_kernel, base, not held), grid=(...]
    psum x1 -> x0, waiting for transfers between devices: 85.9 us -> none  [per_device(): packed = lax.psum(packed, BOTH).reshape(-1)]
    ppermute x0 -> x65, starting transfers between devices: none -> 83.2 us  [swap(): return lax.ppermute(value, BOTH, pairs)]
    ppermute x0 -> x65, waiting for transfers between devices: none -> 78.5 us  [swap(): return lax.ppermute(value, BOTH, pairs)]
    all_gather x1 -> x0, blocking collectives: 71.2 us -> none  [per_device(): lax.all_gather(small, BOTH, axis=0, tiled=False).reshape(peers, 1024)]
    ppermute x8 -> x9, waiting for transfers between devices: 86.6 us -> 28.7 us  [passed_along(): return lax.ppermute(value, axis, pairs)]
  transfers between devices with their start and end apart: 17 -> 74, of which waited for: 13 -> 23; matrix products, arithmetic and copies ran while one was open for 8% -> 29% of each run, Pallas kernels for 3% -> 21%
where the time goes in v3:
time: 560 us; the launch traced here: 552 us
  Pallas kernels  159 us (28%)
  waiting for transfers between devices  107 us (19%)
  starting transfers between devices  104 us (19%)
  other arithmetic  82.1 us (15%)
  local copies, waits for them, and re-layouts  63.2 us (11%)
  matrix products  34.3 us (6%)
    ppermute x65, starting transfers between devices, swap(): return lax.ppermute(value, BOTH, pairs)  83.2 us
    ppermute x65, waiting for transfers between devices, swap(): return lax.ppermute(value, BOTH, pairs)  78.5 us
    pallas_call x4, Pallas kernels, backward_parts(): pl.pallas_call(functools.partial(backward_kernel, base, not held), grid=(...  44.8 us
    pallas_call x1, Pallas kernels, feed_forward(): pl.pallas_call(functools.partial(feed_kernel, grid), grid_spec=pltpu.Pref...  41.7 us
    pallas_call x1, Pallas kernels, forward_parts(): pl.pallas_call(forward_kernel, grid=(seqs, HEADS // PAIR), in_specs=token...  36.8 us
    ppermute x9, waiting for transfers between devices, passed_along(): return lax.ppermute(value, axis, pairs)  28.7 us
    convert_element_type x21, other arithmetic, summed(): totals.append(total.astype(kind))  26.7 us
    pallas_call x2, Pallas kernels, placed(): pl.pallas_call(functools.partial(place_kernel, cuts), grid_spec=pltpu.Pre...  24.7 us
  transfers between devices with their start and end apart: 74, of which 23 were waited for; matrix products, arithmetic and copies ran while one was open for 29% of the time, Pallas kernels for 21%

profile of v3, /device:TPU:0, one launch (start us, length us, event | category | flops | bytes accessed | tf_op | source)
XLA Modules:
  0.0 552.0 jit_solution(6573315711465647160)
XLA Ops:
  4.0 3.1 collective-permute-start
  7.1 2.6 collective-permute-start.1
  11.5 11.8 %collective-permute-done.2 = bf16[32,3200]{1,0:T(8,128)(2,1)S(1)} collective-permute-done((bf16[32,3200]{1,0:T(8,128)(2,1)S(1)}, bf16[32,3200]{1,0:T(8,128)(2,1)S(1)}, u32[]{:S(2)}, u32[]{:S(2)}) %collective-permute-start.2) | collective-permute-done | bytes 204832 | tf_op jit(solution)/shard_map/ppermute | solution.py:414
  28.1 5.2 collective-permute-done.3
  35.1 3.1 collective-permute-done.5
  38.7 4.6 collective-permute-start.10
  45.9 19.5 %collective-permute-done.10 = bf16[32,5632]{1,0:T(8,128)(2,1)S(1)} collective-permute-done((bf16[32,5632]{1,0:T(8,128)(2,1)S(1)}, bf16[32,5632]{1,0:T(8,128)(2,1)S(1)}, u32[]{:S(2)}, u32[]{:S(2)}) %collective-permute-start.10) | collective-permute-done | bytes 360480 | tf_op jit(solution)/shard_map/ppermute | solution.py:414
  67.5 7.0 %collective-permute-start.14 = (bf16[120,1024]{1,0:T(8,128)(2,1)S(1)}, bf16[120,1024]{1,0:T(8,128)(2,1)S(1)}, u32[]{:S(2)}, u32[]{:S(2)}) collective-permute-start(bf16[120,1024]{1,0:T(8,128)(2,1)S(1)} %pad_maximum_fusion.23), channel_id=1, source_target_pairs={{0,1},{1,0},{2,3},{3,2},{4,5},{5,4},{6,7},{7,6},{8,9},{9,8},{10,11... | collective-permute-start | bytes 737288 | tf_op jit(solution)/shard_map/ppermute | solution.py:414
  80.7 12.1 %place_rows.2 = (bf16[2,2,2,4,32,3072]{5,4,3,2,1,0:T(8,128)(2,1)}, bf16[2,2,2,4,32,128]{5,4,3,2,1,0:T(8,128)(2,1)}) custom-call(s32[4]{0:T(128)} %pad_add_fusion.spot, bf16[2,2,4,32,1536]{4,3,2,1,0:T(8,128)(2,1)} %copy-done.33, bf16[2,2,4,32,1664]{4,3,2,1,0:T(8,128)(2,1)} %copy-done.32, bf16[2,2,4,32,1536]{4,3,2,1,0:T(8,128)(2,1)} %copy-done.56, ...), custom_call_target="tpu_custom_call" | custom-call | flops 16099999744 | bytes 1048576 | tf_op jit(solution)/shard_map/place_rows/pallas_call | solution.py:488
  94.4 6.8 %convolution_convert_fusion.q_ref.k_ref.v_ref = bf16[2,256,3072]{2,1,0:T(8,128)(2,1)S(1)} fusion(bf16[2,256,1024]{2,1,0:T(8,128)(2,1)S(1)} %fusion.2, bf16[1024,3072,1]{1,0,2:T(8,128)(2,1)} %bitcast.348), kind=kOutput, calls=%fused_computation.13 | convolution fusion | flops 3222798336 | bytes 10485760 | tf_op jit(solution)/shard_map/sga,ab->sgb/dot_general | solution.py:684
  112.6 3.7 collective-permute-start.17
  121.1 36.8 %delta_forward.1 = (f32[2,8,256,256]{3,2,1,0:T(8,128)}, f32[2,8,256,128]{3,2,1,0:T(8,128)}, f32[2,8,256,128]{3,2,1,0:T(8,128)}, f32[2,256,1024]{2,1,0:T(8,128)},...) custom-call(bf16[2,256,3072]{2,1,0:T(8,128)(2,1)} %copy-done.54, ...), custom_call_target="tpu_custom_call" | custom-call | flops 42550001664 | bytes 1048576 | tf_op jit(solution)/shard_map/delta_forward/pallas_call | solution.py:187
  165.8 3.3 pad_maximum_fusion.3.ou_ref
  169.1 3.3 pad_maximum_fusion.2.og_ref
  172.9 2.6 collective-permute-start.23
  175.5 8.5 %collective-permute-done.23 = bf16[2,8,128,128]{3,2,1,0:T(8,128)(2,1)S(1)} collective-permute-done((bf16[2,8,128,128]{3,2,1,0:T(8,128)(2,1)S(1)}, bf16[2,8,128,128]{3,2,1,0:T(8,128)(2,1)S(1)}, u32[]{:S(2)}, u32[]{:S(2)}) %collective-permute-start.23) | collective-permute-done | bytes 524320 | tf_op jit(solution)/shard_map/ppermute | solution.py:676
  188.8 5.4 collective-permute-start.24
  194.3 12.5 %place_rows.3 = (bf16[2,2,2,4,32,1024]{5,4,3,2,1,0:T(8,128)(2,1)}, bf16[2,2,2,4,88,1024]{5,4,3,2,1,0:T(8,128)(2,1)}) custom-call(s32[4]{0:T(128)} %pad_add_fusion.spot, bf16[2,2,4,120,512]{4,3,2,1,0:T(8,128)(2,1)} %pad_maximum_fusion.4.own_left, bf16[2,2,4,120,512]{4,3,2,1,0:T(8,128)(2,1)} %copy-done.28, ...), custom_call_target="tpu_custom_call" | custom-call | flops 16099999744 | bytes 1048576 | tf_op jit(solution)/shard_map/place_rows/pallas_call | solution.py:488
  206.8 5.1 mix_heads.1
  211.9 4.2 multiply_reduce_fusion.5
  219.6 41.7 %feed_forward.1 = (f32[512,1024]{1,0:T(8,128)}, f32[512,1024]{1,0:T(8,128)}, bf16[2816,1024]{1,0:T(8,128)(2,1)}, bf16[2,2,4,32,2816]{4,3,2,1,0:T(8,128)(2,1)}, b...) custom-call(s32[4]{0:T(128)} %pad_add_fusion.spot, ...), custom_call_target="tpu_custom_call" | custom-call | flops 37950001152 | bytes 1048576 | tf_op jit(solution)/shard_map/feed_forward/pallas_call | solution.py:652
  261.4 3.7 copy.195
  271.3 2.5 dynamic-slice_bitcast_fusion
  273.8 2.5 pad_maximum_fusion.1
  278.6 5.8 %mix_heads_back.1 = (f32[2,256,1024]{2,1,0:T(8,128)}, f32[2,8,128,128]{3,2,1,0:T(8,128)}, f32[2,2,8,128]{3,2,1,0:T(8,128)}) custom-call(f32[2,256,1024]{2,1,0:T(8,128)} %get-tuple-element.186.mixed_ref, f32[2,256,1024]{2,1,0:T(8,128)} %get-tuple-element.157.reach_ref, f32[1,128]{1,0:T(1,128)} %bitcast_convert_fusion.3.gain_ref, ...), custom_call_target="tpu_custom_call" | custom-call | flops 6899999744 | bytes 1048576 | tf_op jit(solution)/shard_map/mix_heads_back/pallas_call | solution.py:369
  287.3 2.5 pad_maximum_fusion
  290.0 2.6 add_convert_fusion.1
  295.4 2.6 add_convert_fusion.2
  304.1 4.1 add_convert_fusion
  311.5 6.7 %collective-permute-done.34 = bf16[2,8,128,128]{3,2,1,0:T(8,128)(2,1)S(1)} collective-permute-done((bf16[2,8,128,128]{3,2,1,0:T(8,128)(2,1)S(1)}, bf16[2,8,128,128]{3,2,1,0:T(8,128)(2,1)S(1)}, u32[]{:S(2)}, u32[]{:S(2)}) %collective-permute-start.34) | collective-permute-done | bytes 524320 | tf_op jit(solution)/shard_map/ppermute | solution.py:676
  325.8 8.8 %collective-permute-done.36.leaving_ref = bf16[2,8,128,128]{3,2,1,0:T(8,128)(2,1)} collective-permute-done((bf16[2,8,128,128]{3,2,1,0:T(8,128)(2,1)}, bf16[2,8,128,128]{3,2,1,0:T(8,128)(2,1)}, u32[]{:S(2)}, u32[]{:S(2)}) %collective-permute-start.36) | collective-permute-done | bytes 524320 | tf_op jit(solution)/shard_map/ppermute | solution.py:676
  334.6 11.1 %delta_backward.4 = (bf16[2,256,1536]{2,1,0:T(8,128)(2,1)}, f32[2,8,1536]{2,1,0:T(8,128)}, f32[2,8,1536]{2,1,0:T(8,128)}, f32[2,4,1536]{2,1,0:T(4,128)}, f32[2,4,256,1]{3,2,1,0:T(8,128)}) custom-call(bf16[2,256,3072]{2,1,0:T(8,128)(2,1)} %copy-done.54, bf16[2,256,3072]{2,1,0:T(8,128)(2,1)} %copy-done.54, bf16[2,256,3072]{2,1,0:T(8,128)(2,1)} %copy-done.54, ...), custom_call_target="tpu_custom_call" | custom-call | flops 11500000256 | bytes 1048576 | tf_op jit(solution)/shard_map/delta_backward/pallas_call | solution.py:306
  345.7 10.2 %collective-permute-done.38 = bf16[2,4,32,2816]{3,2,1,0:T(8,128)(2,1)} collective-permute-done((bf16[2,4,32,2816]{3,2,1,0:T(8,128)(2,1)}, bf16[2,4,32,2816]{3,2,1,0:T(8,128)(2,1)}, u32[]{:S(2)}, u32[]{:S(2)}) %collective-permute-start.38) | collective-permute-done | bytes 1441824 | tf_op jit(solution)/shard_map/ppermute | solution.py:414
  364.5 11.4 %delta_backward.5 = (bf16[2,256,1536]{2,1,0:T(8,128)(2,1)}, f32[2,8,1536]{2,1,0:T(8,128)}, f32[2,8,1536]{2,1,0:T(8,128)}, f32[2,4,1536]{2,1,0:T(4,128)}, f32[2,4,256,1]{3,2,1,0:T(8,128)}) custom-call(bf16[2,256,3072]{2,1,0:T(8,128)(2,1)} %copy-done.54, ...), custom_call_target="tpu_custom_call", output_to_operand_aliasing={{0}: (16, {}), {1}: (17, {}), {2}: (18, {}), {3}: (19, {}),... | custom-call | flops 11500000256 | bytes 1048576 | tf_op jit(solution)/shard_map/delta_backward/pallas_call | solution.py:306
  387.0 11.0 %delta_backward.6 = (bf16[2,256,1536]{2,1,0:T(8,128)(2,1)}, f32[2,8,1536]{2,1,0:T(8,128)}, f32[2,8,1536]{2,1,0:T(8,128)}, f32[2,4,1536]{2,1,0:T(4,128)}, f32[2,4,256,1]{3,2,1,0:T(8,128)}) custom-call(bf16[2,256,3072]{2,1,0:T(8,128)(2,1)} %copy-done.54, bf16[2,256,3072]{2,1,0:T(8,128)(2,1)} %copy-done.54, bf16[2,256,3072]{2,1,0:T(8,128)(2,1)} %copy-done.54, ...), custom_call_target="tpu_custom_call" | custom-call | flops 11500000256 | bytes 1048576 | tf_op jit(solution)/shard_map/delta_backward/pallas_call | solution.py:306
  398.7 3.2 bitcast_convert_fusion.1
  407.6 3.3 collective-permute-start.71
  413.2 11.2 %delta_backward.7 = (bf16[2,256,1536]{2,1,0:T(8,128)(2,1)}, f32[2,8,1536]{2,1,0:T(8,128)}, f32[2,8,1536]{2,1,0:T(8,128)}, f32[2,4,1536]{2,1,0:T(4,128)}, f32[2,4,256,1]{3,2,1,0:T(8,128)}) custom-call(bf16[2,256,3072]{2,1,0:T(8,128)(2,1)} %copy-done.54, ...), custom_call_target="tpu_custom_call", output_to_operand_aliasing={{0}: (16, {}), {1}: (17, {}), {2}: (18, {}), {3}: (19, {}),... | custom-call | flops 11500000256 | bytes 1048576 | tf_op jit(solution)/shard_map/delta_backward/pallas_call | solution.py:306
  447.4 2.5 collective-permute-done.44
  454.9 3.4 fusion.97
  473.0 13.7 %collective-permute-done.69 = bf16[120,1024]{1,0:T(8,128)(2,1)S(1)} collective-permute-done((bf16[120,1024]{1,0:T(8,128)(2,1)S(1)}, bf16[120,1024]{1,0:T(8,128)(2,1)S(1)}, u32[]{:S(2)}, u32[]{:S(2)}) %collective-permute-start.69) | collective-permute-done | bytes 245792 | tf_op jit(solution)/shard_map/ppermute | solution.py:414
  496.8 3.2 fusion.8
  499.9 2.7 concatenate.61
  504.9 5.2 fusion.5
  513.9 4.8 collective-permute-start.54
  520.4 2.5 collective-permute-start.55
  536.1 2.6 collective-permute-done.64
  543.6 2.7 collective-permute-done.66
  (428 shorter events, 199.9 us)
Async XLA Ops:
  4.0 20.8 %collective-permute-start = (bf16[32,3200]{1,0:T(8,128)(2,1)S(1)}, bf16[32,3200]{1,0:T(8,128)(2,1)S(1)}, u32[]{:S(2)}, u32[]{:S(2)}) collective-permute-start(bf16[32,3200]{1,0:T(8,128)(2,1)S(1)} %pad_maximum_fusion.22), channel_id=1, source_target_pairs={{0,1},{1,0},{2,3},{3,2},{4,5},{5,4},{6,7},{7,6},{8,9},{9,8},{10,11... | collective-permute-start | bytes 614408 | tf_op jit(solution)/shard_map/ppermute | solution.py:414
  7.1 17.7 %collective-permute-start.1 = (bf16[32,3200]{1,0:T(8,128)(2,1)S(1)}, bf16[32,3200]{1,0:T(8,128)(2,1)S(1)}, u32[]{:S(2)}, u32[]{:S(2)}) collective-permute-start(bf16[32,3200]{1,0:T(8,128)(2,1)S(1)} %pad_maximum_fusion.22), channel_id=1, source_target_pairs={{0,2},{1,3},{2,0},{3,1},{4,6},{5,7},{6,4},{7,5},{8,10},{9,11},{10,... | collective-permute-start | bytes 614408 | tf_op jit(solution)/shard_map/ppermute | solution.py:414
  33.5 32.1 %collective-permute-start.4 = (bf16[2,4,32,1536]{3,2,1,0:T(8,128)(2,1)S(1)}, bf16[2,4,32,1536]{3,2,1,0:T(8,128)(2,1)S(1)}, u32[]{:S(2)}, u32[]{:S(2)}) collective-permute-start(bf16[2,4,32,1536]{3,2,1,0:T(8,128)(2,1)S(1)} %get-tuple-element.391), channel_id=1, source_target_pairs={{0,16},{1,17},{2,18},{3,19},{4,20},{5,21},{6,22},{7,23},{8,24},{9,... | collective-permute-start | bytes 2359304 | tf_op jit(solution)/shard_map/ppermute | solution.py:414
  38.3 27.5 %collective-permute-start.6 = (bf16[2,4,32,1664]{3,2,1,0:T(8,128)(2,1)S(1)}, bf16[2,4,32,1664]{3,2,1,0:T(8,128)(2,1)S(1)}, u32[]{:S(2)}, u32[]{:S(2)}) collective-permute-start(bf16[2,4,32,1664]{3,2,1,0:T(8,128)(2,1)S(1)} %get-tuple-element.383), channel_id=1, source_target_pairs={{0,8},{1,9},{2,10},{3,11},{4,12},{5,13},{6,14},{7,15},{8,0},{9,1},... | collective-permute-start | bytes 2555912 | tf_op jit(solution)/shard_map/ppermute | solution.py:414
  38.7 26.7 %collective-permute-start.10 = (bf16[32,5632]{1,0:T(8,128)(2,1)S(1)}, bf16[32,5632]{1,0:T(8,128)(2,1)S(1)}, u32[]{:S(2)}, u32[]{:S(2)}) collective-permute-start(bf16[32,5632]{1,0:T(8,128)(2,1)S(1)} %copy-done.41), channel_id=1, source_target_pairs={{0,2},{1,3},{2,0},{3,1},{4,6},{5,7},{6,4},{7,5},{8,10},{9,11},{10,... | collective-permute-start | bytes 1081352 | tf_op jit(solution)/shard_map/ppermute | solution.py:414
  43.4 22.1 %collective-permute-start.11 = (bf16[32,5632]{1,0:T(8,128)(2,1)S(1)}, bf16[32,5632]{1,0:T(8,128)(2,1)S(1)}, u32[]{:S(2)}, u32[]{:S(2)}) collective-permute-start(bf16[32,5632]{1,0:T(8,128)(2,1)S(1)} %copy-done.41), channel_id=1, source_target_pairs={{0,3},{1,2},{2,1},{3,0},{4,7},{5,6},{6,5},{7,4},{8,11},{9,10},{10,... | collective-permute-start | bytes 1081352 | tf_op jit(solution)/shard_map/ppermute | solution.py:414
  44.7 20.9 %collective-permute-start.9 = (bf16[32,5632]{1,0:T(8,128)(2,1)S(1)}, bf16[32,5632]{1,0:T(8,128)(2,1)S(1)}, u32[]{:S(2)}, u32[]{:S(2)}) collective-permute-start(bf16[32,5632]{1,0:T(8,128)(2,1)S(1)} %copy-done.41), channel_id=1, source_target_pairs={{0,1},{1,0},{2,3},{3,2},{4,5},{5,4},{6,7},{7,6},{8,9},{9,8},{10,11... | collective-permute-start | bytes 1081352 | tf_op jit(solution)/shard_map/ppermute | solution.py:414
  67.5 33.7 %collective-permute-start.14 = (bf16[120,1024]{1,0:T(8,128)(2,1)S(1)}, bf16[120,1024]{1,0:T(8,128)(2,1)S(1)}, u32[]{:S(2)}, u32[]{:S(2)}) collective-permute-start(bf16[120,1024]{1,0:T(8,128)(2,1)S(1)} %pad_maximum_fusion.23), channel_id=1, source_target_pairs={{0,1},{1,0},{2,3},{3,2},{4,5},{5,4},{6,7},{7,6},{8,9},{9,8},{10,11... | collective-permute-start | bytes 737288 | tf_op jit(solution)/shard_map/ppermute | solution.py:414
  74.5 26.7 %collective-permute-start.15 = (bf16[120,1024]{1,0:T(8,128)(2,1)S(1)}, bf16[120,1024]{1,0:T(8,128)(2,1)}, u32[]{:S(2)}, u32[]{:S(2)}) collective-permute-start(bf16[120,1024]{1,0:T(8,128)(2,1)S(1)} %pad_maximum_fusion.23), channel_id=1, source_target_pairs={{0,2},{1,3},{2,0},{3,1},{4,6},{5,7},{6,4},{7,5},{8,10},{9,11},{10,... | collective-permute-start | bytes 737288 | tf_op jit(solution)/shard_map/ppermute | solution.py:414
  74.5 26.7 %collective-permute-start.16 = (bf16[120,1024]{1,0:T(8,128)(2,1)S(1)}, bf16[120,1024]{1,0:T(8,128)(2,1)}, u32[]{:S(2)}, u32[]{:S(2)}) collective-permute-start(bf16[120,1024]{1,0:T(8,128)(2,1)S(1)} %pad_maximum_fusion.23), channel_id=1, source_target_pairs={{0,3},{1,2},{2,1},{3,0},{4,7},{5,6},{6,5},{7,4},{8,11},{9,10},{10,... | collective-permute-start | bytes 737288 | tf_op jit(solution)/shard_map/ppermute | solution.py:414
  77.0 26.9 %collective-permute-start.13 = (bf16[4,32,2816]{2,1,0:T(8,128)(2,1)S(1)}, bf16[4,32,2816]{2,1,0:T(8,128)(2,1)}, u32[]{:S(2)}, u32[]{:S(2)}) collective-permute-start(bf16[4,32,2816]{2,1,0:T(8,128)(2,1)S(1)} %pad_maximum_fusion.15), channel_id=1, source_target_pairs={{0,16},{1,17},{2,18},{3,19},{4,20},{5,21},{6,22},{7,23},{8,24},{9,... | collective-permute-start | bytes 2162696 | tf_op jit(solution)/shard_map/ppermute | solution.py:414
  79.4 24.4 %collective-permute-start.12 = (bf16[4,32,2816]{2,1,0:T(8,128)(2,1)S(1)}, bf16[4,32,2816]{2,1,0:T(8,128)(2,1)}, u32[]{:S(2)}, u32[]{:S(2)}) collective-permute-start(bf16[4,32,2816]{2,1,0:T(8,128)(2,1)S(1)} %pad_maximum_fusion.14), channel_id=1, source_target_pairs={{0,8},{1,9},{2,10},{3,11},{4,12},{5,13},{6,14},{7,15},{8,0},{9,1},... | collective-permute-start | bytes 2162696 | tf_op jit(solution)/shard_map/ppermute | solution.py:414
  105.1 60.6 %collective-permute-start.22 = (bf16[2,4,32,2816]{3,2,1,0:T(8,128)(2,1)S(1)}, bf16[2,4,32,2816]{3,2,1,0:T(8,128)(2,1)}, u32[]{:S(2)}, u32[]{:S(2)}) collective-permute-start(bf16[2,4,32,2816]{3,2,1,0:T(8,128)(2,1)S(1)} %pad_maximum_fusion.9), channel_id=1, source_target_pairs={{0,8},{1,9},{2,10},{3,11},{4,12},{5,13},{6,14},{7,15},{8,0},{9,1},... | collective-permute-start | bytes 4325384 | tf_op jit(solution)/shard_map/ppermute | solution.py:414
  107.2 58.6 %collective-permute-start.21 = (bf16[2,4,32,2816]{3,2,1,0:T(8,128)(2,1)S(1)}, bf16[2,4,32,2816]{3,2,1,0:T(8,128)(2,1)}, u32[]{:S(2)}, u32[]{:S(2)}) collective-permute-start(bf16[2,4,32,2816]{3,2,1,0:T(8,128)(2,1)S(1)} %pad_maximum_fusion.8), channel_id=1, source_target_pairs={{0,16},{1,17},{2,18},{3,19},{4,20},{5,21},{6,22},{7,23},{8,24},{9,... | collective-permute-start | bytes 4325384 | tf_op jit(solution)/shard_map/ppermute | solution.py:414
  109.1 52.3 %collective-permute-start.20 = (bf16[4,120,512]{2,1,0:T(8,128)(2,1)}, bf16[4,120,512]{2,1,0:T(8,128)(2,1)}, u32[]{:S(2)}, u32[]{:S(2)}) collective-permute-start(bf16[4,120,512]{2,1,0:T(8,128)(2,1)} %pad_maximum_fusion.18), channel_id=1, source_target_pairs={{0,16},{1,17},{2,18},{3,19},{4,20},{5,21},{6,22},{7,23},{8,24},{9,... | collective-permute-start | bytes 1474568 | tf_op jit(solution)/shard_map/ppermute | solution.py:414
  111.0 50.4 %collective-permute-start.19 = (bf16[4,120,512]{2,1,0:T(8,128)(2,1)}, bf16[4,120,512]{2,1,0:T(8,128)(2,1)}, u32[]{:S(2)}, u32[]{:S(2)}) collective-permute-start(bf16[4,120,512]{2,1,0:T(8,128)(2,1)} %pad_maximum_fusion.17), channel_id=1, source_target_pairs={{0,8},{1,9},{2,10},{3,11},{4,12},{5,13},{6,14},{7,15},{8,0},{9,1},... | collective-permute-start | bytes 1474568 | tf_op jit(solution)/shard_map/ppermute | solution.py:414
  162.7 22.6 %collective-permute-start.26 = (bf16[2,4,120,512]{3,2,1,0:T(8,128)(2,1)S(1)}, bf16[2,4,120,512]{3,2,1,0:T(8,128)(2,1)S(1)}, u32[]{:S(2)}, u32[]{:S(2)}) collective-permute-start(bf16[2,4,120,512]{3,2,1,0:T(8,128)(2,1)S(1)} %pad_maximum_fusion.11), channel_id=1, source_target_pairs={{0,8},{1,9},{2,10},{3,11},{4,12},{5,13},{6,14},{7,15},{8,0},{9,1},... | collective-permute-start | bytes 2949128 | tf_op jit(solution)/shard_map/ppermute | solution.py:414
  164.8 20.7 %collective-permute-start.25 = (bf16[2,4,120,512]{3,2,1,0:T(8,128)(2,1)S(1)}, bf16[2,4,120,512]{3,2,1,0:T(8,128)(2,1)S(1)}, u32[]{:S(2)}, u32[]{:S(2)}) collective-permute-start(bf16[2,4,120,512]{3,2,1,0:T(8,128)(2,1)S(1)} %pad_maximum_fusion.10), channel_id=1, source_target_pairs={{0,16},{1,17},{2,18},{3,19},{4,20},{5,21},{6,22},{7,23},{8,24},{9,... | collective-permute-start | bytes 2949128 | tf_op jit(solution)/shard_map/ppermute | solution.py:414
  188.3 31.4 %collective-permute-start.30 = (bf16[2,2,4,32,2816]{4,3,2,1,0:T(8,128)(2,1)}, bf16[2,2,4,32,2816]{4,3,2,1,0:T(8,128)(2,1)}, u32[]{:S(2)}, u32[]{:S(2)}) collective-permute-start(bf16[2,2,4,32,2816]{4,3,2,1,0:T(8,128)(2,1)} %pad_maximum_fusion.3.ou_ref), channel_id=1, source_target_pairs={{0,4},{1,5},{2,6},{3,7},{4,0},{5,1},{6,2},{7,3},{8,12},{9,13},{10,... | collective-permute-start | bytes 8650760 | tf_op jit(solution)/shard_map/ppermute | solution.py:414
  188.5 31.1 %collective-permute-start.29 = (bf16[2,2,4,32,2816]{4,3,2,1,0:T(8,128)(2,1)}, bf16[2,2,4,32,2816]{4,3,2,1,0:T(8,128)(2,1)}, u32[]{:S(2)}, u32[]{:S(2)}) collective-permute-start(bf16[2,2,4,32,2816]{4,3,2,1,0:T(8,128)(2,1)} %pad_maximum_fusion.2.og_ref), channel_id=1, source_target_pairs={{0,4},{1,5},{2,6},{3,7},{4,0},{5,1},{6,2},{7,3},{8,12},{9,13},{10,... | collective-permute-start | bytes 8650760 | tf_op jit(solution)/shard_map/ppermute | solution.py:414
  188.8 18.0 %collective-permute-start.24 = (bf16[2,8,128,128]{3,2,1,0:T(8,128)(2,1)}, bf16[2,8,128,128]{3,2,1,0:T(8,128)(2,1)}, u32[]{:S(2)}, u32[]{:S(2)}) collective-permute-start(bf16[2,8,128,128]{3,2,1,0:T(8,128)(2,1)} %fusion.14), channel_id=1, source_target_pairs={{0,1},{1,2},{2,3},{4,5},{5,6},{6,7},{8,9},{9,10},{10,11},{12,13},{... | collective-permute-start | bytes 1572872 | tf_op jit(solution)/shard_map/ppermute | solution.py:676
  265.1 24.7 %collective-permute-start.32 = (bf16[2,2,4,32,2816]{4,3,2,0,1:T(8,128)(2,1)}, bf16[2,2,4,32,2816]{4,3,2,0,1:T(8,128)(2,1)}, u32[]{:S(2)}, u32[]{:S(2)}) collective-permute-start(bf16[2,2,4,32,2816]{4,3,2,0,1:T(8,128)(2,1)} %copy.195), channel_id=1, source_target_pairs={{0,4},{1,5},{2,6},{3,7},{4,0},{5,1},{6,2},{7,3},{8,12},{9,13},{10,... | collective-permute-start | bytes 8650760 | tf_op jit(solution)/shard_map/ppermute | solution.py:414
  265.1 24.7 %collective-permute-start.33 = (bf16[2,2,4,32,2816]{4,3,2,1,0:T(8,128)(2,1)}, bf16[2,2,4,32,2816]{4,3,2,1,0:T(8,128)(2,1)}, u32[]{:S(2)}, u32[]{:S(2)}) collective-permute-start(bf16[2,2,4,32,2816]{4,3,2,1,0:T(8,128)(2,1)} %get-tuple-element.193), channel_id=1, source_target_pairs={{0,4},{1,5},{2,6},{3,7},{4,0},{5,1},{6,2},{7,3},{8,12},{9,13},{10,... | collective-permute-start | bytes 8650760 | tf_op jit(solution)/shard_map/ppermute | solution.py:414
  276.3 27.8 %collective-permute-start.35 = (bf16[2,2,4,120,1024]{4,3,2,1,0:T(8,128)(2,1)}, bf16[2,2,4,120,1024]{4,3,2,1,0:T(8,128)(2,1)}, u32[]{:S(2)}, u32[]{:S(2)}) collective-permute-start(bf16[2,2,4,120,1024]{4,3,2,1,0:T(8,128)(2,1)} %pad_maximum_fusion.1), channel_id=1, source_target_pairs={{0,4},{1,5},{2,6},{3,7},{4,0},{5,1},{6,2},{7,3},{8,12},{9,13},{10,... | collective-permute-start | bytes 11796488 | tf_op jit(solution)/shard_map/ppermute | solution.py:414
  321.0 34.9 %collective-permute-start.38 = (bf16[2,4,32,2816]{3,2,1,0:T(8,128)(2,1)}, bf16[2,4,32,2816]{3,2,1,0:T(8,128)(2,1)}, u32[]{:S(2)}, u32[]{:S(2)}) collective-permute-start(bf16[2,4,32,2816]{3,2,1,0:T(8,128)(2,1)} %get-tuple-element.352), channel_id=1, source_target_pairs={{0,16},{1,17},{2,18},{3,19},{4,20},{5,21},{6,22},{7,23},{8,24},{9,... | collective-permute-start | bytes 4325384 | tf_op jit(solution)/shard_map/ppermute | solution.py:414
  322.2 34.7 %collective-permute-start.37 = (bf16[2,4,32,2816]{3,2,1,0:T(8,128)(2,1)}, bf16[2,4,32,2816]{3,2,1,0:T(8,128)(2,1)S(1)}, u32[]{:S(2)}, u32[]{:S(2)}) collective-permute-start(bf16[2,4,32,2816]{3,2,1,0:T(8,128)(2,1)} %get-tuple-element.354), channel_id=1, source_target_pairs={{0,8},{1,9},{2,10},{3,11},{4,12},{5,13},{6,14},{7,15},{8,0},{9,1},... | collective-permute-start | bytes 4325384 | tf_op jit(solution)/shard_map/ppermute | solution.py:414
  323.9 56.4 %collective-permute-start.41 = (bf16[2,4,120,512]{3,2,1,0:T(8,128)(2,1)}, bf16[2,4,120,512]{3,2,1,0:T(8,128)(2,1)}, u32[]{:S(2)}, u32[]{:S(2)}) collective-permute-start(bf16[2,4,120,512]{3,2,1,0:T(8,128)(2,1)} %get-tuple-element.361), channel_id=1, source_target_pairs={{0,16},{1,17},{2,18},{3,19},{4,20},{5,21},{6,22},{7,23},{8,24},{9,... | collective-permute-start | bytes 2949128 | tf_op jit(solution)/shard_map/ppermute | solution.py:414
  325.3 54.9 %collective-permute-start.40 = (bf16[2,4,120,512]{3,2,1,0:T(8,128)(2,1)}, bf16[2,4,120,512]{3,2,1,0:T(8,128)(2,1)}, u32[]{:S(2)}, u32[]{:S(2)}) collective-permute-start(bf16[2,4,120,512]{3,2,1,0:T(8,128)(2,1)} %get-tuple-element.363), channel_id=1, source_target_pairs={{0,8},{1,9},{2,10},{3,11},{4,12},{5,13},{6,14},{7,15},{8,0},{9,1},... | collective-permute-start | bytes 2949128 | tf_op jit(solution)/shard_map/ppermute | solution.py:414
  362.0 41.9 %collective-permute-start.43 = (bf16[4,32,2816]{2,1,0:T(8,128)(2,1)}, bf16[4,32,2816]{2,1,0:T(8,128)(2,1)}, u32[]{:S(2)}, u32[]{:S(2)}) collective-permute-start(bf16[4,32,2816]{2,1,0:T(8,128)(2,1)} %get-tuple-element.370), channel_id=1, source_target_pairs={{0,8},{1,9},{2,10},{3,11},{4,12},{5,13},{6,14},{7,15},{8,0},{9,1},... | collective-permute-start | bytes 2162696 | tf_op jit(solution)/shard_map/ppermute | solution.py:414
  363.1 40.8 %collective-permute-start.42 = (bf16[4,32,2816]{2,1,0:T(8,128)(2,1)}, bf16[4,32,2816]{2,1,0:T(8,128)(2,1)}, u32[]{:S(2)}, u32[]{:S(2)}) collective-permute-start(bf16[4,32,2816]{2,1,0:T(8,128)(2,1)} %get-tuple-element.372), channel_id=1, source_target_pairs={{0,16},{1,17},{2,18},{3,19},{4,20},{5,21},{6,22},{7,23},{8,24},{9,... | collective-permute-start | bytes 2162696 | tf_op jit(solution)/shard_map/ppermute | solution.py:414
  376.0 22.0 %collective-permute-start.39 = (f32[2,8,1536]{2,1,0:T(8,128)}, f32[2,8,1536]{2,1,0:T(8,128)S(1)}, u32[]{:S(2)}, u32[]{:S(2)}) collective-permute-start(f32[2,8,1536]{2,1,0:T(8,128)} %get-tuple-element.215), channel_id=1, source_target_pairs={{1,0},{2,1},{3,2},{5,4},{6,5},{7,6},{9,8},{10,9},{11,10},{13,12},{... | collective-permute-start | bytes 294920 | tf_op jit(solution)/shard_map/ppermute | solution.py:676
  385.4 73.0 %collective-permute-start.50 = (bf16[4,120,512]{2,1,0:T(8,128)(2,1)}, bf16[4,120,512]{2,1,0:T(8,128)(2,1)}, u32[]{:S(2)}, u32[]{:S(2)}) collective-permute-start(bf16[4,120,512]{2,1,0:T(8,128)(2,1)} %get-tuple-element.377), channel_id=1, source_target_pairs={{0,8},{1,9},{2,10},{3,11},{4,12},{5,13},{6,14},{7,15},{8,0},{9,1},... | collective-permute-start | bytes 1474568 | tf_op jit(solution)/shard_map/ppermute | solution.py:414
  385.9 72.5 %collective-permute-start.49 = (bf16[4,120,512]{2,1,0:T(8,128)(2,1)}, bf16[4,120,512]{2,1,0:T(8,128)(2,1)}, u32[]{:S(2)}, u32[]{:S(2)}) collective-permute-start(bf16[4,120,512]{2,1,0:T(8,128)(2,1)} %get-tuple-element.379), channel_id=1, source_target_pairs={{0,16},{1,17},{2,18},{3,19},{4,20},{5,21},{6,22},{7,23},{8,24},{9,... | collective-permute-start | bytes 1474568 | tf_op jit(solution)/shard_map/ppermute | solution.py:414
  403.9 39.3 %collective-permute-start.45 = (bf16[2,2,4,32,1536]{4,3,2,1,0:T(8,128)(2,1)}, bf16[2,2,4,32,1536]{4,3,2,1,0:T(8,128)(2,1)}, u32[]{:S(2)}, u32[]{:S(2)}) collective-permute-start(bf16[2,2,4,32,1536]{4,3,2,1,0:T(8,128)(2,1)} %get-tuple-element.350), channel_id=1, source_target_pairs={{0,4},{1,5},{2,6},{3,7},{4,0},{5,1},{6,2},{7,3},{8,12},{9,13},{10,... | collective-permute-start | bytes 4718600 | tf_op jit(solution)/shard_map/ppermute | solution.py:414
  407.6 57.0 %collective-permute-start.71 = (bf16[32,5632]{1,0:T(8,128)(2,1)}, bf16[32,5632]{1,0:T(8,128)(2,1)}, u32[]{:S(2)}, u32[]{:S(2)}) collective-permute-start(bf16[32,5632]{1,0:T(8,128)(2,1)} %get-tuple-element.367), channel_id=1, source_target_pairs={{0,1},{1,0},{2,3},{3,2},{4,5},{5,4},{6,7},{7,6},{8,9},{9,8},{10,11... | collective-permute-start | bytes 1081352 | tf_op jit(solution)/shard_map/ppermute | solution.py:414
  410.8 54.7 %collective-permute-start.72 = (bf16[32,5632]{1,0:T(8,128)(2,1)}, bf16[32,5632]{1,0:T(8,128)(2,1)}, u32[]{:S(2)}, u32[]{:S(2)}) collective-permute-start(bf16[32,5632]{1,0:T(8,128)(2,1)} %get-tuple-element.368), channel_id=1, source_target_pairs={{0,2},{1,3},{2,0},{3,1},{4,6},{5,7},{6,4},{7,5},{8,10},{9,11},{10,... | collective-permute-start | bytes 1081352 | tf_op jit(solution)/shard_map/ppermute | solution.py:414
  464.5 27.7 %collective-permute-start.48 = (bf16[2,2,4,32,1664]{4,3,2,1,0:T(8,128)(2,1)S(1)}, bf16[2,2,4,32,1664]{4,3,2,1,0:T(8,128)(2,1)S(1)}, u32[]{:S(2)}, u32[]{:S(2)}) collective-permute-start(bf16[2,2,4,32,1664]{4,3,2,1,0:T(8,128)(2,1)S(1)} %get-tuple-element.348), channel_id=1, source_target_pairs={{0,4},{1,5},{2,6},{3,7},{4,0},{5,1},{6,2},{7,3},{8,12},{9,13},{10,... | collective-permute-start | bytes 5111816 | tf_op jit(solution)/shard_map/ppermute | solution.py:414
  464.6 23.8 %collective-permute-start.47 = (bf16[2,4,32,768]{3,2,1,0:T(8,128)(2,1)S(1)}, bf16[2,4,32,768]{3,2,1,0:T(8,128)(2,1)S(1)}, u32[]{:S(2)}, u32[]{:S(2)}) collective-permute-start(bf16[2,4,32,768]{3,2,1,0:T(8,128)(2,1)S(1)} %get-tuple-element.387), channel_id=1, source_target_pairs={{0,16},{1,17},{2,18},{3,19},{4,20},{5,21},{6,22},{7,23},{8,24},{9,... | collective-permute-start | bytes 1179656 | tf_op jit(solution)/shard_map/ppermute | solution.py:414
  465.5 22.8 %collective-permute-start.46 = (bf16[2,4,32,768]{3,2,1,0:T(8,128)(2,1)S(1)}, bf16[2,4,32,768]{3,2,1,0:T(8,128)(2,1)S(1)}, u32[]{:S(2)}, u32[]{:S(2)}) collective-permute-start(bf16[2,4,32,768]{3,2,1,0:T(8,128)(2,1)S(1)} %get-tuple-element.389), channel_id=1, source_target_pairs={{0,8},{1,9},{2,10},{3,11},{4,12},{5,13},{6,14},{7,15},{8,0},{9,1},... | collective-permute-start | bytes 1179656 | tf_op jit(solution)/shard_map/ppermute | solution.py:414
  467.0 19.7 %collective-permute-start.69 = (bf16[120,1024]{1,0:T(8,128)(2,1)S(1)}, bf16[120,1024]{1,0:T(8,128)(2,1)S(1)}, u32[]{:S(2)}, u32[]{:S(2)}) collective-permute-start(bf16[120,1024]{1,0:T(8,128)(2,1)S(1)} %get-tuple-element.375), channel_id=1, source_target_pairs={{0,2},{1,3},{2,0},{3,1},{4,6},{5,7},{6,4},{7,5},{8,10},{9,11},{10,... | collective-permute-start | bytes 737288 | tf_op jit(solution)/shard_map/ppermute | solution.py:414
  469.4 17.4 %collective-permute-start.70 = (bf16[120,1024]{1,0:T(8,128)(2,1)S(1)}, bf16[120,1024]{1,0:T(8,128)(2,1)S(1)}, u32[]{:S(2)}, u32[]{:S(2)}) collective-permute-start(bf16[120,1024]{1,0:T(8,128)(2,1)S(1)} %get-tuple-element.373), channel_id=1, source_target_pairs={{0,3},{1,2},{2,1},{3,0},{4,7},{5,6},{6,5},{7,4},{8,11},{9,10},{10,... | collective-permute-start | bytes 737288 | tf_op jit(solution)/shard_map/ppermute | solution.py:414
  489.2 20.9 %collective-permute-start.57 = (bf16[4,32,768]{2,1,0:T(8,128)(2,1)}, bf16[4,32,768]{2,1,0:T(8,128)(2,1)}, u32[]{:S(2)}, u32[]{:S(2)}) collective-permute-start(bf16[4,32,768]{2,1,0:T(8,128)(2,1)} %get-tuple-element.401), channel_id=1, source_target_pairs={{0,8},{1,9},{2,10},{3,11},{4,12},{5,13},{6,14},{7,15},{8,0},{9,1},... | collective-permute-start | bytes 589832 | tf_op jit(solution)/shard_map/ppermute | solution.py:414
  491.2 19.0 %collective-permute-start.56 = (bf16[4,32,768]{2,1,0:T(8,128)(2,1)}, bf16[4,32,768]{2,1,0:T(8,128)(2,1)}, u32[]{:S(2)}, u32[]{:S(2)}) collective-permute-start(bf16[4,32,768]{2,1,0:T(8,128)(2,1)} %get-tuple-element.403), channel_id=1, source_target_pairs={{0,16},{1,17},{2,18},{3,19},{4,20},{5,21},{6,22},{7,23},{8,24},{9,... | collective-permute-start | bytes 589832 | tf_op jit(solution)/shard_map/ppermute | solution.py:414
  494.8 34.4 %collective-permute-start.62 = (bf16[2,4,32,896]{3,2,1,0:T(8,128)(2,1)}, bf16[2,4,32,896]{3,2,1,0:T(8,128)(2,1)}, u32[]{:S(2)}, u32[]{:S(2)}) collective-permute-start(bf16[2,4,32,896]{3,2,1,0:T(8,128)(2,1)} %get-tuple-element.381), channel_id=1, source_target_pairs={{0,16},{1,17},{2,18},{3,19},{4,20},{5,21},{6,22},{7,23},{8,24},{9,... | collective-permute-start | bytes 1376264 | tf_op jit(solution)/shard_map/ppermute | solution.py:414
  495.7 33.4 %collective-permute-start.61 = (bf16[2,4,32,768]{3,2,1,0:T(8,128)(2,1)}, bf16[2,4,32,768]{3,2,1,0:T(8,128)(2,1)}, u32[]{:S(2)}, u32[]{:S(2)}) collective-permute-start(bf16[2,4,32,768]{3,2,1,0:T(8,128)(2,1)} %get-tuple-element.385), channel_id=1, source_target_pairs={{0,8},{1,9},{2,10},{3,11},{4,12},{5,13},{6,14},{7,15},{8,0},{9,1},... | collective-permute-start | bytes 1179656 | tf_op jit(solution)/shard_map/ppermute | solution.py:414
  522.9 18.4 %collective-permute-start.58 = (bf16[32,1536]{1,0:T(8,128)(2,1)S(1)}, bf16[32,1536]{1,0:T(8,128)(2,1)S(1)}, u32[]{:S(2)}, u32[]{:S(2)}) collective-permute-start(bf16[32,1536]{1,0:T(8,128)(2,1)S(1)} %get-tuple-element.397), channel_id=1, source_target_pairs={{0,1},{1,0},{2,3},{3,2},{4,5},{5,4},{6,7},{7,6},{8,9},{9,8},{10,11... | collective-permute-start | bytes 294920 | tf_op jit(solution)/shard_map/ppermute | solution.py:414
  523.0 20.2 %collective-permute-start.59 = (bf16[32,1536]{1,0:T(8,128)(2,1)S(1)}, bf16[32,1536]{1,0:T(8,128)(2,1)S(1)}, u32[]{:S(2)}, u32[]{:S(2)}) collective-permute-start(bf16[32,1536]{1,0:T(8,128)(2,1)S(1)} %get-tuple-element.398), channel_id=1, source_target_pairs={{0,2},{1,3},{2,0},{3,1},{4,6},{5,7},{6,4},{7,5},{8,10},{9,11},{10,... | collective-permute-start | bytes 294920 | tf_op jit(solution)/shard_map/ppermute | solution.py:414
  525.4 17.8 %collective-permute-start.60 = (bf16[32,1536]{1,0:T(8,128)(2,1)S(1)}, bf16[32,1536]{1,0:T(8,128)(2,1)S(1)}, u32[]{:S(2)}, u32[]{:S(2)}) collective-permute-start(bf16[32,1536]{1,0:T(8,128)(2,1)S(1)} %get-tuple-element.399), channel_id=1, source_target_pairs={{0,3},{1,2},{2,1},{3,0},{4,7},{5,6},{6,5},{7,4},{8,11},{9,10},{10,... | collective-permute-start | bytes 294920 | tf_op jit(solution)/shard_map/ppermute | solution.py:414
  (90 other events, 770.0 us)
